TPU v7x, 32 devices: a whole 2x2x4 slice. The times are simulated.
32 devices in a mesh: groups: 2 (over x), dom: 16 (over z, y, core).
Axes of the slice: x: 2, y: 2, z: 4, core: 2. Of those that a mesh axis runs over, the one named last changes fastest.
Arguments:
- features: bfloat16 [65536, 256], P(('groups', 'dom')), parts along dimension 0, may hold values from -6 to 6
- cotangent: bfloat16 [65536, 256], P(('groups', 'dom')), parts along dimension 0, may hold values from -6 to 6
- w_fine: bfloat16 [4, 256, 256], replicated, may hold values from -0.375 to 0.375
- w_coarse: bfloat16 [4, 256, 256], replicated, may hold values from -0.375 to 0.375
- bias: float32 [2, 256], replicated, may hold values from -3 to 3
- fine_src: int32 [131072], P('dom'), may hold values from 0 to 2559
- fine_dst: int32 [131072], P('dom'), may hold values from 0 to 127
- send_left: int32 [4096], P('dom'), may hold values from 0 to 2047
- send_right: int32 [4096], P('dom'), may hold values from 0 to 2047
- pool_map: int32 [32768], P('dom'), may hold values from 0 to 511, as said below
- coarse_src: int32 [32768], P('dom'), may hold values from 0 to 1023
- coarse_dst: int32 [32768], P('dom'), may hold values from 0 to 127
- coarse_send: int32 [256, 32], P('dom'), may hold values from 0 to 511
Outputs:
- grad_input: float32 [65536, 256], P(('groups', 'dom')), parts along dimension 0
- grad_fine: float32 [8, 256, 256], P('groups'), parts along dimension 0
- grad_coarse: float32 [8, 256, 256], P('groups'), parts along dimension 0
- grad_bias: float32 [4, 256], P('groups'), parts along dimension 0
There are 2 independent parts, one for each index of `groups`. A program takes and returns all parts, laid end to end along the dimension named above; an argument that names none is the same for every part. Nothing has to cross between parts.
Inputs may be any that keep to these rules, and one draw needn't show every extreme that they name: `fine_src`: rows below 2048 are the partition's own nodes, then 256 rows from the lower neighbour, then 256 from the upper one. `pool_map`: every coarse index of 0 to 511 is the image of at least one fine node of each partition. `coarse_src`: rows below 512 are the partition's own coarse nodes, then 32 rows from each partition in order.
All inputs are finite; a program needn't handle non-finite values.
Results may differ from a plain program's by a relative error of at most 0.012.
The roundings to bfloat16 on the way count: a program that leaves them out, or rounds other values in their place, can miss the bound.
Values may be sent and summed in bfloat16 or wider, within the bound.
No kernel may reach another device: no remote copies, remote signals or barrier semaphores. Data moves between devices by JAX's collectives and lax.ppermute only.
A program may use at most 128 MiB of HBM per device.

v0:
```python
import jax
import jax.numpy as jnp
from jax import lax
from jax.sharding import PartitionSpec as P


def shifted(block, axis, distance):
    devices = range(lax.axis_size(axis))
    route = [(i - distance, i) for i in devices if i - distance in devices]
    return lax.ppermute(block, axis, route)


def silu_grad(value):
    sig = jax.nn.sigmoid(value)
    return sig * (1.0 + value * (1.0 - sig))


def tile_onehot(dst, per_tile):
    tiles = dst.reshape(-1, per_tile)
    return (tiles[:, :, None] == jnp.arange(128, dtype=jnp.int32)[None, None, :]).astype(
        jnp.bfloat16
    )


def inner_rows(left, right):
    return lax.dot_general(
        left, right, (((0,), (0,)), ((), ())), preferred_element_type=jnp.float32
    )


def project(hidden, weights):
    send_proj = jnp.dot(hidden, weights[0], preferred_element_type=jnp.float32).astype(jnp.bfloat16)
    recv_proj = jnp.dot(hidden, weights[1], preferred_element_type=jnp.float32).astype(jnp.bfloat16)
    return (send_proj, recv_proj)


def edge_update(hidden, extended, recv_proj, onehot, src, weights, edge_bias):
    tiles, per_tile, width = onehot.shape
    latent = hidden.shape[1]
    gathered = jnp.take(extended, src, axis=0).astype(jnp.float32)
    at_edges = jnp.einsum(
        "tej,tjl->tel",
        onehot,
        recv_proj.reshape(tiles, width, latent),
        preferred_element_type=jnp.float32,
    ).reshape(-1, latent)
    zvals = gathered + at_edges + edge_bias[None, :]
    message = jax.nn.silu(zvals).astype(jnp.bfloat16)
    summed = jnp.einsum(
        "tej,tel->tjl",
        onehot,
        message.reshape(tiles, per_tile, latent),
        preferred_element_type=jnp.float32,
    )
    aggregate = summed.reshape(-1, latent).astype(jnp.bfloat16)
    update = jnp.dot(hidden, weights[3], preferred_element_type=jnp.float32) + jnp.dot(
        aggregate, weights[2], preferred_element_type=jnp.float32
    )
    newer = (hidden.astype(jnp.float32) + jax.nn.silu(update)).astype(jnp.bfloat16)
    return (newer, zvals, aggregate, update)


def edge_back(rows_ext, grad_new, hidden, zvals, aggregate, update, onehot, src, weights):
    tiles, per_tile, width = onehot.shape
    latent = hidden.shape[1]
    grad_u = (grad_new * silu_grad(update)).astype(jnp.bfloat16)
    grad_w3 = inner_rows(hidden, grad_u)
    grad_w2 = inner_rows(aggregate, grad_u)
    grad_h = grad_new + lax.dot_general(
        grad_u, weights[3], (((1,), (1,)), ((), ())), preferred_element_type=jnp.float32
    )
    grad_agg = lax.dot_general(
        grad_u, weights[2], (((1,), (1,)), ((), ())), preferred_element_type=jnp.float32
    ).astype(jnp.bfloat16)
    grad_msg = jnp.einsum(
        "tej,tjl->tel",
        onehot,
        grad_agg.reshape(tiles, width, latent),
        preferred_element_type=jnp.float32,
    ).reshape(-1, latent)
    grad_z = (grad_msg * silu_grad(zvals)).astype(jnp.bfloat16)
    grad_b = jnp.sum(grad_z.astype(jnp.float32), axis=0)
    grad_q = (
        jnp.einsum(
            "tej,tel->tjl",
            onehot,
            grad_z.reshape(tiles, per_tile, latent),
            preferred_element_type=jnp.float32,
        )
        .reshape(-1, latent)
        .astype(jnp.bfloat16)
    )
    grad_ext = jax.ops.segment_sum(grad_z.astype(jnp.float32), src, num_segments=rows_ext).astype(
        jnp.bfloat16
    )
    return (grad_h, grad_ext, grad_q, grad_w3, grad_w2, grad_b)


def front_back(grad_h, hidden, grad_p, grad_q, weights):
    grad_h = grad_h + lax.dot_general(
        grad_p, weights[0], (((1,), (1,)), ((), ())), preferred_element_type=jnp.float32
    )
    grad_h = grad_h + lax.dot_general(
        grad_q, weights[1], (((1,), (1,)), ((), ())), preferred_element_type=jnp.float32
    )
    return (grad_h, inner_rows(hidden, grad_p), inner_rows(hidden, grad_q))


def add_rows(local_part, arrivals, index):
    latent = local_part.shape[-1]
    total = (
        jnp.zeros(local_part.shape, jnp.float32)
        .at[index.reshape(-1)]
        .add(arrivals.reshape(-1, latent).astype(jnp.float32))
    )
    return (total + local_part.astype(jnp.float32)).astype(jnp.bfloat16)


def shards(
    features,
    cotangent,
    w_fine,
    w_coarse,
    bias,
    fine_src,
    fine_dst,
    send_left,
    send_right,
    pool_map,
    coarse_src,
    coarse_dst,
    coarse_send,
):
    nodes, latent = features.shape
    parts = lax.axis_size("dom")
    halo_rows = send_left.shape[0]
    coarse_nodes = nodes // 4
    per_tile = fine_src.shape[0] // (nodes // 128)
    fine_hot = tile_onehot(fine_dst, per_tile)
    coarse_hot = tile_onehot(coarse_dst, per_tile)
    fine_rows = nodes + 2 * halo_rows
    coarse_rows = coarse_nodes + coarse_send.shape[0] * coarse_send.shape[1]
    send_f, recv_f = project(features, w_fine)
    to_right = jnp.take(send_f, send_right, axis=0)
    to_left = jnp.take(send_f, send_left, axis=0)
    from_left = shifted(to_right, "dom", 1)
    from_right = shifted(to_left, "dom", -1)
    fine_ext = jnp.concatenate([send_f, from_left, from_right], axis=0)
    h_one, z_one, agg_one, u_one = edge_update(
        features, fine_ext, recv_f, fine_hot, fine_src, w_fine, bias[0]
    )
    pool_hot = (pool_map[None, :] == jnp.arange(coarse_nodes, dtype=jnp.int32)[:, None]).astype(
        jnp.bfloat16
    )
    counts = jnp.sum(pool_hot.astype(jnp.float32), axis=1)
    pooled = (
        jnp.dot(pool_hot, h_one, preferred_element_type=jnp.float32) / counts[:, None]
    ).astype(jnp.bfloat16)
    send_c, recv_c = project(pooled, w_coarse)
    outgoing = jnp.take(send_c, coarse_send.reshape(-1), axis=0).reshape(
        coarse_send.shape[0], coarse_send.shape[1], latent
    )
    incoming = lax.all_to_all(outgoing, "dom", split_axis=0, concat_axis=0, tiled=True)
    coarse_ext = jnp.concatenate([send_c, incoming.reshape(-1, latent)], axis=0)
    h_c, z_c, agg_c, u_c = edge_update(
        pooled, coarse_ext, recv_c, coarse_hot, coarse_src, w_coarse, bias[1]
    )
    divisor = float(nodes * parts // 256)
    grad_hc = jnp.dot(pool_hot, cotangent, preferred_element_type=jnp.float32)
    grad_c, gext_c, gq_c, gw3_c, gw2_c, gb_c = edge_back(
        coarse_rows, grad_hc, pooled, z_c, agg_c, u_c, coarse_hot, coarse_src, w_coarse
    )
    returned = lax.all_to_all(
        gext_c[coarse_nodes:].reshape(coarse_send.shape[0], coarse_send.shape[1], latent),
        "dom",
        split_axis=0,
        concat_axis=0,
        tiled=True,
    )
    gp_c = add_rows(gext_c[:coarse_nodes], returned, coarse_send)
    grad_c, gw0_c, gw1_c = front_back(grad_c, pooled, gp_c, gq_c, w_coarse)
    coarse_terms = (jnp.stack([gw0_c, gw1_c, gw2_c, gw3_c]), gb_c)
    scaled = (grad_c / counts[:, None]).astype(jnp.bfloat16)
    grad_h1 = cotangent.astype(jnp.float32) + inner_rows(pool_hot, scaled)
    grad_f, gext_f, gq_f, gw3_f, gw2_f, gb_f = edge_back(
        fine_rows, grad_h1, features, z_one, agg_one, u_one, fine_hot, fine_src, w_fine
    )
    got_left = gext_f[nodes : nodes + halo_rows]
    got_right = gext_f[nodes + halo_rows :]
    for_right = shifted(got_left, "dom", -1)
    for_left = shifted(got_right, "dom", 1)
    gp_f = add_rows(
        gext_f[:nodes],
        jnp.concatenate([for_right, for_left], axis=0),
        jnp.concatenate([send_right, send_left], axis=0),
    )
    grad_f, gw0_f, gw1_f = front_back(grad_f, features, gp_f, gq_f, w_fine)
    fine_terms = (jnp.stack([gw0_f, gw1_f, gw2_f, gw3_f]), gb_f)
    fine_w, fine_b, coarse_w, coarse_b = lax.psum(
        (fine_terms[0], fine_terms[1], coarse_terms[0], coarse_terms[1]), "dom"
    )
    grad_bias = jnp.stack([fine_b, coarse_b]) / divisor
    return (grad_f, fine_w / divisor, coarse_w / divisor, grad_bias)


def solution(mesh):
    return jax.shard_map(
        shards,
        mesh=mesh,
        in_specs=(
            P(("groups", "dom"), None),
            P(("groups", "dom"), None),
            P(),
            P(),
            P(),
            P("dom"),
            P("dom"),
            P("dom"),
            P("dom"),
            P("dom"),
            P("dom"),
            P("dom"),
            P("dom", None),
        ),
        out_specs=(
            P(("groups", "dom"), None),
            P("groups", None, None),
            P("groups", None, None),
            P("groups", None),
        ),
        check_vma=False,
    )
```

profile of v0, /device:TPU:13, one launch (start us, length us, event | category | flops | bytes accessed | tf_op | source)
XLA Modules:
  0.0 378.8 jit_solution(7154513134916787184)
XLA Ops:
  11.6 3.7 collective-permute-start
  17.3 1.9 collective-permute-start.1
  20.8 2.7 fusion.67
  25.9 2.8 fusion.11
  28.7 4.6 %fusion.7 = f32[16,512,256]{2,1,0:T(8,128)} fusion(bf16[16,128,256]{2,1,0:T(8,128)(2,1)S(1)} %bitcast.147, s32[16,512]{1,0:T(8,128)S(1)} %eq.46), kind=kOutput, calls=%fused_computation.25 | convolution fusion | flops 537919488 | bytes 9469952 | tf_op jit(solution)/shard_map/tej,tjl->tel/dot_general | solution.py:41
  37.5 33.0 %gather_fusion = bf16[8192,256]{1,0:T(8,128)(2,1)} fusion(bf16[2560,256]{1,0:T(8,128)(2,1)S(1)} %pad_maximum_fusion, s32[8192]{0:T(1024)S(1)} %fusion.88), kind=kCustom, calls=%fused_computation.2 | custom fusion | bytes 8421376 | tf_op jit(solution)/shard_map/jit(_take)/gather | solution.py:40
  70.5 7.3 %fusion.25 = bf16[16,128,256]{2,1,0:T(8,128)(2,1)S(1)} fusion(f32[16,512,256]{2,1,0:T(8,128)} %fusion.7, f32[256]{0:T(256)S(1)} %bitcast.166, bf16[16,512,256]{2,1,0:T(8,128)(2,1)} %bitcast.145, pred[16,512]{1,0:T(8,128)(4,1)S(1)} %copy-done.26, s32[16,512]{1,0:T(8,128)S(1)} %eq.46), kind=kOutput, calls=%fused_computation.62 | convolution fusion | flops 557318144 | bytes 13673472 | tf_op jit(solution)/shard_map/tej,tel->tjl/dot_general | solution.py:49
  82.2 1.9 gather_fusion.1
  85.0 6.5 %all-to-all-start = ((bf16[16,32,256]{2,1,0:T(8,128)(2,1)}), bf16[16,32,256]{2,1,0:T(8,128)(2,1)S(1)}, u32[]{:S(2)}, u32[]{:S(2)}) async-start(bf16[16,32,256]{2,1,0:T(8,128)(2,1)} %broadcast_select_fusion.4), calls=%async_computation | async-start | bytes 524288 | tf_op jit(solution)/shard_map/all_to_all | solution.py:163
  91.7 1.8 fusion.33
  93.5 5.9 %all-to-all-done = bf16[16,32,256]{2,1,0:T(8,128)(2,1)S(1)} async-done(((bf16[16,32,256]{2,1,0:T(8,128)(2,1)}), bf16[16,32,256]{2,1,0:T(8,128)(2,1)S(1)}, u32[]{:S(2)}, u32[]{:S(2)}) %all-to-all-start) | async-done | bytes 262176 | tf_op jit(solution)/shard_map/all_to_all | solution.py:163
  99.5 7.5 %gather_fusion.2 = bf16[2048,256]{1,0:T(8,128)(2,1)S(1)} fusion(bf16[1024,256]{1,0:T(8,128)(2,1)S(1)} %pad_maximum_fusion.3, s32[2048]{0:T(1024)S(1)} %fusion.89), kind=kCustom, calls=%fused_computation.4 | custom fusion | bytes 2105344 | tf_op jit(solution)/shard_map/jit(_take)/gather | solution.py:40
  107.0 2.9 convolution_convert_fusion.5
  111.6 2.3 convert_reduce_fusion.2
  113.9 2.3 fusion.14
  116.2 12.6 %scatter_custom_fusion = f32[1024,256]{1,0:T(8,128)} fusion(s32[2048]{0:T(1024)S(1)} %copy-done.25, bf16[2048,256]{1,0:T(8,128)(2,1)S(1)} %fusion.14, f32[]{:T(128)} %constant.53.clone.1), kind=kCustom, calls=%fused_computation.47 | custom fusion | flops 1048576 | bytes 2097156 | tf_op jit(solution)/shard_map/scatter-add | solution.py:93
  132.5 5.5 %all-to-all-start.1 = ((bf16[16,32,256]{2,1,0:T(8,128)(2,1)}), bf16[16,32,256]{2,1,0:T(8,128)(2,1)S(1)}, u32[]{:S(2)}, u32[]{:S(2)}) async-start(bf16[16,32,256]{2,1,0:T(8,128)(2,1)} %bitcast.22), calls=%async_computation.1 | async-start | bytes 524288 | tf_op jit(solution)/shard_map/all_to_all | solution.py:173
  141.3 4.7 %all-to-all-done.1 = bf16[16,32,256]{2,1,0:T(8,128)(2,1)S(1)} async-done(((bf16[16,32,256]{2,1,0:T(8,128)(2,1)}), bf16[16,32,256]{2,1,0:T(8,128)(2,1)S(1)}, u32[]{:S(2)}, u32[]{:S(2)}) %all-to-all-start.1) | async-done | bytes 262176 | tf_op jit(solution)/shard_map/all_to_all | solution.py:173
  146.0 3.8 scatter_custom_fusion.1
  151.9 5.2 %multiply_convert_fusion.3 = (bf16[2048,256]{1,0:T(8,128)(2,1)S(1)}, f32[2048,256]{1,0:T(8,128)}) fusion(f32[2048,256]{1,0:T(8,128)} %copy-done.9, f32[512,256]{1,0:T(8,128)} %convolution_add_fusion.5, bf16[512,256]{1,0:T(8,128)(2,1)} %bitcast.160, f32[512]{0:T(512)S(1)} %copy-done.37, bf16[4,256,256]{2,1,0:T(8,128)(2,1)S(1)} %copy-done.13, ...), kind=kOutput, calls=%fused_computation.45 | convolution fusion | flops 611188736 | bytes 7219200 | tf_op jit(solution)/shard_map/dot_general | solution.py:26
  157.1 2.9 convolution_bitcast_fusion.5
  162.8 10.3 %convert_reduce_fusion = (f32[256]{0:T(256)S(1)}, bf16[16,512,256]{2,1,0:T(8,128)(2,1)}, f32[16,512,256]{2,1,0:T(8,128)S(1)}) fusion(f32[256]{0:T(256)S(1)} %bitcast.167, f32[16,512,256]{2,1,0:T(8,128)} %fusion.7, bf16[16,512,256]{2,1,0:T(8,128)(2,1)S(1)} %bitcast.146, pred[16,512]{1,0:T(8,128)(4,1)S(1)} %copy-done.27, ...), kind=kOutput, calls=%fused_computation.13 | convolution fusion | flops 569376512 | bytes 26257408 | tf_op jit(solution)/shard_map/tej,tjl->tel/dot_general | solution.py:75
  173.1 6.9 %fusion.1 = bf16[8192,256]{1,0:T(8,128)(2,1)} fusion(f32[16,512,256]{2,1,0:T(8,128)S(1)} %get-tuple-element.30, f32[16,512,256]{2,1,0:T(8,128)S(1)} %bitcast.144, f32[256]{0:T(256)S(1)} %bitcast.168, bf16[8192,256]{1,0:T(8,128)(2,1)S(1)} %copy-done.1, pred[8192]{0:T(1024)(128)(4,1)S(1)} %compare_and_fusion), kind=kLoop, calls=%fused_computation.12 | loop fusion | flops 27262976 | bytes 25175040 | tf_op jit(solution)/shard_map/convert_element_type | solution.py:81
  179.9 42.4 %scatter_custom_fusion.2 = f32[2560,256]{1,0:T(8,128)} fusion(s32[8192]{0:T(1024)S(1)} %copy-done.23, bf16[8192,256]{1,0:T(8,128)(2,1)} %fusion.1, f32[]{:T(128)} %constant.53.clone.1), kind=kCustom, calls=%fused_computation.15 | custom fusion | flops 4194304 | bytes 6815748 | tf_op jit(solution)/shard_map/scatter-add | solution.py:93
  222.4 2.0 convert_element_type.191
  225.3 2.1 collective-permute-start.2
  227.4 4.4 %collective-permute-start.3 = (bf16[256,256]{1,0:T(8,128)(2,1)}, bf16[256,256]{1,0:T(8,128)(2,1)}, u32[]{:S(2)}, u32[]{:S(2)}) collective-permute-start(bf16[256,256]{1,0:T(8,128)(2,1)} %get-tuple-element.22), channel_id=1, source_target_pairs={{0,1},{1,2},{2,3},{3,4},{4,5},{5,6},{6,7},{7,8},{8,9},{9,10},{10,1... | collective-permute-start | bytes 393224 | tf_op jit(solution)/shard_map/ppermute | solution.py:10
  234.7 21.7 %all-reduce = (f32[1,256]{1,0:T(1,128)S(1)}, f32[1,256]{1,0:T(1,128)S(1)}) all-reduce(f32[1,256]{1,0:T(1,128)S(1)} %bitcast.175, f32[1,256]{1,0:T(1,128)S(1)} %bitcast.176), channel_id=1, replica_groups=mesh['groups'=2,'dom'=16] {'dom'}, use_global_device_ids=true, to_apply=%region_10.12 | all-reduce | flops 512 | bytes 4096 | tf_op jit(solution)/shard_map/psum | solution.py:199
  257.0 2.2 pad_maximum_fusion.2
  259.2 4.8 %scatter_custom_fusion.3 = f32[2048,256]{1,0:T(8,128)S(1)} fusion(f32[2048,256]{1,0:T(8,128)S(1)} %slice_convert_fusion, s32[512]{0:T(512)} %bitcast.174, bf16[256,256]{1,0:T(8,128)(2,1)} %collective-permute-done.3, bf16[]{:T(256)} %constant.82, bf16[256,256]{1,0:T(8,128)(2,1)} %collective-permute-done.2), kind=kCustom, calls=%fused_computation.101 | custom fusion | flops 655360 | bytes 2359808 | tf_op jit(solution)/shard_map/scatter-add | solution.py:114
  266.7 2.2 convolution_add_fusion.2
  271.9 95.7 %all-reduce.4.cloned.1.call-done = (f32[4,256,256]{1,2,0:T(8,128)}, f32[4,256,256]{1,2,0:T(8,128)}) async-done(((f32[4,256,256]{1,2,0:T(8,128)}, f32[4,256,256]{1,2,0:T(8,128)}), (f32[4,256,256]{1,2,0:T(8,128)}, f32[4,256,256]{1,2,0:T(8,128)})) %all-reduce.4.cloned.1.call-update) | async-done | bytes 2097168 | tf_op jit(solution)/shard_map/psum | solution.py:199
  (149 shorter events, 47.6 us)
Async XLA Ops:
  7.2 8.2 %copy-start.31 = (s32[256]{0:T(256)S(1)}, s32[256]{0:T(256)}, u32[]{:S(2)}) copy-start(s32[256]{0:T(256)} %param.22) | copy-start | bytes 3076
  8.6 10.6 %copy-start.24 = (s32[16,32]{1,0:T(8,128)S(1)}, s32[16,32]{1,0:T(8,128)}, u32[]{:S(2)}) copy-start(s32[16,32]{1,0:T(8,128)} %param.27) | copy-start | bytes 6148
  8.6 10.7 %copy-start.25 = (s32[2048]{0:T(1024)S(1)}, s32[2048]{0:T(1024)}, u32[]{:S(2)}) copy-start(s32[2048]{0:T(1024)} %param.25) | copy-start | bytes 24580
  8.6 10.8 %copy-start.23 = (s32[8192]{0:T(1024)S(1)}, s32[8192]{0:T(1024)}, u32[]{:S(2)}) copy-start(s32[8192]{0:T(1024)} %param.20) | copy-start | bytes 98308
  8.6 10.8 %copy-start = (bf16[2048,256]{1,0:T(8,128)(2,1)S(1)}, bf16[2048,256]{1,0:T(8,128)(2,1)}, u32[]{:S(2)}) copy-start(bf16[2048,256]{1,0:T(8,128)(2,1)} %param.15) | copy-start | bytes 3145732
  11.6 24.2 %collective-permute-start = (bf16[256,256]{1,0:T(8,128)(2,1)S(1)}, bf16[256,256]{1,0:T(8,128)(2,1)S(1)}, u32[]{:S(2)}, u32[]{:S(2)}) collective-permute-start(bf16[256,256]{1,0:T(8,128)(2,1)S(1)} %broadcast_select_fusion.6), channel_id=1, source_target_pairs={{0,1},{1,2},{2,3},{3,4},{4,5},{5,6},{6,7},{7,8},{8,9},{9,10},{10,1... | collective-permute-start | bytes 393224 | tf_op jit(solution)/shard_map/ppermute | solution.py:10
  17.3 19.1 %collective-permute-start.1 = (bf16[256,256]{1,0:T(8,128)(2,1)}, bf16[256,256]{1,0:T(8,128)(2,1)}, u32[]{:S(2)}, u32[]{:S(2)}) collective-permute-start(bf16[256,256]{1,0:T(8,128)(2,1)} %broadcast_select_fusion.5), channel_id=1, source_target_pairs={{1,0},{2,1},{3,2},{4,3},{5,4},{6,5},{7,6},{8,7},{9,8},{10,9},{11,1... | collective-permute-start | bytes 393224 | tf_op jit(solution)/shard_map/ppermute | solution.py:10
  20.7 3.8 copy-start.33
  28.7 4.6 %copy-start.32 = (s32[256]{0:T(256)S(1)}, s32[256]{0:T(256)}, u32[]{:S(2)}) copy-start(s32[256]{0:T(256)} %param.23) | copy-start | bytes 3076
  37.5 33.0 %copy-start.26 = (pred[16,512]{1,0:T(8,128)(4,1)S(1)}, pred[16,512]{1,0:T(8,128)(4,1)}, u32[]{:S(2)}) copy-start(pred[16,512]{1,0:T(8,128)(4,1)} %broadcast_in_dim.77) | copy-start | bytes 24580
  37.5 33.0 %copy-start.28 = (f32[1,256]{1,0:T(1,128)S(1)}, f32[1,256]{1,0:T(1,128)}, u32[]{:S(2)}) copy-start(f32[1,256]{1,0:T(1,128)} %get-tuple-element.26) | copy-start | bytes 3076
  70.5 7.4 %copy-start.5 = (f32[2048,256]{1,0:T(8,128)S(1)}, f32[2048,256]{1,0:T(8,128)}, u32[]{:S(2)}) copy-start(f32[2048,256]{1,0:T(8,128)} %fusion.67) | copy-start | bytes 6291460
  85.0 14.4 %all-to-all-start = ((bf16[16,32,256]{2,1,0:T(8,128)(2,1)}), bf16[16,32,256]{2,1,0:T(8,128)(2,1)S(1)}, u32[]{:S(2)}, u32[]{:S(2)}) async-start(bf16[16,32,256]{2,1,0:T(8,128)(2,1)} %broadcast_select_fusion.4), calls=%async_computation | async-start | bytes 524288 | tf_op jit(solution)/shard_map/all_to_all | solution.py:163
  99.5 7.5 %copy-start.30 = (f32[1,256]{1,0:T(1,128)S(1)}, f32[1,256]{1,0:T(1,128)}, u32[]{:S(2)}) copy-start(f32[1,256]{1,0:T(1,128)} %get-tuple-element.25) | copy-start | bytes 3076
  99.5 7.5 %copy-start.34 = (pred[4,512]{1,0:T(4,128)(4,1)S(1)}, pred[4,512]{1,0:T(4,128)(4,1)}, u32[]{:S(2)}) copy-start(pred[4,512]{1,0:T(4,128)(4,1)} %broadcast_in_dim.81) | copy-start | bytes 6148
  107.0 4.6 %copy-start.8 = (bf16[2048,256]{1,0:T(8,128)(2,1)}, bf16[2048,256]{1,0:T(8,128)(2,1)S(1)}, u32[]{:S(2)}) copy-start(bf16[2048,256]{1,0:T(8,128)(2,1)S(1)} %gather_fusion.2) | copy-start | bytes 3145732
  107.0 2.9 copy-start.12
  107.0 2.9 copy-start.18
  130.1 9.9 %copy-start.13 = (bf16[4,256,256]{2,1,0:T(8,128)(2,1)S(1)}, bf16[4,256,256]{2,1,0:T(8,128)(2,1)}, u32[]{:S(2)}) copy-start(bf16[4,256,256]{2,1,0:T(8,128)(2,1)} %param.18) | copy-start | bytes 1572868
  131.7 7.4 %copy-start.20 = (bf16[4,128,256]{2,1,0:T(8,128)(2,1)}, bf16[4,128,256]{2,1,0:T(8,128)(2,1)S(1)}, u32[]{:S(2)}) copy-start(bf16[4,128,256]{2,1,0:T(8,128)(2,1)S(1)} %convolution_convert_fusion.3) | copy-start | bytes 786436
  132.5 13.5 %all-to-all-start.1 = ((bf16[16,32,256]{2,1,0:T(8,128)(2,1)}), bf16[16,32,256]{2,1,0:T(8,128)(2,1)S(1)}, u32[]{:S(2)}, u32[]{:S(2)}) async-start(bf16[16,32,256]{2,1,0:T(8,128)(2,1)} %bitcast.22), calls=%async_computation.1 | async-start | bytes 524288 | tf_op jit(solution)/shard_map/all_to_all | solution.py:173
  138.0 229.5 %all-reduce.4.cloned.1.call-start = ((), (), s32[]{:S(2)}) async-start(), calls=%async_computation.2 | async-start | bytes 4194304 | tf_op jit(solution)/shard_map/psum | solution.py:199
  157.1 4.1 %copy-start.2 = (bf16[2048,256]{1,0:T(8,128)(2,1)}, bf16[2048,256]{1,0:T(8,128)(2,1)S(1)}, u32[]{:S(2)}) copy-start(bf16[2048,256]{1,0:T(8,128)(2,1)S(1)} %get-tuple-element.28) | copy-start | bytes 3145732
  157.1 5.6 %copy-start.1 = (bf16[8192,256]{1,0:T(8,128)(2,1)S(1)}, bf16[8192,256]{1,0:T(8,128)(2,1)}, u32[]{:S(2)}) copy-start(bf16[8192,256]{1,0:T(8,128)(2,1)} %gather_fusion) | copy-start | bytes 12582916
  157.1 5.7 %copy-start.27 = (pred[16,512]{1,0:T(8,128)(4,1)S(1)}, pred[16,512]{1,0:T(8,128)(4,1)}, u32[]{:S(2)}) copy-start(pred[16,512]{1,0:T(8,128)(4,1)} %broadcast_in_dim.77) | copy-start | bytes 24580
  157.1 5.7 %copy-start.29 = (f32[1,256]{1,0:T(1,128)S(1)}, f32[1,256]{1,0:T(1,128)}, u32[]{:S(2)}) copy-start(f32[1,256]{1,0:T(1,128)} %get-tuple-element.26) | copy-start | bytes 3076
  160.0 13.1 %slice-start = ((s8[8388608]{0:T(1024)(128)(4,1)}), s8[4194304]{0:T(1024)(128)(4,1)S(1)}, s32[]{:S(2)}) async-start(s8[8388608]{0:T(1024)(128)(4,1)} %bitcast.143), calls=%async_computation.3 | async-start | bytes 8388608
  162.8 10.3 %slice-start.1 = ((s8[8388608]{0:T(1024)(128)(4,1)}), s8[4194304]{0:T(1024)(128)(4,1)S(1)}, s32[]{:S(2)}) async-start(s8[8388608]{0:T(1024)(128)(4,1)} %bitcast.143), calls=%async_computation.4 | async-start | bytes 8388608
  222.4 9.4 %copy-start.38 = (bf16[16,512,256]{2,1,0:T(8,128)(2,1)S(1)}, bf16[16,512,256]{2,1,0:T(8,128)(2,1)}, u32[]{:S(2)}) copy-start(bf16[16,512,256]{2,1,0:T(8,128)(2,1)} %get-tuple-element.18) | copy-start | bytes 12582916
  225.3 33.9 %collective-permute-start.2 = (bf16[256,256]{1,0:T(8,128)(2,1)}, bf16[256,256]{1,0:T(8,128)(2,1)}, u32[]{:S(2)}, u32[]{:S(2)}) collective-permute-start(bf16[256,256]{1,0:T(8,128)(2,1)} %get-tuple-element.21), channel_id=1, source_target_pairs={{1,0},{2,1},{3,2},{4,3},{5,4},{6,5},{7,6},{8,7},{9,8},{10,9},{11,1... | collective-permute-start | bytes 393224 | tf_op jit(solution)/shard_map/ppermute | solution.py:10
  227.4 31.8 %collective-permute-start.3 = (bf16[256,256]{1,0:T(8,128)(2,1)}, bf16[256,256]{1,0:T(8,128)(2,1)}, u32[]{:S(2)}, u32[]{:S(2)}) collective-permute-start(bf16[256,256]{1,0:T(8,128)(2,1)} %get-tuple-element.22), channel_id=1, source_target_pairs={{0,1},{1,2},{2,3},{3,4},{4,5},{5,6},{6,7},{7,8},{8,9},{9,10},{10,1... | collective-permute-start | bytes 393224 | tf_op jit(solution)/shard_map/ppermute | solution.py:10
  232.5 24.5 %copy-start.15 = (f32[1,256,256]{1,2,0:T(8,128)S(1)}, f32[1,256,256]{1,2,0:T(8,128)}, u32[]{:S(2)}) copy-start(f32[1,256,256]{1,2,0:T(8,128)} %convolution_bitcast_fusion.1) | copy-start | bytes 786436
  (16 other events, 24.6 us)
Sparse Core Ops, SparseCore 0:
  266.3 101.2 all-reduce.3
where the time goes:
time: 384 us; the launch traced here: 379 us
  waiting for transfers between devices  106 us (28%)
  other arithmetic  88.4 us (23%)
  matrix products  68.4 us (18%)
  local copies, waits for them, and re-layouts  55.1 us (14%)
  starting transfers between devices  24.1 us (6%)
  blocking collectives  21.7 us (6%)
  between operations  14.8 us (4%)
    psum x1, waiting for transfers between devices, shards(): lax.psum((fine_terms[0], fine_terms[1], coarse_terms[0], coarse_terms[1])...  95.7 us
    scatter-add x2, other arithmetic, edge_back(): jax.ops.segment_sum(grad_z.astype(jnp.float32), src, num_segments=rows_ext)  55 us
    gather x2, local copies, waits for them, and re-layouts, edge_update(): gathered = jnp.take(extended, src, axis=0).astype(jnp.float32)  40.5 us
    psum x1, blocking collectives, shards(): lax.psum((fine_terms[0], fine_terms[1], coarse_terms[0], coarse_terms[1])...  21.7 us
    dot_general x9, matrix products, inner_rows(): lax.dot_general(left, right, (((0,), (0,)), ((), ())), preferred_element_...  14.9 us
    dot_general x2, matrix products, edge_back(): jnp.einsum('tej,tjl->tel', onehot, grad_agg.reshape(tiles, width, latent)...  12.6 us
    ppermute x4, starting transfers between devices, shifted(): return lax.ppermute(block, axis, route)  12.1 us
    dot_general x2, matrix products, edge_update(): jnp.einsum('tej,tel->tjl', onehot, message.reshape(tiles, per_tile, laten...  10.2 us
  transfers between devices with their start and end apart: 7, of which 3 were waited for; matrix products, arithmetic and copies ran while one was open for 9% of the time, Pallas kernels for 0%

commit v1 on v0

v1 whole, which is shorter than its diff:
```python
import functools

import jax
import jax.numpy as jnp
from jax import lax
from jax.experimental import pallas as pl
from jax.experimental.pallas import tpu as pltpu
from jax.sharding import PartitionSpec as P

bf = jnp.bfloat16
f32 = jnp.float32
TILE = 128
LANES = 128


def mm(a, b):
    return jnp.dot(a, b, preferred_element_type=f32)


def mm_tn(a, b):
    return lax.dot_general(a, b, (((0,), (0,)), ((), ())), preferred_element_type=f32)


def mm_nt(a, b):
    return lax.dot_general(a, b, (((1,), (1,)), ((), ())), preferred_element_type=f32)


def as_bf(x):
    return x.astype(f32).astype(bf)


def row_form(ref, first, count):
    return jnp.concatenate([ref[pl.ds(first + j, 1), :] for j in range(count)], axis=1)


def hot_rows(row, rows):
    cols = row.shape[1]
    if rows <= 256:
        io = as_bf(lax.broadcasted_iota(jnp.int32, (rows, cols), 0))
        return jnp.where(io == as_bf(row), bf(1), bf(0))
    low = as_bf(row & 255)
    high = as_bf(lax.shift_right_arithmetic(row, 8))
    io = as_bf(lax.broadcasted_iota(jnp.int32, (256, cols), 0))
    base = jnp.where(io == low, bf(1), bf(0))
    return jnp.concatenate(
        [jnp.where(high == bf(k), base, bf(0)) for k in range(rows // 256)], axis=0
    )


def silu_parts(v):
    sig = jax.nn.sigmoid(v)
    return v * sig, sig * (1.0 + v * (1.0 - sig))


def call(kernel, outs, args, grid=(), specs=None, out_specs=None, scratch=(), cost=(0, 0)):
    def whole(a):
        return pl.BlockSpec(a.shape, lambda *_: (0,) * len(a.shape))

    in_specs = [whole(a) for a in args]
    o_specs = [whole(o) for o in outs]
    for k, s in (specs or {}).items():
        in_specs[k] = s
    for k, s in (out_specs or {}).items():
        o_specs[k] = s
    return pl.pallas_call(
        kernel,
        grid=grid or (1,),
        in_specs=in_specs,
        out_specs=o_specs,
        out_shape=outs,
        scratch_shapes=list(scratch),
        compiler_params=pltpu.CompilerParams(vmem_limit_bytes=56 << 20),
        cost_estimate=pl.CostEstimate(
            flops=int(cost[0]), bytes_accessed=int(cost[1]), transcendentals=0
        ),
    )(*args)


def sds(shape, dtype):
    return jax.ShapeDtypeStruct(shape, dtype)


def halo_kernel(h_ref, right_ref, left_ref, to_right_ref, to_left_ref):
    h = h_ref[...]
    n = right_ref.shape[0]
    to_right_ref[...] = mm_tn(hot_rows(row_form(right_ref, 0, n), h.shape[0]), h).astype(bf)
    to_left_ref[...] = mm_tn(hot_rows(row_form(left_ref, 0, n), h.shape[0]), h).astype(bf)


def own_kernel(per, h_ref, w_ref, b_ref, src_ref, dst_ref, z_ref, p_ref, q_ref):
    t = pl.program_id(0)

    @pl.when(t == 0)
    def _():
        h = h_ref[...]
        p_ref[...] = mm(h, w_ref[0]).astype(bf)
        q_ref[...] = mm(h, w_ref[1]).astype(bf)

    src = row_form(src_ref, t * per, per)
    dst = row_form(dst_ref, t * per, per)
    qt = q_ref[pl.ds(pl.multiple_of(t * TILE, TILE), TILE), :]
    z_ref[...] = (
        mm_tn(hot_rows(src, p_ref.shape[0]), p_ref[...])
        + mm_tn(hot_rows(dst, TILE), qt)
        + b_ref[0:1, :]
    )


def fine_kernel(
    per, tiles, z_ref, left_ref, right_ref, h_ref, w_ref, src_ref, dst_ref, pool_ref, send_ref,
    d_ref, agg_ref, dsu_ref, pooled_ref, out_ref, count_ref, halo_p,
):
    t = pl.program_id(0)
    nodes = h_ref.shape[0]
    halo = left_ref.shape[0]

    @pl.when(t == 0)
    def _():
        halo_p[0:halo, :] = mm(left_ref[...], w_ref[0]).astype(bf)
        halo_p[halo : 2 * halo, :] = mm(right_ref[...], w_ref[0]).astype(bf)

    src = row_form(src_ref, t * per, per) - nodes
    dst = row_form(dst_ref, t * per, per)
    z = z_ref[...] + mm_tn(hot_rows(src, 2 * halo), halo_p[...])
    m, d = silu_parts(z)
    d_ref[...] = d.astype(bf)
    rows = pl.ds(pl.multiple_of(t * TILE, TILE), TILE)
    agg_ref[rows, :] = mm(hot_rows(dst, TILE), m.astype(bf)).astype(bf)

    @pl.when(t == tiles - 1)
    def _():
        h = h_ref[...]
        u = mm(h, w_ref[3]) + mm(agg_ref[...], w_ref[2])
        su, dsu = silu_parts(u)
        dsu_ref[...] = dsu.astype(bf)
        h1 = (h.astype(f32) + su).astype(bf)
        coarse = pooled_ref.shape[0]
        hot = hot_rows(row_form(pool_ref, 0, pool_ref.shape[0]), coarse)
        count = mm(hot, jnp.ones((nodes, LANES), bf))
        count_ref[...] = count
        pooled = (mm(hot, h1) / jnp.concatenate([count, count], axis=1)).astype(bf)
        pooled_ref[...] = pooled
        sends = hot_rows(row_form(send_ref, 0, send_ref.shape[0]), coarse)
        out_ref[...] = mm_tn(sends, pooled).astype(bf)


def coarse_own_kernel(
    per, pooled_ref, w_ref, b_ref, src_ref, dst_ref, pool_ref, cot_ref, z_ref, ghc_ref, u_ref
):
    pooled = pooled_ref[...]
    coarse = pooled.shape[0]
    proj = mm(pooled, w_ref[0]).astype(bf)
    recv = mm(pooled, w_ref[1]).astype(bf)
    u_ref[...] = mm(pooled, w_ref[3])
    edges = per * LANES
    for t in range(coarse // TILE):
        src = row_form(src_ref, t * per, per)
        dst = row_form(dst_ref, t * per, per)
        z_ref[t * edges : (t + 1) * edges, :] = (
            mm_tn(hot_rows(src, coarse), proj)
            + mm_tn(hot_rows(dst, TILE), recv[t * TILE : (t + 1) * TILE, :])
            + b_ref[1:2, :]
        )
    hot = hot_rows(row_form(pool_ref, 0, pool_ref.shape[0]), coarse)
    ghc_ref[...] = mm(hot, cot_ref[...])


def coarse_kernel(
    per, z_ref, in_ref, ghc_ref, u_ref, w_ref, src_ref, dst_ref,
    own_ref, back_ref, dz_ref, du_ref, agg_ref, deriv,
):
    coarse = ghc_ref.shape[0]
    edges = per * LANES
    tiles = coarse // TILE
    proj = mm(in_ref[...], w_ref[0]).astype(bf)
    for t in range(tiles):
        src = row_form(src_ref, t * per, per) - coarse
        dst = row_form(dst_ref, t * per, per)
        z = z_ref[t * edges : (t + 1) * edges, :] + mm_tn(hot_rows(src, proj.shape[0]), proj)
        m, d = silu_parts(z)
        deriv[t * edges : (t + 1) * edges, :] = d
        agg_ref[t * TILE : (t + 1) * TILE, :] = mm(hot_rows(dst, TILE), m.astype(bf)).astype(bf)
    u = u_ref[...] + mm(agg_ref[...], w_ref[2])
    _, dsu = silu_parts(u)
    du = (ghc_ref[...] * dsu).astype(bf)
    du_ref[...] = du
    dagg = mm_nt(du, w_ref[2]).astype(bf)
    total = None
    for t in range(tiles):
        src = row_form(src_ref, t * per, per)
        dst = row_form(dst_ref, t * per, per)
        gm = mm_tn(hot_rows(dst, TILE), dagg[t * TILE : (t + 1) * TILE, :])
        dz = (gm * deriv[t * edges : (t + 1) * edges, :]).astype(bf)
        dz_ref[t * edges : (t + 1) * edges, :] = dz
        part = mm(hot_rows(src, coarse + proj.shape[0]), dz)
        total = part if total is None else total + part
    own_ref[...] = total[:coarse].astype(bf)
    back_ref[...] = total[coarse:].astype(bf)


def coarse_grad_kernel(
    per, pooled_ref, in_ref, ghc_ref, w_ref, dst_ref, own_ref, back_ref, dz_ref, du_ref, agg_ref,
    gw_ref, gb_ref, part_ref,
):
    pooled = pooled_ref[...]
    coarse, width = pooled.shape
    edges = per * LANES
    dqs = []
    gb = jnp.zeros((1, width), f32)
    for t in range(coarse // TILE):
        dst = row_form(dst_ref, t * per, per)
        dq = mm(hot_rows(dst, TILE), dz_ref[t * edges : (t + 1) * edges, :])
        gb = gb + jnp.sum(dq, axis=0, keepdims=True)
        dqs.append(dq.astype(bf))
    dq = jnp.concatenate(dqs, axis=0)
    du = du_ref[...]
    gb_ref[...] = jnp.broadcast_to(gb, gb_ref.shape)
    gw_ref[0:width, :] = (mm_tn(pooled, own_ref[...]) + mm_tn(in_ref[...], back_ref[...])).astype(bf)
    gw_ref[width : 2 * width, :] = mm_tn(pooled, dq).astype(bf)
    gw_ref[2 * width : 3 * width, :] = mm_tn(agg_ref[...], du).astype(bf)
    gw_ref[3 * width : 4 * width, :] = mm_tn(pooled, du).astype(bf)
    part_ref[...] = ghc_ref[...] + mm_nt(du, w_ref[3]) + mm_nt(dq, w_ref[1])


def node_back_kernel(
    own_ref, ret_ref, send_ref, part_ref, wc_ref, count_ref, pool_ref, cot_ref, dsu_ref, w_ref,
    g_ref, du_ref, dagg_ref,
):
    coarse = own_ref.shape[0]
    sends = hot_rows(row_form(send_ref, 0, send_ref.shape[0]), coarse)
    dp = (own_ref[...].astype(f32) + mm(sends, ret_ref[...])).astype(bf)
    dc = part_ref[...] + mm_nt(dp, wc_ref[0])
    count = count_ref[...]
    dcs = (dc / jnp.concatenate([count, count], axis=1)).astype(bf)
    hot = hot_rows(row_form(pool_ref, 0, pool_ref.shape[0]), coarse)
    g = cot_ref[...].astype(f32) + mm_tn(hot, dcs)
    g_ref[...] = g
    du = (g * dsu_ref[...].astype(f32)).astype(bf)
    du_ref[...] = du
    dagg_ref[...] = mm_nt(du, w_ref[2]).astype(bf)


def edge_back_kernel(
    per, tiles, d_ref, dagg_ref, h_ref, left_ref, right_ref, src_ref, dst_ref,
    own_ref, gl_ref, gr_ref, dq_ref, gw_ref, gb_ref, acc,
):
    t = pl.program_id(0)
    nodes = h_ref.shape[0]
    halo = left_ref.shape[0]

    @pl.when(t == 0)
    def _():
        acc[...] = jnp.zeros_like(acc)
        gb_ref[...] = jnp.zeros_like(gb_ref)

    src = row_form(src_ref, t * per, per)
    dst = row_form(dst_ref, t * per, per)
    hot = hot_rows(dst, TILE)
    rows = pl.ds(pl.multiple_of(t * TILE, TILE), TILE)
    gm = mm_tn(hot, dagg_ref[rows, :])
    dz = (gm * d_ref[...].astype(f32)).astype(bf)
    dq = mm(hot, dz)
    gb_ref[...] += jnp.sum(dq, axis=0, keepdims=True)
    dq_ref[rows, :] = dq.astype(bf)
    acc[...] += mm(hot_rows(src, acc.shape[0]), dz)

    @pl.when(t == tiles - 1)
    def _():
        own = acc[0:nodes, :].astype(bf)
        gl = acc[nodes : nodes + halo, :].astype(bf)
        gr = acc[nodes + halo : nodes + 2 * halo, :].astype(bf)
        own_ref[...] = own
        gl_ref[...] = gl
        gr_ref[...] = gr
        gw_ref[...] = (
            mm_tn(h_ref[...], own) + mm_tn(left_ref[...], gl) + mm_tn(right_ref[...], gr)
        ).astype(bf)


def fine_grad_kernel(h_ref, dq_ref, du_ref, agg_ref, g_ref, w_ref, gw_ref, part_ref):
    h = h_ref[...]
    width = h.shape[1]
    dq = dq_ref[...]
    du = du_ref[...]
    gw_ref[0:width, :] = mm_tn(h, dq).astype(bf)
    gw_ref[width : 2 * width, :] = mm_tn(agg_ref[...], du).astype(bf)
    gw_ref[2 * width : 3 * width, :] = mm_tn(h, du).astype(bf)
    part_ref[...] = g_ref[...] + mm_nt(du, w_ref[3]) + mm_nt(dq, w_ref[1])


def input_kernel(own_ref, from_right_ref, from_left_ref, right_ref, left_ref, part_ref, w_ref, o_ref):
    nodes = own_ref.shape[0]
    n = right_ref.shape[0]
    add = mm(hot_rows(row_form(right_ref, 0, n), nodes), from_right_ref[...]) + mm(
        hot_rows(row_form(left_ref, 0, n), nodes), from_left_ref[...]
    )
    dp = (own_ref[...].astype(f32) + add).astype(bf)
    o_ref[...] = part_ref[...] + mm_nt(dp, w_ref[0])


def shifted(block, axis, distance):
    devices = range(lax.axis_size(axis))
    route = [(i - distance, i) for i in devices if i - distance in devices]
    return lax.ppermute(block, axis, route)


def exchange(block, parts):
    rows, width = block.shape
    got = lax.all_to_all(
        block.reshape(parts, rows // parts, width), "dom", split_axis=0, concat_axis=0, tiled=True
    )
    return got


def reduced(block, parts):
    rows, width = block.shape
    mine = jnp.sum(exchange(block, parts).astype(f32), axis=0).astype(bf)
    spread = jnp.broadcast_to(mine[None], (parts,) + mine.shape)
    full = lax.all_to_all(spread, "dom", split_axis=0, concat_axis=0, tiled=True)
    return full.reshape(rows, width)


def shards(
    features, cotangent, w_fine, w_coarse, bias, fine_src, fine_dst, send_left, send_right,
    pool_map, coarse_src, coarse_dst, coarse_send,
):
    nodes, width = features.shape
    parts = lax.axis_size("dom")
    coarse = nodes // 4
    tiles = nodes // TILE
    halo = send_left.shape[0]
    per = fine_src.shape[0] // tiles // LANES
    edges = per * LANES
    fsrc, fdst = fine_src.reshape(-1, LANES), fine_dst.reshape(-1, LANES)
    csrc, cdst = coarse_src.reshape(-1, LANES), coarse_dst.reshape(-1, LANES)
    right, left = send_right.reshape(-1, LANES), send_left.reshape(-1, LANES)
    pool = pool_map.reshape(-1, LANES)
    csend = coarse_send.reshape(-1, LANES)
    crows = coarse_send.shape[0] * coarse_send.shape[1]
    part = functools.partial

    to_right, to_left = call(
        halo_kernel, [sds((halo, width), bf)] * 2, [features, right, left]
    )
    h_left = shifted(to_right, "dom", 1)
    h_right = shifted(to_left, "dom", -1)
    edge_tile = pl.BlockSpec((edges, width), lambda t: (t, 0))
    (z_own,) = call(
        part(own_kernel, per),
        [sds((tiles * edges, width), f32)],
        [features, w_fine, bias, fsrc, fdst],
        grid=(tiles,),
        out_specs={0: edge_tile},
        scratch=[pltpu.VMEM((nodes, width), bf)] * 2,
        cost=(9e9, 10e6),
    )
    d_edge, agg, dsu, pooled, outgoing, count = call(
        part(fine_kernel, per, tiles),
        [
            sds((tiles * edges, width), bf),
            sds((nodes, width), bf),
            sds((nodes, width), bf),
            sds((coarse, width), bf),
            sds((crows, width), bf),
            sds((coarse, LANES), f32),
        ],
        [z_own, h_left, h_right, features, w_fine, fsrc, fdst, pool, csend],
        grid=(tiles,),
        specs={0: edge_tile},
        out_specs={0: edge_tile},
        scratch=[pltpu.VMEM((2 * halo, width), bf)],
    )
    incoming = exchange(outgoing, parts).reshape(crows, width)
    cedges = coarse_src.shape[0]
    zc, ghc, uc = call(
        part(coarse_own_kernel, per),
        [sds((cedges, width), f32), sds((coarse, width), f32), sds((coarse, width), f32)],
        [pooled, w_coarse, bias, csrc, cdst, pool, cotangent],
        cost=(4e9, 10e6),
    )
    own_c, back_c, dz_c, du_c, agg_c = call(
        part(coarse_kernel, per),
        [
            sds((coarse, width), bf),
            sds((crows, width), bf),
            sds((cedges, width), bf),
            sds((coarse, width), bf),
            sds((coarse, width), bf),
        ],
        [zc, incoming, ghc, uc, w_coarse, csrc, cdst],
        scratch=[pltpu.VMEM((cedges, width), f32)],
    )
    returned = exchange(back_c, parts).reshape(crows, width)
    gw_c, gb_c, part_c = call(
        part(coarse_grad_kernel, per),
        [sds((4 * width, width), bf), sds((8, width), f32), sds((coarse, width), f32)],
        [pooled, incoming, ghc, w_coarse, cdst, own_c, back_c, dz_c, du_c, agg_c],
        cost=(4e9, 10e6),
    )
    g, du, dagg = call(
        node_back_kernel,
        [sds((nodes, width), f32), sds((nodes, width), bf), sds((nodes, width), bf)],
        [own_c, returned, csend, part_c, w_coarse, count, pool, cotangent, dsu, w_fine],
    )
    own_f, gl, gr, dq, gw0, gb_f = call(
        part(edge_back_kernel, per, tiles),
        [
            sds((nodes, width), bf),
            sds((halo, width), bf),
            sds((halo, width), bf),
            sds((nodes, width), bf),
            sds((width, width), bf),
            sds((8, width), f32),
        ],
        [d_edge, dagg, features, h_left, h_right, fsrc, fdst],
        grid=(tiles,),
        specs={0: edge_tile},
        scratch=[pltpu.VMEM((nodes + 2 * halo, width), f32)],
    )
    from_right = shifted(gl, "dom", -1)
    from_left = shifted(gr, "dom", 1)
    gw_rest, part_f = call(
        fine_grad_kernel,
        [sds((3 * width, width), bf), sds((nodes, width), f32)],
        [features, dq, du, agg, g, w_fine],
    )
    (grad_input,) = call(
        input_kernel,
        [sds((nodes, width), f32)],
        [own_f, from_right, from_left, right, left, part_f, w_fine],
    )
    scale = 1.0 / float(nodes * parts // 256)
    total = reduced(jnp.concatenate([gw_c, gw0, gw_rest], axis=0), parts).astype(f32) * scale
    total = total.reshape(8, width, width)
    gb = jnp.stack([gb_f[0], gb_c[0]])
    spread = jnp.broadcast_to(gb[None], (parts,) + gb.shape)
    gbs = lax.all_to_all(spread, "dom", split_axis=0, concat_axis=0, tiled=True)
    grad_bias = jnp.sum(gbs, axis=0) * scale
    return (grad_input, total[4:], total[:4], grad_bias)


def solution(mesh):
    return jax.shard_map(
        shards,
        mesh=mesh,
        in_specs=(
            P(("groups", "dom"), None),
            P(("groups", "dom"), None),
            P(),
            P(),
            P(),
            P("dom"),
            P("dom"),
            P("dom"),
            P("dom"),
            P("dom"),
            P("dom"),
            P("dom"),
            P("dom", None),
        ),
        out_specs=(
            P(("groups", "dom"), None),
            P("groups", None, None),
            P("groups", None, None),
            P("groups", None),
        ),
        check_vma=False,
    )
```

time: 384 us -> 203 us (0.53)
  Pallas kernels: 0 us -> 94.9 us
  other arithmetic: 88.4 us -> 3 us
  matrix products: 68.4 us -> 0 us
  waiting for transfers between devices: 106 us -> 53.9 us
  local copies, waits for them, and re-layouts: 55.1 us -> 8.05 us
  blocking collectives: 21.7 us -> 0 us
  starting transfers between devices: 24.1 us -> 40.9 us
  between operations: 14.8 us -> 0.75 us
    psum x1 -> x0, waiting for transfers between devices: 95.7 us -> none  [shards(): lax.psum((fine_terms[0], fine_terms[1], coarse_terms[0], coarse_terms[1])...]
    pallas_call x0 -> x10, Pallas kernels: none -> 94.9 us  [call(): pl.pallas_call(kernel, grid=grid or (1,), in_specs=in_specs, out_specs=o_...]
    dot_general x34 -> x0, matrix products: 68.4 us -> none  [the longest x9 14.9 us: inner_rows(): lax.dot_general(left, right, (((0,), (0,)), ((), ())), preferred_element_...]
    scatter-add x4 -> x0, other arithmetic: 63.6 us -> none  [the longest x2 55 us: edge_back(): jax.ops.segment_sum(grad_z.astype(jnp.float32), src, num_segments=rows_ext)]
    gather x5 -> x0, local copies, waits for them, and re-layouts: 44.7 us -> none  [the longest x2 40.5 us: edge_update(): gathered = jnp.take(extended, src, axis=0).astype(jnp.float32)]
    all_to_all x2 -> x5, waiting for transfers between devices: 10.6 us -> 34.7 us  [the longest x3 30.7 us: exchange(): lax.all_to_all(block.reshape(parts, rows // parts, width), 'dom', split_a...]
    psum x1 -> x0, blocking collectives: 21.7 us -> none  [shards(): lax.psum((fine_terms[0], fine_terms[1], coarse_terms[0], coarse_terms[1])...]
    ppermute x4, waiting for transfers between devices: 0.01 us -> 19.2 us  [shifted(): return lax.ppermute(block, axis, route)]
  transfers between devices with their start and end apart: 7 -> 9, of which waited for: 3 -> 5; matrix products, arithmetic and copies ran while one was open for 9% -> 1% of each run, Pallas kernels for 0% -> 15%
where the time goes in v1:
time: 203 us; the launch traced here: 201 us
  Pallas kernels  94.9 us (47%)
  waiting for transfers between devices  53.9 us (27%)
  starting transfers between devices  40.9 us (20%)
  local copies, waits for them, and re-layouts  8.05 us (4%)
  other arithmetic  3 us (1%)
    pallas_call x10, Pallas kernels, call(): pl.pallas_call(kernel, grid=grid or (1,), in_specs=in_specs, out_specs=o_...  94.9 us
    all_to_all x3, waiting for transfers between devices, exchange(): lax.all_to_all(block.reshape(parts, rows // parts, width), 'dom', split_a...  30.7 us
    ppermute x4, waiting for transfers between devices, shifted(): return lax.ppermute(block, axis, route)  19.2 us
    all_to_all x3, starting transfers between devices, exchange(): lax.all_to_all(block.reshape(parts, rows // parts, width), 'dom', split_a...  17.8 us
    ppermute x4, starting transfers between devices, shifted(): return lax.ppermute(block, axis, route)  12.1 us
    all_to_all x1, starting transfers between devices, reduced(): lax.all_to_all(spread, 'dom', split_axis=0, concat_axis=0, tiled=True)  6.05 us
    all_to_all x1, starting transfers between devices, shards(): gbs = lax.all_to_all(spread, 'dom', split_axis=0, concat_axis=0, tiled=True)  4.91 us
  transfers between devices with their start and end apart: 9, of which 5 were waited for; matrix products, arithmetic and copies ran while one was open for 1% of the time, Pallas kernels for 15%

profile of v1, /device:TPU:13, one launch (start us, length us, event | category | flops | bytes accessed | tf_op | source)
XLA Modules:
  0.0 201.5 jit_solution(18234149349145127915)
XLA Ops:
  0.6 2.7 %shard_map.157 = (bf16[256,256]{1,0:T(8,128)(2,1)}, bf16[256,256]{1,0:T(8,128)(2,1)}) custom-call(bf16[2048,256]{1,0:T(8,128)(2,1)} %h_ref.9, s32[2,128]{1,0:T(2,128)} %bitcast.35, s32[2,128]{1,0:T(2,128)} %bitcast.37), custom_call_target="tpu_custom_call" | custom-call | tf_op jit(solution)/shard_map/pallas_call | solution.py:65
  3.3 3.7 %collective-permute-start = (bf16[256,256]{1,0:T(8,128)(2,1)}, bf16[256,256]{1,0:T(8,128)(2,1)S(1)}, u32[]{:S(2)}, u32[]{:S(2)}) collective-permute-start(bf16[256,256]{1,0:T(8,128)(2,1)} %get-tuple-element.34), channel_id=1, source_target_pairs={{0,1},{1,2},{2,3},{3,4},{4,5},{5,6},{6,7},{7,8},{8,9},{9,10},{10,1... | collective-permute-start | bytes 393224 | tf_op jit(solution)/shard_map/ppermute | solution.py:304
  7.0 1.9 collective-permute-start.1
  9.0 16.4 %shard_map.156.z_ref = f32[8192,256]{1,0:T(8,128)} custom-call(bf16[2048,256]{1,0:T(8,128)(2,1)} %h_ref.9, bf16[4,256,256]{2,1,0:T(8,128)(2,1)} %w_ref.15, f32[2,256]{1,0:T(2,128)} %b_ref.3, s32[64,128]{1,0:T(8,128)} %bitcast.21, s32[64,128]{1,0:T(8,128)} %bitcast.24), custom_call_target="tpu_custom_call" | custom-call | flops 8999999488 | bytes 10000000 | tf_op jit(solution)/shard_map/pallas_call | solution.py:65
  25.4 0.7 reshape.65.send_ref
  26.7 19.3 %shard_map.158 = (bf16[8192,256]{1,0:T(8,128)(2,1)}, bf16[2048,256]{1,0:T(8,128)(2,1)}, bf16[2048,256]{1,0:T(8,128)(2,1)}, bf16[512,256]{1,0:T(8,128)(2,1)}, bf1...) custom-call(f32[8192,256]{1,0:T(8,128)} %shard_map.156.z_ref, bf16[256,256]{1,0:T(8,128)(2,1)} %copy-done.2, ...), custom_call_target="tpu_custom_call" | custom-call | tf_op jit(solution)/shard_map/pallas_call | solution.py:65
  46.0 6.6 %all-to-all-start = ((bf16[16,32,256]{2,1,0:T(8,128)(2,1)}), bf16[16,32,256]{2,1,0:T(8,128)(2,1)S(1)}, u32[]{:S(2)}, u32[]{:S(2)}) async-start(bf16[16,32,256]{2,1,0:T(8,128)(2,1)} %bitcast.20), calls=%async_computation | async-start | bytes 524288 | tf_op jit(solution)/shard_map/all_to_all | solution.py:309
  52.6 4.9 %shard_map.159 = (f32[2048,256]{1,0:T(8,128)}, f32[512,256]{1,0:T(8,128)}, f32[512,256]{1,0:T(8,128)}) custom-call(bf16[512,256]{1,0:T(8,128)(2,1)} %get-tuple-element.37.pooled_ref, bf16[4,256,256]{2,1,0:T(8,128)(2,1)} %wc_ref.1, f32[2,256]{1,0:T(2,128)} %b_ref.3, s32[16,128]{1,0:T(8,128)} %bitcast.30, s32[16,128]{1,0:T(8,128)} %bitcast.32, ...), custom_call_target="tpu_custom_call" | custom-call | flops 4000000000 | bytes 10000000 | tf_op jit(solution)/shard_map/pallas_call | solution.py:65
  57.5 3.1 %all-to-all-done = bf16[16,32,256]{2,1,0:T(8,128)(2,1)S(1)} async-done(((bf16[16,32,256]{2,1,0:T(8,128)(2,1)}), bf16[16,32,256]{2,1,0:T(8,128)(2,1)S(1)}, u32[]{:S(2)}, u32[]{:S(2)}) %all-to-all-start) | async-done | bytes 262176 | tf_op jit(solution)/shard_map/all_to_all | solution.py:309
  60.6 0.7 copy-done.1
  61.3 7.9 %shard_map.160 = (bf16[512,256]{1,0:T(8,128)(2,1)}, bf16[512,256]{1,0:T(8,128)(2,1)}, bf16[2048,256]{1,0:T(8,128)(2,1)}, bf16[512,256]{1,0:T(8,128)(2,1)}, bf16[512,256]{1,0:T(8,128)(2,1)}) custom-call(f32[2048,256]{1,0:T(8,128)} %get-tuple-element.38.z_ref, bf16[512,256]{1,0:T(8,128)(2,1)} %bitcast.17, f32[512,256]{1,0:T(8,128)} %get-tuple-element.40.ghc_ref, ...), custom_call_target="tpu_custom_call" | custom-call | tf_op jit(solution)/shard_map/pallas_call | solution.py:65
  69.2 5.5 %all-to-all-start.1 = ((bf16[16,32,256]{2,1,0:T(8,128)(2,1)}), bf16[16,32,256]{2,1,0:T(8,128)(2,1)S(1)}, u32[]{:S(2)}, u32[]{:S(2)}) async-start(bf16[16,32,256]{2,1,0:T(8,128)(2,1)} %bitcast.19), calls=%async_computation.1 | async-start | bytes 524288 | tf_op jit(solution)/shard_map/all_to_all | solution.py:309
  74.8 3.8 %shard_map.161 = (bf16[1024,256]{1,0:T(8,128)(2,1)}, f32[8,256]{1,0:T(8,128)}, f32[512,256]{1,0:T(8,128)}) custom-call(bf16[512,256]{1,0:T(8,128)(2,1)} %get-tuple-element.37.pooled_ref, bf16[512,256]{1,0:T(8,128)(2,1)} %bitcast.18, f32[512,256]{1,0:T(8,128)} %get-tuple-element.40.ghc_ref, bf16[4,256,256]{2,1,0:T(8,128)(2,1)} %wc_ref.1, s32[16,128]{1,0:T(8,128)} %bitcast.34, ...), custom_call_target="tpu_custom_call" | custom-call | flops 4000000000 | bytes 10000000 | tf_op jit(solution)/shard_map/pallas_call | solution.py:65
  78.6 4.2 %all-to-all-done.1 = bf16[16,32,256]{2,1,0:T(8,128)(2,1)S(1)} async-done(((bf16[16,32,256]{2,1,0:T(8,128)(2,1)}), bf16[16,32,256]{2,1,0:T(8,128)(2,1)S(1)}, u32[]{:S(2)}, u32[]{:S(2)}) %all-to-all-start.1) | async-done | bytes 262176 | tf_op jit(solution)/shard_map/all_to_all | solution.py:309
  82.8 0.7 copy-done
  83.5 5.8 %shard_map.162 = (f32[2048,256]{1,0:T(8,128)}, bf16[2048,256]{1,0:T(8,128)(2,1)}, bf16[2048,256]{1,0:T(8,128)(2,1)}) custom-call(bf16[512,256]{1,0:T(8,128)(2,1)} %get-tuple-element.42.own_ref, bf16[512,256]{1,0:T(8,128)(2,1)} %bitcast.14, s32[4,128]{1,0:T(4,128)} %reshape.65.send_ref, f32[512,256]{1,0:T(8,128)} %get-tuple-element.47.part_ref, ...), custom_call_target="tpu_custom_call" | custom-call | tf_op jit(solution)/shard_map/pallas_call | solution.py:65
  89.3 23.6 %shard_map.163 = (bf16[2048,256]{1,0:T(8,128)(2,1)}, bf16[256,256]{1,0:T(8,128)(2,1)}, bf16[256,256]{1,0:T(8,128)(2,1)}, bf16[2048,256]{1,0:T(8,128)(2,1)}, bf16[256,256]{1,0:T(8,128)(2,1)}, /*index=5*/f32[8,256]{1,0:T(8,128)}) custom-call(bf16[8192,256]{1,0:T(8,128)(2,1)} %get-tuple-element.36.d_ref, bf16[2048,256]{1,0:T(8,128)(2,1)} %get-tuple-element.50.dagg_ref, ...), custom_call_target="tpu_custom_call" | custom-call | tf_op jit(solution)/shard_map/pallas_call | solution.py:65
  113.0 5.9 %shard_map.164 = (bf16[768,256]{1,0:T(8,128)(2,1)}, f32[2048,256]{1,0:T(8,128)}) custom-call(bf16[2048,256]{1,0:T(8,128)(2,1)} %h_ref.9, bf16[2048,256]{1,0:T(8,128)(2,1)} %get-tuple-element.54.dq_ref, bf16[2048,256]{1,0:T(8,128)(2,1)} %get-tuple-element.55.du_ref, bf16[2048,256]{1,0:T(8,128)(2,1)} %get-tuple-element.56.agg_ref, ...), custom_call_target="tpu_custom_call" | custom-call | tf_op jit(solution)/shard_map/pallas_call | solution.py:65
  118.8 2.0 %pad_maximum_fusion = bf16[2048,256]{1,0:T(8,128)(2,1)} fusion(bf16[768,256]{1,0:T(8,128)(2,1)} %get-tuple-element.61, bf16[256,256]{1,0:T(8,128)(2,1)S(1)} %copy-done.6, bf16[1024,256]{1,0:T(8,128)(2,1)S(1)} %copy-done.4), kind=kLoop, calls=%fused_computation.1 | loop fusion | flops 3145728 | bytes 2097152 | tf_op jit(solution)/shard_map/concatenate | solution.py:433
  120.9 5.7 %all-to-all-start.2 = ((bf16[16,128,256]{2,1,0:T(8,128)(2,1)}), bf16[16,128,256]{2,1,0:T(8,128)(2,1)S(1)}, u32[]{:S(2)}, u32[]{:S(2)}) async-start(bf16[16,128,256]{2,1,0:T(8,128)(2,1)} %bitcast.11), calls=%async_computation.2 | async-start | bytes 2097152 | tf_op jit(solution)/shard_map/all_to_all | solution.py:309
  126.6 0.7 slice.25
  127.3 0.7 slice.24
  128.0 23.5 %all-to-all-done.2 = bf16[16,128,256]{2,1,0:T(8,128)(2,1)S(1)} async-done(((bf16[16,128,256]{2,1,0:T(8,128)(2,1)}), bf16[16,128,256]{2,1,0:T(8,128)(2,1)S(1)}, u32[]{:S(2)}, u32[]{:S(2)}) %all-to-all-start.2) | async-done | bytes 1048608 | tf_op jit(solution)/shard_map/all_to_all | solution.py:309
  152.1 4.9 %all-to-all-start.4 = ((f32[16,2,256]{2,1,0:T(2,128)}), f32[16,2,256]{2,1,0:T(2,128)S(1)}, u32[]{:S(2)}, u32[]{:S(2)}) async-start(f32[16,2,256]{2,1,0:T(2,128)} %broadcast_in_dim.5), calls=%async_computation.4 | async-start | bytes 65536 | tf_op jit(solution)/shard_map/all_to_all | solution.py:437
  157.2 4.0 %all-to-all-done.4 = f32[16,2,256]{2,1,0:T(2,128)S(1)} async-done(((f32[16,2,256]{2,1,0:T(2,128)}), f32[16,2,256]{2,1,0:T(2,128)S(1)}, u32[]{:S(2)}, u32[]{:S(2)}) %all-to-all-start.4) | async-done | bytes 32800 | tf_op jit(solution)/shard_map/all_to_all | solution.py:437
  161.2 1.1 broadcast_in_dim.4
  162.2 6.0 %all-to-all-start.3 = ((bf16[16,128,256]{2,1,0:T(8,128)(2,1)}), bf16[16,128,256]{2,1,0:T(8,128)(2,1)S(1)}, u32[]{:S(2)}, u32[]{:S(2)}) async-start(bf16[16,128,256]{2,1,0:T(8,128)(2,1)} %broadcast_in_dim.4), calls=%async_computation.3 | async-start | bytes 2097152 | tf_op jit(solution)/shard_map/all_to_all | solution.py:319
  168.3 2.3 %collective-permute-start.2 = (bf16[256,256]{1,0:T(8,128)(2,1)S(1)}, bf16[256,256]{1,0:T(8,128)(2,1)S(1)}, u32[]{:S(2)}, u32[]{:S(2)}) collective-permute-start(bf16[256,256]{1,0:T(8,128)(2,1)S(1)} %copy-done.10), channel_id=1, source_target_pairs={{1,0},{2,1},{3,2},{4,3},{5,4},{6,5},{7,6},{8,7},{9,8},{10,9},{11,1... | collective-permute-start | bytes 393224 | tf_op jit(solution)/shard_map/ppermute | solution.py:304
  170.6 4.2 %collective-permute-start.3 = (bf16[256,256]{1,0:T(8,128)(2,1)S(1)}, bf16[256,256]{1,0:T(8,128)(2,1)S(1)}, u32[]{:S(2)}, u32[]{:S(2)}) collective-permute-start(bf16[256,256]{1,0:T(8,128)(2,1)S(1)} %copy-done.9), channel_id=1, source_target_pairs={{0,1},{1,2},{2,3},{3,4},{4,5},{5,6},{6,7},{7,8},{8,9},{9,10},{10,1... | collective-permute-start | bytes 393224 | tf_op jit(solution)/shard_map/ppermute | solution.py:304
  175.4 19.2 %collective-permute-done.2.from_right_ref = bf16[256,256]{1,0:T(8,128)(2,1)S(1)} collective-permute-done((bf16[256,256]{1,0:T(8,128)(2,1)S(1)}, bf16[256,256]{1,0:T(8,128)(2,1)S(1)}, u32[]{:S(2)}, u32[]{:S(2)}) %collective-permute-start.2) | collective-permute-done | bytes 131104 | tf_op jit(solution)/shard_map/ppermute | solution.py:304
  195.3 4.5 %shard_map.165 = f32[2048,256]{1,0:T(8,128)} custom-call(bf16[2048,256]{1,0:T(8,128)(2,1)} %get-tuple-element.51.own_ref, bf16[256,256]{1,0:T(8,128)(2,1)} %copy-done.5, bf16[256,256]{1,0:T(8,128)(2,1)} %copy-done.7, s32[2,128]{1,0:T(2,128)} %bitcast.36, s32[2,128]{1,0:T(2,128)} %bitcast.38, f32[2048,256]{1,0:T(8,128)} %get-tuple-element.58.part_ref, ...), custom_call_target="tpu_custom_call" | custom-call | tf_op jit(solution)/shard_map/pallas_call | solution.py:65
  200.0 1.5 fusion
  (30 shorter events, 3.0 us)
Async XLA Ops:
  3.3 22.7 %collective-permute-start = (bf16[256,256]{1,0:T(8,128)(2,1)}, bf16[256,256]{1,0:T(8,128)(2,1)S(1)}, u32[]{:S(2)}, u32[]{:S(2)}) collective-permute-start(bf16[256,256]{1,0:T(8,128)(2,1)} %get-tuple-element.34), channel_id=1, source_target_pairs={{0,1},{1,2},{2,3},{3,4},{4,5},{5,6},{6,7},{7,8},{8,9},{9,10},{10,1... | collective-permute-start | bytes 393224 | tf_op jit(solution)/shard_map/ppermute | solution.py:304
  7.0 19.0 %collective-permute-start.1 = (bf16[256,256]{1,0:T(8,128)(2,1)}, bf16[256,256]{1,0:T(8,128)(2,1)S(1)}, u32[]{:S(2)}, u32[]{:S(2)}) collective-permute-start(bf16[256,256]{1,0:T(8,128)(2,1)} %get-tuple-element.35), channel_id=1, source_target_pairs={{1,0},{2,1},{3,2},{4,3},{5,4},{6,5},{7,6},{8,7},{9,8},{10,9},{11,1... | collective-permute-start | bytes 393224 | tf_op jit(solution)/shard_map/ppermute | solution.py:304
  9.0 16.4 %copy-start.8 = (s32[16,32]{1,0:T(8,128)S(1)}, s32[16,32]{1,0:T(8,128)}, u32[]{:S(2)}) copy-start(s32[16,32]{1,0:T(8,128)} %param.25) | copy-start | bytes 6148
  26.0 0.7 copy-start.2
  26.0 0.7 copy-start.3
  46.0 14.6 %all-to-all-start = ((bf16[16,32,256]{2,1,0:T(8,128)(2,1)}), bf16[16,32,256]{2,1,0:T(8,128)(2,1)S(1)}, u32[]{:S(2)}, u32[]{:S(2)}) async-start(bf16[16,32,256]{2,1,0:T(8,128)(2,1)} %bitcast.20), calls=%async_computation | async-start | bytes 524288 | tf_op jit(solution)/shard_map/all_to_all | solution.py:309
  60.6 0.7 copy-start.1
  69.2 13.5 %all-to-all-start.1 = ((bf16[16,32,256]{2,1,0:T(8,128)(2,1)}), bf16[16,32,256]{2,1,0:T(8,128)(2,1)S(1)}, u32[]{:S(2)}, u32[]{:S(2)}) async-start(bf16[16,32,256]{2,1,0:T(8,128)(2,1)} %bitcast.19), calls=%async_computation.1 | async-start | bytes 524288 | tf_op jit(solution)/shard_map/all_to_all | solution.py:309
  82.8 0.7 copy-start
  113.0 5.9 %copy-start.4 = (bf16[1024,256]{1,0:T(8,128)(2,1)S(1)}, bf16[1024,256]{1,0:T(8,128)(2,1)}, u32[]{:S(2)}) copy-start(bf16[1024,256]{1,0:T(8,128)(2,1)} %get-tuple-element.59) | copy-start | bytes 1572868
  113.0 5.9 %copy-start.6 = (bf16[256,256]{1,0:T(8,128)(2,1)S(1)}, bf16[256,256]{1,0:T(8,128)(2,1)}, u32[]{:S(2)}) copy-start(bf16[256,256]{1,0:T(8,128)(2,1)} %get-tuple-element.60) | copy-start | bytes 393220
  120.9 30.6 %all-to-all-start.2 = ((bf16[16,128,256]{2,1,0:T(8,128)(2,1)}), bf16[16,128,256]{2,1,0:T(8,128)(2,1)S(1)}, u32[]{:S(2)}, u32[]{:S(2)}) async-start(bf16[16,128,256]{2,1,0:T(8,128)(2,1)} %bitcast.11), calls=%async_computation.2 | async-start | bytes 2097152 | tf_op jit(solution)/shard_map/all_to_all | solution.py:309
  152.1 9.1 %all-to-all-start.4 = ((f32[16,2,256]{2,1,0:T(2,128)}), f32[16,2,256]{2,1,0:T(2,128)S(1)}, u32[]{:S(2)}, u32[]{:S(2)}) async-start(f32[16,2,256]{2,1,0:T(2,128)} %broadcast_in_dim.5), calls=%async_computation.4 | async-start | bytes 65536 | tf_op jit(solution)/shard_map/all_to_all | solution.py:437
  157.0 11.3 %copy-start.10 = (bf16[256,256]{1,0:T(8,128)(2,1)S(1)}, bf16[256,256]{1,0:T(8,128)(2,1)}, u32[]{:S(2)}) copy-start(bf16[256,256]{1,0:T(8,128)(2,1)} %get-tuple-element.52) | copy-start | bytes 393220
  157.0 13.6 %copy-start.9 = (bf16[256,256]{1,0:T(8,128)(2,1)S(1)}, bf16[256,256]{1,0:T(8,128)(2,1)}, u32[]{:S(2)}) copy-start(bf16[256,256]{1,0:T(8,128)(2,1)} %get-tuple-element.53) | copy-start | bytes 393220
  162.2 37.6 %all-to-all-start.3 = ((bf16[16,128,256]{2,1,0:T(8,128)(2,1)}), bf16[16,128,256]{2,1,0:T(8,128)(2,1)S(1)}, u32[]{:S(2)}, u32[]{:S(2)}) async-start(bf16[16,128,256]{2,1,0:T(8,128)(2,1)} %broadcast_in_dim.4), calls=%async_computation.3 | async-start | bytes 2097152 | tf_op jit(solution)/shard_map/all_to_all | solution.py:319
  168.3 26.3 %collective-permute-start.2 = (bf16[256,256]{1,0:T(8,128)(2,1)S(1)}, bf16[256,256]{1,0:T(8,128)(2,1)S(1)}, u32[]{:S(2)}, u32[]{:S(2)}) collective-permute-start(bf16[256,256]{1,0:T(8,128)(2,1)S(1)} %copy-done.10), channel_id=1, source_target_pairs={{1,0},{2,1},{3,2},{4,3},{5,4},{6,5},{7,6},{8,7},{9,8},{10,9},{11,1... | collective-permute-start | bytes 393224 | tf_op jit(solution)/shard_map/ppermute | solution.py:304
  170.6 24.0 %collective-permute-start.3 = (bf16[256,256]{1,0:T(8,128)(2,1)S(1)}, bf16[256,256]{1,0:T(8,128)(2,1)S(1)}, u32[]{:S(2)}, u32[]{:S(2)}) collective-permute-start(bf16[256,256]{1,0:T(8,128)(2,1)S(1)} %copy-done.9), channel_id=1, source_target_pairs={{0,1},{1,2},{2,3},{3,4},{4,5},{5,6},{6,7},{7,8},{8,9},{9,10},{10,1... | collective-permute-start | bytes 393224 | tf_op jit(solution)/shard_map/ppermute | solution.py:304
  194.6 0.6 copy-start.5
  194.6 0.7 copy-start.7

commit v2 on v1

--- a/solution.py
+++ b/solution.py
@@ -48,8 +48,23 @@
 
 
 def silu_parts(v):
-    sig = jax.nn.sigmoid(v)
-    return v * sig, sig * (1.0 + v * (1.0 - sig))
+    sig = 0.5 * jnp.tanh(0.5 * v) + 0.5
+    silu = v * sig
+    return silu, sig + silu * (1.0 - sig)
+
+
+def to_pairs(ref, first, rows):
+    n = rows.shape[0]
+    for j in range(2):
+        ref[pl.ds(2 * first + j, n, stride=2), :] = rows[:, j * LANES : (j + 1) * LANES]
+
+
+def from_pairs(ref, first, n):
+    return jnp.concatenate([ref[pl.ds(2 * first + j, n, stride=2), :] for j in range(2)], axis=1)
+
+
+def pair(index):
+    return pl.ds(pl.multiple_of(index * 2, 2), 2)
 
 
 def call(kernel, outs, args, grid=(), specs=None, out_specs=None, scratch=(), cost=(0, 0)):
@@ -87,45 +102,35 @@
     to_left_ref[...] = mm_tn(hot_rows(row_form(left_ref, 0, n), h.shape[0]), h).astype(bf)
 
 
-def own_kernel(per, h_ref, w_ref, b_ref, src_ref, dst_ref, z_ref, p_ref, q_ref):
-    t = pl.program_id(0)
-
-    @pl.when(t == 0)
-    def _():
-        h = h_ref[...]
-        p_ref[...] = mm(h, w_ref[0]).astype(bf)
-        q_ref[...] = mm(h, w_ref[1]).astype(bf)
-
-    src = row_form(src_ref, t * per, per)
-    dst = row_form(dst_ref, t * per, per)
-    qt = q_ref[pl.ds(pl.multiple_of(t * TILE, TILE), TILE), :]
-    z_ref[...] = (
-        mm_tn(hot_rows(src, p_ref.shape[0]), p_ref[...])
-        + mm_tn(hot_rows(dst, TILE), qt)
-        + b_ref[0:1, :]
-    )
+def project_kernel(h_ref, w_ref, p_ref, q_ref):
+    h = h_ref[...]
+    p_ref[...] = mm(h, w_ref[0]).astype(bf)
+    q_ref[...] = mm(h, w_ref[1]).astype(bf)
 
 
 def fine_kernel(
-    per, tiles, z_ref, left_ref, right_ref, h_ref, w_ref, src_ref, dst_ref, pool_ref, send_ref,
-    d_ref, agg_ref, dsu_ref, pooled_ref, out_ref, count_ref, halo_p,
+    per, tiles, src_ref, p_ref, q_ref, left_ref, right_ref, h_ref, w_ref, b_ref, dst_ref, pool_ref,
+    send_ref, d_ref, agg_ref, dsu_ref, pooled_ref, out_ref, count_ref, table, taken,
 ):
     t = pl.program_id(0)
     nodes = h_ref.shape[0]
     halo = left_ref.shape[0]
+    edges = per * LANES
 
     @pl.when(t == 0)
     def _():
-        halo_p[0:halo, :] = mm(left_ref[...], w_ref[0]).astype(bf)
-        halo_p[halo : 2 * halo, :] = mm(right_ref[...], w_ref[0]).astype(bf)
-
-    src = row_form(src_ref, t * per, per) - nodes
-    dst = row_form(dst_ref, t * per, per)
-    z = z_ref[...] + mm_tn(hot_rows(src, 2 * halo), halo_p[...])
+        to_pairs(table, 0, p_ref[...].astype(f32))
+        to_pairs(table, nodes, as_bf(mm(left_ref[...], w_ref[0])).astype(f32))
+        to_pairs(table, nodes + halo, as_bf(mm(right_ref[...], w_ref[0])).astype(f32))
+
+    for e in range(edges):
+        taken[2 * e : 2 * e + 2, :] = table[pair(src_ref[t * edges + e]), :]
+    rows = pl.ds(pl.multiple_of(t * TILE, TILE), TILE)
+    hot = hot_rows(row_form(dst_ref, t * per, per), TILE)
+    z = from_pairs(taken, 0, edges) + mm_tn(hot, q_ref[rows, :]) + b_ref[0:1, :]
     m, d = silu_parts(z)
     d_ref[...] = d.astype(bf)
-    rows = pl.ds(pl.multiple_of(t * TILE, TILE), TILE)
-    agg_ref[rows, :] = mm(hot_rows(dst, TILE), m.astype(bf)).astype(bf)
+    agg_ref[rows, :] = mm(hot, m.astype(bf)).astype(bf)
 
     @pl.when(t == tiles - 1)
     def _():
@@ -224,9 +229,10 @@
 
 def node_back_kernel(
     own_ref, ret_ref, send_ref, part_ref, wc_ref, count_ref, pool_ref, cot_ref, dsu_ref, w_ref,
-    g_ref, du_ref, dagg_ref,
+    h_ref, agg_ref, g_ref, du_ref, dagg_ref, gw_ref,
 ):
     coarse = own_ref.shape[0]
+    width = h_ref.shape[1]
     sends = hot_rows(row_form(send_ref, 0, send_ref.shape[0]), coarse)
     dp = (own_ref[...].astype(f32) + mm(sends, ret_ref[...])).astype(bf)
     dc = part_ref[...] + mm_nt(dp, wc_ref[0])
@@ -238,54 +244,64 @@
     du = (g * dsu_ref[...].astype(f32)).astype(bf)
     du_ref[...] = du
     dagg_ref[...] = mm_nt(du, w_ref[2]).astype(bf)
+    gw_ref[0:width, :] = mm_tn(agg_ref[...], du).astype(bf)
+    gw_ref[width : 2 * width, :] = mm_tn(h_ref[...], du).astype(bf)
 
 
 def edge_back_kernel(
-    per, tiles, d_ref, dagg_ref, h_ref, left_ref, right_ref, src_ref, dst_ref,
-    own_ref, gl_ref, gr_ref, dq_ref, gw_ref, gb_ref, acc,
+    per, tiles, src_ref, d_ref, dagg_ref, h_ref, left_ref, right_ref, dst_ref, gbc_ref,
+    own_ref, gl_ref, gr_ref, dq_ref, gw_ref, gb, dzs, *accs,
 ):
     t = pl.program_id(0)
-    nodes = h_ref.shape[0]
+    nodes, width = h_ref.shape
     halo = left_ref.shape[0]
+    edges = per * LANES
 
     @pl.when(t == 0)
     def _():
-        acc[...] = jnp.zeros_like(acc)
-        gb_ref[...] = jnp.zeros_like(gb_ref)
-
-    src = row_form(src_ref, t * per, per)
-    dst = row_form(dst_ref, t * per, per)
-    hot = hot_rows(dst, TILE)
+        gb[...] = jnp.zeros_like(gb)
+        for acc in accs:
+            acc[...] = jnp.zeros_like(acc)
+
+    hot = hot_rows(row_form(dst_ref, t * per, per), TILE)
     rows = pl.ds(pl.multiple_of(t * TILE, TILE), TILE)
     gm = mm_tn(hot, dagg_ref[rows, :])
     dz = (gm * d_ref[...].astype(f32)).astype(bf)
     dq = mm(hot, dz)
-    gb_ref[...] += jnp.sum(dq, axis=0, keepdims=True)
+    gb[...] += jnp.sum(dq, axis=0, keepdims=True)
     dq_ref[rows, :] = dq.astype(bf)
-    acc[...] += mm(hot_rows(src, acc.shape[0]), dz)
+    to_pairs(dzs, 0, dz.astype(f32))
+    for e in range(edges):
+        acc = accs[e % len(accs)]
+        at = pair(src_ref[t * edges + e])
+        acc[at, :] = acc[at, :] + dzs[2 * e : 2 * e + 2, :]
 
     @pl.when(t == tiles - 1)
     def _():
-        own = acc[0:nodes, :].astype(bf)
-        gl = acc[nodes : nodes + halo, :].astype(bf)
-        gr = acc[nodes + halo : nodes + 2 * halo, :].astype(bf)
+        def summed(first, n):
+            total = from_pairs(accs[0], first, n)
+            for acc in accs[1:]:
+                total = total + from_pairs(acc, first, n)
+            return total.astype(bf)
+
+        own = summed(0, nodes)
+        gl = summed(nodes, halo)
+        gr = summed(nodes + halo, halo)
         own_ref[...] = own
         gl_ref[...] = gl
         gr_ref[...] = gr
-        gw_ref[...] = (
+        gw_ref[0:width, :] = (
             mm_tn(h_ref[...], own) + mm_tn(left_ref[...], gl) + mm_tn(right_ref[...], gr)
         ).astype(bf)
-
-
-def fine_grad_kernel(h_ref, dq_ref, du_ref, agg_ref, g_ref, w_ref, gw_ref, part_ref):
-    h = h_ref[...]
-    width = h.shape[1]
-    dq = dq_ref[...]
-    du = du_ref[...]
-    gw_ref[0:width, :] = mm_tn(h, dq).astype(bf)
-    gw_ref[width : 2 * width, :] = mm_tn(agg_ref[...], du).astype(bf)
-    gw_ref[2 * width : 3 * width, :] = mm_tn(h, du).astype(bf)
-    part_ref[...] = g_ref[...] + mm_nt(du, w_ref[3]) + mm_nt(dq, w_ref[1])
+        gw_ref[width : width + 16, :] = jnp.broadcast_to(gb[0:1, :], (16, width)).astype(bf)
+        gw_ref[width + 16 : 2 * width + 16, :] = mm_tn(h_ref[...], dq_ref[...]).astype(bf)
+        gw_ref[2 * width + 16 :, :] = jnp.broadcast_to(gbc_ref[0:1, :], (16, width)).astype(bf)
+
+
+def part_kernel(dq_ref, du_ref, g_ref, w_ref, part_ref):
+    part_ref[...] = (
+        g_ref[...] + mm_nt(du_ref[...], w_ref[3]) + mm_nt(dq_ref[...], w_ref[1])
+    )
 
 
 def input_kernel(own_ref, from_right_ref, from_left_ref, right_ref, left_ref, part_ref, w_ref, o_ref):
@@ -298,12 +314,46 @@
     o_ref[...] = part_ref[...] + mm_nt(dp, w_ref[0])
 
 
+def finish_kernel(scale, core_ref, a_ref, ax_ref, b_ref, bx_ref, gf_ref, gc_ref, gb_ref):
+    width = a_ref.shape[1]
+
+    def write(a0, a1, b0, b1):
+        def put(ref, k, src, at):
+            ref[k * width : (k + 1) * width, :] = (
+                src[at * width : (at + 1) * width, :].astype(f32) * scale
+            )
+
+        for k in range(3):
+            put(gc_ref, k, a0, k)
+        put(gc_ref, 3, a1, 0)
+        put(gf_ref, 2, a1, 1)
+        put(gf_ref, 3, a1, 2)
+        put(gf_ref, 0, b0, 0)
+        put(gf_ref, 1, b1, 0)
+        gb_ref[0:1, :] = b0[width : width + 1, :].astype(f32) * scale
+        gb_ref[1:2, :] = b1[width : width + 1, :].astype(f32) * scale
+
+    core = core_ref[0]
+
+    @pl.when(core == 0)
+    def _():
+        write(a_ref, ax_ref, b_ref, bx_ref)
+
+    @pl.when(core != 0)
+    def _():
+        write(ax_ref, a_ref, bx_ref, b_ref)
+
+
 def shifted(block, axis, distance):
     devices = range(lax.axis_size(axis))
     route = [(i - distance, i) for i in devices if i - distance in devices]
     return lax.ppermute(block, axis, route)
 
 
+def swapped(block, parts, bit):
+    return lax.ppermute(block, "dom", [(i, i ^ bit) for i in range(parts)])
+
+
 def exchange(block, parts):
     rows, width = block.shape
     got = lax.all_to_all(
@@ -312,12 +362,15 @@
     return got
 
 
-def reduced(block, parts):
-    rows, width = block.shape
-    mine = jnp.sum(exchange(block, parts).astype(f32), axis=0).astype(bf)
-    spread = jnp.broadcast_to(mine[None], (parts,) + mine.shape)
-    full = lax.all_to_all(spread, "dom", split_axis=0, concat_axis=0, tiled=True)
-    return full.reshape(rows, width)
+def halves(block, core):
+    two = block.reshape((2, block.shape[0] // 2) + block.shape[1:])
+    mine = lax.dynamic_index_in_dim(two, core, 0, keepdims=False)
+    other = lax.dynamic_index_in_dim(two, 1 - core, 0, keepdims=False)
+    return mine, other
+
+
+def add(a, b):
+    return (a.astype(f32) + b.astype(f32)).astype(bf)
 
 
 def shards(
@@ -345,15 +398,14 @@
     h_left = shifted(to_right, "dom", 1)
     h_right = shifted(to_left, "dom", -1)
     edge_tile = pl.BlockSpec((edges, width), lambda t: (t, 0))
-    (z_own,) = call(
-        part(own_kernel, per),
-        [sds((tiles * edges, width), f32)],
-        [features, w_fine, bias, fsrc, fdst],
-        grid=(tiles,),
-        out_specs={0: edge_tile},
-        scratch=[pltpu.VMEM((nodes, width), bf)] * 2,
-        cost=(9e9, 10e6),
-    )
+    proj, recv = call(
+        project_kernel,
+        [sds((nodes, width), bf)] * 2,
+        [features, w_fine],
+        cost=(3e9, 10e6),
+    )
+    smem = pl.BlockSpec(memory_space=pltpu.SMEM)
+    ext_pairs = 2 * (nodes + 2 * halo)
     d_edge, agg, dsu, pooled, outgoing, count = call(
         part(fine_kernel, per, tiles),
         [
@@ -364,11 +416,11 @@
             sds((crows, width), bf),
             sds((coarse, LANES), f32),
         ],
-        [z_own, h_left, h_right, features, w_fine, fsrc, fdst, pool, csend],
+        [fine_src, proj, recv, h_left, h_right, features, w_fine, bias, fdst, pool, csend],
         grid=(tiles,),
-        specs={0: edge_tile},
+        specs={0: smem},
         out_specs={0: edge_tile},
-        scratch=[pltpu.VMEM((2 * halo, width), bf)],
+        scratch=[pltpu.VMEM((ext_pairs, LANES), f32), pltpu.VMEM((2 * edges, LANES), f32)],
     )
     incoming = exchange(outgoing, parts).reshape(crows, width)
     cedges = coarse_src.shape[0]
@@ -397,46 +449,78 @@
         [pooled, incoming, ghc, w_coarse, cdst, own_c, back_c, dz_c, du_c, agg_c],
         cost=(4e9, 10e6),
     )
-    g, du, dagg = call(
+    g, du, dagg, gw_n = call(
         node_back_kernel,
-        [sds((nodes, width), f32), sds((nodes, width), bf), sds((nodes, width), bf)],
-        [own_c, returned, csend, part_c, w_coarse, count, pool, cotangent, dsu, w_fine],
-    )
-    own_f, gl, gr, dq, gw0, gb_f = call(
+        [
+            sds((nodes, width), f32),
+            sds((nodes, width), bf),
+            sds((nodes, width), bf),
+            sds((2 * width, width), bf),
+        ],
+        [
+            own_c, returned, csend, part_c, w_coarse, count, pool, cotangent, dsu, w_fine,
+            features, agg,
+        ],
+    )
+    core = lax.axis_index("dom") % 2
+    same_core = [list(range(c, parts, 2)) for c in range(2)]
+    chips = parts // 2
+    mine, other = halves(jnp.concatenate([gw_c, gw_n], axis=0), core)
+    early = add(mine, swapped(other, parts, 1))
+    early, dagg = lax.optimization_barrier((early, dagg))
+    early = lax.all_to_all(
+        early.reshape(chips, -1, width), "dom", 0, 0, axis_index_groups=same_core, tiled=True
+    )
+    own_f, gl, gr, dq, gw_e = call(
         part(edge_back_kernel, per, tiles),
         [
             sds((nodes, width), bf),
             sds((halo, width), bf),
             sds((halo, width), bf),
             sds((nodes, width), bf),
-            sds((width, width), bf),
-            sds((8, width), f32),
+            sds((2 * (width + 16), width), bf),
         ],
-        [d_edge, dagg, features, h_left, h_right, fsrc, fdst],
+        [fine_src, d_edge, dagg, features, h_left, h_right, fdst, gb_c],
         grid=(tiles,),
-        specs={0: edge_tile},
-        scratch=[pltpu.VMEM((nodes + 2 * halo, width), f32)],
-    )
+        specs={0: smem, 1: edge_tile},
+        scratch=[pltpu.VMEM((8, width), f32), pltpu.VMEM((2 * edges, LANES), f32)]
+        + [pltpu.VMEM((ext_pairs, LANES), f32)] * 8,
+        cost=(30e9, 10e6),
+    )
+    mine, other = halves(gw_e, core)
+    late = add(mine, swapped(other, parts, 1))
+    early = jnp.sum(early.astype(f32), axis=0).astype(bf)
+    early = lax.all_to_all(
+        jnp.broadcast_to(early[None], (chips,) + early.shape),
+        "dom", 0, 0, axis_index_groups=same_core, tiled=True,
+    ).reshape(-1, width)
+    bit = 2
+    while bit < parts:
+        late = add(late, swapped(late, parts, bit))
+        bit *= 2
     from_right = shifted(gl, "dom", -1)
     from_left = shifted(gr, "dom", 1)
-    gw_rest, part_f = call(
-        fine_grad_kernel,
-        [sds((3 * width, width), bf), sds((nodes, width), f32)],
-        [features, dq, du, agg, g, w_fine],
+    (part_f,) = call(
+        part_kernel, [sds((nodes, width), f32)], [dq, du, g, w_fine], cost=(4e9, 10e6)
     )
     (grad_input,) = call(
         input_kernel,
         [sds((nodes, width), f32)],
         [own_f, from_right, from_left, right, left, part_f, w_fine],
+        cost=(4e9, 10e6),
     )
     scale = 1.0 / float(nodes * parts // 256)
-    total = reduced(jnp.concatenate([gw_c, gw0, gw_rest], axis=0), parts).astype(f32) * scale
-    total = total.reshape(8, width, width)
-    gb = jnp.stack([gb_f[0], gb_c[0]])
-    spread = jnp.broadcast_to(gb[None], (parts,) + gb.shape)
-    gbs = lax.all_to_all(spread, "dom", split_axis=0, concat_axis=0, tiled=True)
-    grad_bias = jnp.sum(gbs, axis=0) * scale
-    return (grad_input, total[4:], total[:4], grad_bias)
+    grad_fine, grad_coarse, grad_bias = call(
+        part(finish_kernel, scale),
+        [sds((4 * width, width), f32), sds((4 * width, width), f32), sds((2, width), f32)],
+        [
+            core.astype(jnp.int32).reshape(1), early, swapped(early, parts, 1),
+            late, swapped(late, parts, 1),
+        ],
+        specs={0: smem},
+    )
+    shape = (4, width, width)
+    return (grad_input, grad_fine.reshape(shape), grad_coarse.reshape(shape), grad_bias)
 
 
 def solution(mesh):

time: 203 us -> 157 us (0.77)
  the two profiles are of different devices: /device:TPU:13 before, /device:TPU:1 now
where the time goes in v2:
time: 157 us; the launch traced here: 156 us
  Pallas kernels  83.3 us (53%)
  starting transfers between devices  43.3 us (28%)
  waiting for transfers between devices  20 us (13%)
  local copies, waits for them, and re-layouts  5.97 us (4%)
  other arithmetic  2.97 us (2%)
    pallas_call x11, Pallas kernels, call(): pl.pallas_call(kernel, grid=grid or (1,), in_specs=in_specs, out_specs=o_...  83.3 us
    ppermute x7, starting transfers between devices, swapped(): return lax.ppermute(block, 'dom', [(i, i ^ bit) for i in range(parts)])  13.2 us
    ppermute x4, starting transfers between devices, shifted(): return lax.ppermute(block, axis, route)  12.6 us
    all_to_all x2, waiting for transfers between devices, exchange(): lax.all_to_all(block.reshape(parts, rows // parts, width), 'dom', split_a...  10.4 us
    all_to_all x2, starting transfers between devices, exchange(): lax.all_to_all(block.reshape(parts, rows // parts, width), 'dom', split_a...  9.97 us
    ppermute x7, waiting for transfers between devices, swapped(): return lax.ppermute(block, 'dom', [(i, i ^ bit) for i in range(parts)])  7.88 us
    all_to_all x1, starting transfers between devices, shards(): lax.all_to_all(jnp.broadcast_to(early[None], (chips,) + early.shape), 'do...  4.09 us
    unnamed x28, local copies, waits for them, and re-layouts  3.55 us
  transfers between devices with their start and end apart: 15, of which 7 were waited for; matrix products, arithmetic and copies ran while one was open for 2% of the time, Pallas kernels for 13%

profile of v2, /device:TPU:1, one launch (start us, length us, event | category | flops | bytes accessed | tf_op | source)
XLA Modules:
  0.0 156.4 jit_solution(14208960633795423283)
XLA Ops:
  0.6 2.7 %shard_map.157 = (bf16[256,256]{1,0:T(8,128)(2,1)}, bf16[256,256]{1,0:T(8,128)(2,1)}) custom-call(bf16[2048,256]{1,0:T(8,128)(2,1)} %h_ref.9, s32[2,128]{1,0:T(2,128)} %bitcast.48, s32[2,128]{1,0:T(2,128)} %bitcast.50), custom_call_target="tpu_custom_call" | custom-call | tf_op jit(solution)/shard_map/pallas_call | solution.py:80
  3.3 4.5 %collective-permute-start = (bf16[256,256]{1,0:T(8,128)(2,1)}, bf16[256,256]{1,0:T(8,128)(2,1)S(1)}, u32[]{:S(2)}, u32[]{:S(2)}) collective-permute-start(bf16[256,256]{1,0:T(8,128)(2,1)} %get-tuple-element.41), channel_id=1, source_target_pairs={{0,1},{1,2},{2,3},{3,4},{4,5},{5,6},{6,7},{7,8},{8,9},{9,10},{10,1... | collective-permute-start | bytes 393224 | tf_op jit(solution)/shard_map/ppermute | solution.py:350
  7.9 1.9 %collective-permute-start.1 = (bf16[256,256]{1,0:T(8,128)(2,1)}, bf16[256,256]{1,0:T(8,128)(2,1)S(1)}, u32[]{:S(2)}, u32[]{:S(2)}) collective-permute-start(bf16[256,256]{1,0:T(8,128)(2,1)} %get-tuple-element.42), channel_id=1, source_target_pairs={{1,0},{2,1},{3,2},{4,3},{5,4},{6,5},{7,6},{8,7},{9,8},{10,9},{11,1... | collective-permute-start | bytes 393224 | tf_op jit(solution)/shard_map/ppermute | solution.py:350
  9.8 3.4 %shard_map.156 = (bf16[2048,256]{1,0:T(8,128)(2,1)}, bf16[2048,256]{1,0:T(8,128)(2,1)}) custom-call(bf16[2048,256]{1,0:T(8,128)(2,1)} %h_ref.9, bf16[4,256,256]{2,1,0:T(8,128)(2,1)} %w_ref.15), custom_call_target="tpu_custom_call" | custom-call | flops 3000000000 | bytes 10000000 | tf_op jit(solution)/shard_map/pallas_call | solution.py:80
  15.0 22.7 %shard_map.158 = (bf16[8192,256]{1,0:T(8,128)(2,1)}, bf16[2048,256]{1,0:T(8,128)(2,1)}, bf16[2048,256]{1,0:T(8,128)(2,1)}, bf16[512,256]{1,0:T(8,128)(2,1)}, bf1...) custom-call(s32[8192]{0:T(1024)} %src_ref.3, bf16[2048,256]{1,0:T(8,128)(2,1)} %get-tuple-element.39.p_ref, ...), custom_call_target="tpu_custom_call" | custom-call | tf_op jit(solution)/shard_map/pallas_call | solution.py:80
  37.7 6.0 %all-to-all-start = ((bf16[16,32,256]{2,1,0:T(8,128)(2,1)}), bf16[16,32,256]{2,1,0:T(8,128)(2,1)S(1)}, u32[]{:S(2)}, u32[]{:S(2)}) async-start(bf16[16,32,256]{2,1,0:T(8,128)(2,1)} %bitcast.37), calls=%async_computation | async-start | bytes 524288 | tf_op jit(solution)/shard_map/all_to_all | solution.py:359
  43.7 4.9 %shard_map.159 = (f32[2048,256]{1,0:T(8,128)}, f32[512,256]{1,0:T(8,128)}, f32[512,256]{1,0:T(8,128)}) custom-call(bf16[512,256]{1,0:T(8,128)(2,1)} %get-tuple-element.44.pooled_ref, bf16[4,256,256]{2,1,0:T(8,128)(2,1)} %wc_ref.1, f32[2,256]{1,0:T(2,128)} %b_ref.3, s32[16,128]{1,0:T(8,128)} %bitcast.43, s32[16,128]{1,0:T(8,128)} %bitcast.45, ...), custom_call_target="tpu_custom_call" | custom-call | flops 4000000000 | bytes 10000000 | tf_op jit(solution)/shard_map/pallas_call | solution.py:80
  48.6 4.6 %all-to-all-done = bf16[16,32,256]{2,1,0:T(8,128)(2,1)S(1)} async-done(((bf16[16,32,256]{2,1,0:T(8,128)(2,1)}), bf16[16,32,256]{2,1,0:T(8,128)(2,1)S(1)}, u32[]{:S(2)}, u32[]{:S(2)}) %all-to-all-start) | async-done | bytes 262176 | tf_op jit(solution)/shard_map/all_to_all | solution.py:359
  53.9 7.9 %shard_map.160 = (bf16[512,256]{1,0:T(8,128)(2,1)}, bf16[512,256]{1,0:T(8,128)(2,1)}, bf16[2048,256]{1,0:T(8,128)(2,1)}, bf16[512,256]{1,0:T(8,128)(2,1)}, bf16[512,256]{1,0:T(8,128)(2,1)}) custom-call(f32[2048,256]{1,0:T(8,128)} %get-tuple-element.47.z_ref, bf16[512,256]{1,0:T(8,128)(2,1)} %bitcast.32, f32[512,256]{1,0:T(8,128)} %get-tuple-element.46.ghc_ref, ...), custom_call_target="tpu_custom_call" | custom-call | tf_op jit(solution)/shard_map/pallas_call | solution.py:80
  61.8 4.0 %all-to-all-start.1 = ((bf16[16,32,256]{2,1,0:T(8,128)(2,1)}), bf16[16,32,256]{2,1,0:T(8,128)(2,1)S(1)}, u32[]{:S(2)}, u32[]{:S(2)}) async-start(bf16[16,32,256]{2,1,0:T(8,128)(2,1)} %bitcast.36), calls=%async_computation.1 | async-start | bytes 524288 | tf_op jit(solution)/shard_map/all_to_all | solution.py:359
  65.8 3.7 %shard_map.161 = (bf16[1024,256]{1,0:T(8,128)(2,1)}, f32[8,256]{1,0:T(8,128)}, f32[512,256]{1,0:T(8,128)}) custom-call(bf16[512,256]{1,0:T(8,128)(2,1)} %get-tuple-element.44.pooled_ref, bf16[512,256]{1,0:T(8,128)(2,1)} %bitcast.33, f32[512,256]{1,0:T(8,128)} %get-tuple-element.46.ghc_ref, bf16[4,256,256]{2,1,0:T(8,128)(2,1)} %wc_ref.1, s32[16,128]{1,0:T(8,128)} %bitcast.47, ...), custom_call_target="tpu_custom_call" | custom-call | flops 4000000000 | bytes 10000000 | tf_op jit(solution)/shard_map/pallas_call | solution.py:80
  69.5 5.8 %all-to-all-done.1 = bf16[16,32,256]{2,1,0:T(8,128)(2,1)S(1)} async-done(((bf16[16,32,256]{2,1,0:T(8,128)(2,1)}), bf16[16,32,256]{2,1,0:T(8,128)(2,1)S(1)}, u32[]{:S(2)}, u32[]{:S(2)}) %all-to-all-start.1) | async-done | bytes 262176 | tf_op jit(solution)/shard_map/all_to_all | solution.py:359
  76.0 6.6 %shard_map.162 = (f32[2048,256]{1,0:T(8,128)}, bf16[2048,256]{1,0:T(8,128)(2,1)}, bf16[2048,256]{1,0:T(8,128)(2,1)}, bf16[512,256]{1,0:T(8,128)(2,1)}) custom-call(bf16[512,256]{1,0:T(8,128)(2,1)} %get-tuple-element.49.own_ref, bf16[512,256]{1,0:T(8,128)(2,1)} %bitcast.31, s32[4,128]{1,0:T(4,128)} %reshape.71.send_ref, ...), custom_call_target="tpu_custom_call" | custom-call | tf_op jit(solution)/shard_map/pallas_call | solution.py:80
  82.6 1.0 pad_maximum_fusion
  84.4 1.3 collective-permute-done.2
  86.6 19.8 %shard_map.163 = (bf16[2048,256]{1,0:T(8,128)(2,1)}, bf16[256,256]{1,0:T(8,128)(2,1)}, bf16[256,256]{1,0:T(8,128)(2,1)}, bf16[2048,256]{1,0:T(8,128)(2,1)}, bf16[544,256]{1,0:T(8,128)(2,1)}) custom-call(s32[8192]{0:T(1024)} %src_ref.3, bf16[8192,256]{1,0:T(8,128)(2,1)} %get-tuple-element.43.d_ref, bf16[2048,256]{1,0:T(8,128)(2,1)} %get-tuple-element.61.dagg_ref, ...), custom_call_target="tpu_custom_call" | custom-call | flops 30000001024 | bytes 10000000 | tf_op jit(solution)/shard_map/pallas_call | solution.py:80
  106.4 1.0 dynamic-slice_bitcast_fusion.1
  107.8 3.5 %all-to-all-start.2 = ((bf16[8,96,256]{2,1,0:T(8,128)(2,1)}), bf16[8,96,256]{2,1,0:T(8,128)(2,1)S(1)}, u32[]{:S(2)}, u32[]{:S(2)}) async-start(bf16[8,96,256]{2,1,0:T(8,128)(2,1)} %bitcast.14), calls=%async_computation.2 | async-start | bytes 786432 | tf_op jit(solution)/shard_map/all_to_all | solution.py:471
  111.3 1.0 fusion.1
  112.3 1.4 collective-permute-start.7
  113.7 6.3 %collective-permute-done.7 = bf16[272,256]{1,0:T(8,128)(2,1)S(1)} collective-permute-done((bf16[272,256]{1,0:T(8,128)(2,1)S(1)}, bf16[272,256]{1,0:T(8,128)(2,1)S(1)}, u32[]{:S(2)}, u32[]{:S(2)}) %collective-permute-start.7) | collective-permute-done | bytes 139296 | tf_op jit(solution)/shard_map/ppermute | solution.py:354
  120.0 1.4 collective-permute-start.8
  121.4 1.2 all-to-all-done.2
  123.5 4.1 %all-to-all-start.3 = ((bf16[8,96,256]{2,1,0:T(8,128)(2,1)}), bf16[8,96,256]{2,1,0:T(8,128)(2,1)S(1)}, u32[]{:S(2)}, u32[]{:S(2)}) async-start(bf16[8,96,256]{2,1,0:T(8,128)(2,1)} %broadcast_in_dim.2), calls=%async_computation.3 | async-start | bytes 786432 | tf_op jit(solution)/shard_map/all_to_all | solution.py:493
  127.6 2.6 %collective-permute-start.3 = (bf16[256,256]{1,0:T(8,128)(2,1)S(1)}, bf16[256,256]{1,0:T(8,128)(2,1)S(1)}, u32[]{:S(2)}, u32[]{:S(2)}) collective-permute-start(bf16[256,256]{1,0:T(8,128)(2,1)S(1)} %copy-done.11), channel_id=1, source_target_pairs={{1,0},{2,1},{3,2},{4,3},{5,4},{6,5},{7,6},{8,7},{9,8},{10,9},{11,1... | collective-permute-start | bytes 393224 | tf_op jit(solution)/shard_map/ppermute | solution.py:350
  130.2 3.5 %collective-permute-start.4 = (bf16[256,256]{1,0:T(8,128)(2,1)S(1)}, bf16[256,256]{1,0:T(8,128)(2,1)S(1)}, u32[]{:S(2)}, u32[]{:S(2)}) collective-permute-start(bf16[256,256]{1,0:T(8,128)(2,1)S(1)} %copy-done.10), channel_id=1, source_target_pairs={{0,1},{1,2},{2,3},{3,4},{4,5},{5,6},{6,7},{7,8},{8,9},{9,10},{10,1... | collective-permute-start | bytes 393224 | tf_op jit(solution)/shard_map/ppermute | solution.py:350
  133.8 2.1 %collective-permute-start.9 = (bf16[272,256]{1,0:T(8,128)(2,1)S(1)}, bf16[272,256]{1,0:T(8,128)(2,1)S(1)}, u32[]{:S(2)}, u32[]{:S(2)}) collective-permute-start(bf16[272,256]{1,0:T(8,128)(2,1)S(1)} %add_convert_fusion.1), channel_id=1, source_target_pairs={{0,8},{1,9},{2,10},{3,11},{4,12},{5,13},{6,14},{7,15},{8,0},{9,1},... | collective-permute-start | bytes 417800 | tf_op jit(solution)/shard_map/ppermute | solution.py:354
  136.0 4.4 %shard_map.164.part_ref = f32[2048,256]{1,0:T(8,128)} custom-call(bf16[2048,256]{1,0:T(8,128)(2,1)} %get-tuple-element.66.dq_ref, bf16[2048,256]{1,0:T(8,128)(2,1)} %get-tuple-element.67.du_ref, f32[2048,256]{1,0:T(8,128)} %get-tuple-element.68.g_ref, bf16[4,256,256]{2,1,0:T(8,128)(2,1)} %w_ref.15), custom_call_target="tpu_custom_call" | custom-call | flops 4000000000 | bytes 10000000 | tf_op jit(solution)/shard_map/pallas_call | solution.py:80
  140.4 3.8 %collective-permute-start.5 = (bf16[768,256]{1,0:T(8,128)(2,1)S(1)}, bf16[768,256]{1,0:T(8,128)(2,1)S(1)}, u32[]{:S(2)}, u32[]{:S(2)}) collective-permute-start(bf16[768,256]{1,0:T(8,128)(2,1)S(1)} %bitcast.29), channel_id=1, source_target_pairs={{0,1},{1,0},{2,3},{3,2},{4,5},{5,4},{6,7},{7,6},{8,9},{9,8},{10,11... | collective-permute-start | bytes 1179656 | tf_op jit(solution)/shard_map/ppermute | solution.py:354
  144.5 3.2 %collective-permute-start.10 = (bf16[272,256]{1,0:T(8,128)(2,1)S(1)}, bf16[272,256]{1,0:T(8,128)(2,1)S(1)}, u32[]{:S(2)}, u32[]{:S(2)}) collective-permute-start(bf16[272,256]{1,0:T(8,128)(2,1)S(1)} %add_convert_fusion.b_ref), channel_id=1, source_target_pairs={{0,1},{1,0},{2,3},{3,2},{4,5},{5,4},{6,7},{7,6},{8,9},{9,8},{10,11... | collective-permute-start | bytes 417800 | tf_op jit(solution)/shard_map/ppermute | solution.py:354
  148.4 4.5 %shard_map.165 = f32[2048,256]{1,0:T(8,128)} custom-call(bf16[2048,256]{1,0:T(8,128)(2,1)} %get-tuple-element.63.own_ref, bf16[256,256]{1,0:T(8,128)(2,1)} %copy-done.12, bf16[256,256]{1,0:T(8,128)(2,1)} %copy-done.13, s32[2,128]{1,0:T(2,128)} %bitcast.49, s32[2,128]{1,0:T(2,128)} %bitcast.51, f32[2048,256]{1,0:T(8,128)} %shard_map.164.part_ref, ...), custom_call_target="tpu_custom_call" | custom-call | flops 4000000000 | bytes 10000000 | tf_op jit(solution)/shard_map/pallas_call | solution.py:80
  153.7 2.6 %shard_map.166 = (f32[1024,256]{1,0:T(8,128)}, f32[1024,256]{1,0:T(8,128)}, f32[2,256]{1,0:T(2,128)}) custom-call(s32[1]{0:T(128)} %bitcast.13.core_ref, bf16[768,256]{1,0:T(8,128)(2,1)} %bitcast.30, bf16[768,256]{1,0:T(8,128)(2,1)} %copy-done.5, bf16[272,256]{1,0:T(8,128)(2,1)} %copy-done.3, bf16[272,256]{1,0:T(8,128)(2,1)} %copy-done.6), custom_call_target="tpu_custom_call" | custom-call | tf_op jit(solution)/shard_map/pallas_call | solution.py:80
  (48 shorter events, 8.0 us)
Async XLA Ops:
  3.3 10.5 %collective-permute-start = (bf16[256,256]{1,0:T(8,128)(2,1)}, bf16[256,256]{1,0:T(8,128)(2,1)S(1)}, u32[]{:S(2)}, u32[]{:S(2)}) collective-permute-start(bf16[256,256]{1,0:T(8,128)(2,1)} %get-tuple-element.41), channel_id=1, source_target_pairs={{0,1},{1,2},{2,3},{3,4},{4,5},{5,6},{6,7},{7,8},{8,9},{9,10},{10,1... | collective-permute-start | bytes 393224 | tf_op jit(solution)/shard_map/ppermute | solution.py:350
  7.9 5.3 %copy-start.9 = (s32[16,32]{1,0:T(8,128)S(1)}, s32[16,32]{1,0:T(8,128)}, u32[]{:S(2)}) copy-start(s32[16,32]{1,0:T(8,128)} %param.25) | copy-start | bytes 6148
  7.9 6.5 %collective-permute-start.1 = (bf16[256,256]{1,0:T(8,128)(2,1)}, bf16[256,256]{1,0:T(8,128)(2,1)S(1)}, u32[]{:S(2)}, u32[]{:S(2)}) collective-permute-start(bf16[256,256]{1,0:T(8,128)(2,1)} %get-tuple-element.42), channel_id=1, source_target_pairs={{1,0},{2,1},{3,2},{4,3},{5,4},{6,5},{7,6},{8,7},{9,8},{10,9},{11,1... | collective-permute-start | bytes 393224 | tf_op jit(solution)/shard_map/ppermute | solution.py:350
  13.9 0.7 copy-start.7
  14.4 0.6 copy-start.8
  37.7 15.5 %all-to-all-start = ((bf16[16,32,256]{2,1,0:T(8,128)(2,1)}), bf16[16,32,256]{2,1,0:T(8,128)(2,1)S(1)}, u32[]{:S(2)}, u32[]{:S(2)}) async-start(bf16[16,32,256]{2,1,0:T(8,128)(2,1)} %bitcast.37), calls=%async_computation | async-start | bytes 524288 | tf_op jit(solution)/shard_map/all_to_all | solution.py:359
  53.2 0.7 copy-start.2
  61.8 13.5 %all-to-all-start.1 = ((bf16[16,32,256]{2,1,0:T(8,128)(2,1)}), bf16[16,32,256]{2,1,0:T(8,128)(2,1)S(1)}, u32[]{:S(2)}, u32[]{:S(2)}) async-start(bf16[16,32,256]{2,1,0:T(8,128)(2,1)} %bitcast.36), calls=%async_computation.1 | async-start | bytes 524288 | tf_op jit(solution)/shard_map/all_to_all | solution.py:359
  75.3 0.7 copy-start.1
  76.0 6.6 %copy-start.4 = (bf16[1024,256]{1,0:T(8,128)(2,1)S(1)}, bf16[1024,256]{1,0:T(8,128)(2,1)}, u32[]{:S(2)}) copy-start(bf16[1024,256]{1,0:T(8,128)(2,1)} %get-tuple-element.54) | copy-start | bytes 1572868
  83.7 2.1 %collective-permute-start.2 = (bf16[768,256]{1,0:T(8,128)(2,1)S(1)}, bf16[768,256]{1,0:T(8,128)(2,1)S(1)}, u32[]{:S(2)}, u32[]{:S(2)}) collective-permute-start(bf16[768,256]{1,0:T(8,128)(2,1)S(1)} %dynamic-slice_bitcast_fusion), channel_id=1, source_target_pairs={{0,1},{1,0},{2,3},{3,2},{4,5},{5,4},{6,7},{7,6},{8,9},{9,8},{10,11... | collective-permute-start | bytes 1179656 | tf_op jit(solution)/shard_map/ppermute | solution.py:354
  106.4 21.2 %copy-start.11 = (bf16[256,256]{1,0:T(8,128)(2,1)S(1)}, bf16[256,256]{1,0:T(8,128)(2,1)}, u32[]{:S(2)}) copy-start(bf16[256,256]{1,0:T(8,128)(2,1)} %get-tuple-element.64) | copy-start | bytes 393220
  106.4 23.8 %copy-start.10 = (bf16[256,256]{1,0:T(8,128)(2,1)S(1)}, bf16[256,256]{1,0:T(8,128)(2,1)}, u32[]{:S(2)}) copy-start(bf16[256,256]{1,0:T(8,128)(2,1)} %get-tuple-element.65) | copy-start | bytes 393220
  107.4 3.9 %collective-permute-start.6 = (bf16[272,256]{1,0:T(8,128)(2,1)S(1)}, bf16[272,256]{1,0:T(8,128)(2,1)S(1)}, u32[]{:S(2)}, u32[]{:S(2)}) collective-permute-start(bf16[272,256]{1,0:T(8,128)(2,1)S(1)} %dynamic-slice_bitcast_fusion.1), channel_id=1, source_target_pairs={{0,1},{1,0},{2,3},{3,2},{4,5},{5,4},{6,7},{7,6},{8,9},{9,8},{10,11... | collective-permute-start | bytes 417800 | tf_op jit(solution)/shard_map/ppermute | solution.py:354
  107.8 14.8 %all-to-all-start.2 = ((bf16[8,96,256]{2,1,0:T(8,128)(2,1)}), bf16[8,96,256]{2,1,0:T(8,128)(2,1)S(1)}, u32[]{:S(2)}, u32[]{:S(2)}) async-start(bf16[8,96,256]{2,1,0:T(8,128)(2,1)} %bitcast.14), calls=%async_computation.2 | async-start | bytes 786432 | tf_op jit(solution)/shard_map/all_to_all | solution.py:471
  112.3 7.7 %collective-permute-start.7 = (bf16[272,256]{1,0:T(8,128)(2,1)S(1)}, bf16[272,256]{1,0:T(8,128)(2,1)S(1)}, u32[]{:S(2)}, u32[]{:S(2)}) collective-permute-start(bf16[272,256]{1,0:T(8,128)(2,1)S(1)} %fusion.1), channel_id=1, source_target_pairs={{0,2},{1,3},{2,0},{3,1},{4,6},{5,7},{6,4},{7,5},{8,10},{9,11},{10,... | collective-permute-start | bytes 417800 | tf_op jit(solution)/shard_map/ppermute | solution.py:354
  120.0 13.7 %collective-permute-start.8 = (bf16[272,256]{1,0:T(8,128)(2,1)S(1)}, bf16[272,256]{1,0:T(8,128)(2,1)S(1)}, u32[]{:S(2)}, u32[]{:S(2)}) collective-permute-start(bf16[272,256]{1,0:T(8,128)(2,1)S(1)} %add_convert_fusion.2), channel_id=1, source_target_pairs={{0,4},{1,5},{2,6},{3,7},{4,0},{5,1},{6,2},{7,3},{8,12},{9,13},{10,... | collective-permute-start | bytes 417800 | tf_op jit(solution)/shard_map/ppermute | solution.py:354
  123.5 16.9 %all-to-all-start.3 = ((bf16[8,96,256]{2,1,0:T(8,128)(2,1)}), bf16[8,96,256]{2,1,0:T(8,128)(2,1)S(1)}, u32[]{:S(2)}, u32[]{:S(2)}) async-start(bf16[8,96,256]{2,1,0:T(8,128)(2,1)} %broadcast_in_dim.2), calls=%async_computation.3 | async-start | bytes 786432 | tf_op jit(solution)/shard_map/all_to_all | solution.py:493
  127.6 20.1 %collective-permute-start.3 = (bf16[256,256]{1,0:T(8,128)(2,1)S(1)}, bf16[256,256]{1,0:T(8,128)(2,1)S(1)}, u32[]{:S(2)}, u32[]{:S(2)}) collective-permute-start(bf16[256,256]{1,0:T(8,128)(2,1)S(1)} %copy-done.11), channel_id=1, source_target_pairs={{1,0},{2,1},{3,2},{4,3},{5,4},{6,5},{7,6},{8,7},{9,8},{10,9},{11,1... | collective-permute-start | bytes 393224 | tf_op jit(solution)/shard_map/ppermute | solution.py:350
  130.2 17.5 %collective-permute-start.4 = (bf16[256,256]{1,0:T(8,128)(2,1)S(1)}, bf16[256,256]{1,0:T(8,128)(2,1)S(1)}, u32[]{:S(2)}, u32[]{:S(2)}) collective-permute-start(bf16[256,256]{1,0:T(8,128)(2,1)S(1)} %copy-done.10), channel_id=1, source_target_pairs={{0,1},{1,2},{2,3},{3,4},{4,5},{5,6},{6,7},{7,8},{8,9},{9,10},{10,1... | collective-permute-start | bytes 393224 | tf_op jit(solution)/shard_map/ppermute | solution.py:350
  133.8 10.6 %collective-permute-start.9 = (bf16[272,256]{1,0:T(8,128)(2,1)S(1)}, bf16[272,256]{1,0:T(8,128)(2,1)S(1)}, u32[]{:S(2)}, u32[]{:S(2)}) collective-permute-start(bf16[272,256]{1,0:T(8,128)(2,1)S(1)} %add_convert_fusion.1), channel_id=1, source_target_pairs={{0,8},{1,9},{2,10},{3,11},{4,12},{5,13},{6,14},{7,15},{8,0},{9,1},... | collective-permute-start | bytes 417800 | tf_op jit(solution)/shard_map/ppermute | solution.py:354
  140.4 12.5 %copy-start = (bf16[8,96,256]{2,1,0:T(8,128)(2,1)}, bf16[8,96,256]{2,1,0:T(8,128)(2,1)S(1)}, u32[]{:S(2)}) copy-start(bf16[8,96,256]{2,1,0:T(8,128)(2,1)S(1)} %all-to-all-done.3) | copy-start | bytes 1179652
  140.4 12.6 %collective-permute-start.5 = (bf16[768,256]{1,0:T(8,128)(2,1)S(1)}, bf16[768,256]{1,0:T(8,128)(2,1)S(1)}, u32[]{:S(2)}, u32[]{:S(2)}) collective-permute-start(bf16[768,256]{1,0:T(8,128)(2,1)S(1)} %bitcast.29), channel_id=1, source_target_pairs={{0,1},{1,0},{2,3},{3,2},{4,5},{5,4},{6,7},{7,6},{8,9},{9,8},{10,11... | collective-permute-start | bytes 1179656 | tf_op jit(solution)/shard_map/ppermute | solution.py:354
  144.5 8.5 %copy-start.3 = (bf16[272,256]{1,0:T(8,128)(2,1)}, bf16[272,256]{1,0:T(8,128)(2,1)S(1)}, u32[]{:S(2)}) copy-start(bf16[272,256]{1,0:T(8,128)(2,1)S(1)} %add_convert_fusion.b_ref) | copy-start | bytes 417796
  144.5 8.5 %collective-permute-start.10 = (bf16[272,256]{1,0:T(8,128)(2,1)S(1)}, bf16[272,256]{1,0:T(8,128)(2,1)S(1)}, u32[]{:S(2)}, u32[]{:S(2)}) collective-permute-start(bf16[272,256]{1,0:T(8,128)(2,1)S(1)} %add_convert_fusion.b_ref), channel_id=1, source_target_pairs={{0,1},{1,0},{2,3},{3,2},{4,5},{5,4},{6,7},{7,6},{8,9},{9,8},{10,11... | collective-permute-start | bytes 417800 | tf_op jit(solution)/shard_map/ppermute | solution.py:354
  147.7 0.7 copy-start.12
  147.7 0.7 copy-start.13
  152.9 0.7 copy-start.6
  153.0 0.8 copy-start.5

commit v3 on v2

--- a/solution.py
+++ b/solution.py
@@ -102,15 +102,9 @@
     to_left_ref[...] = mm_tn(hot_rows(row_form(left_ref, 0, n), h.shape[0]), h).astype(bf)
 
 
-def project_kernel(h_ref, w_ref, p_ref, q_ref):
-    h = h_ref[...]
-    p_ref[...] = mm(h, w_ref[0]).astype(bf)
-    q_ref[...] = mm(h, w_ref[1]).astype(bf)
-
-
 def fine_kernel(
-    per, tiles, src_ref, p_ref, q_ref, left_ref, right_ref, h_ref, w_ref, b_ref, dst_ref, pool_ref,
-    send_ref, d_ref, agg_ref, dsu_ref, pooled_ref, out_ref, count_ref, table, taken,
+    per, tiles, src_ref, left_ref, right_ref, h_ref, w_ref, b_ref, dst_ref, pool_ref, send_ref,
+    d_ref, he_ref, agg_ref, dsu_ref, pooled_ref, out_ref, count_ref, recv, table, taken,
 ):
     t = pl.program_id(0)
     nodes = h_ref.shape[0]
@@ -119,15 +113,19 @@
 
     @pl.when(t == 0)
     def _():
-        to_pairs(table, 0, p_ref[...].astype(f32))
-        to_pairs(table, nodes, as_bf(mm(left_ref[...], w_ref[0])).astype(f32))
-        to_pairs(table, nodes + halo, as_bf(mm(right_ref[...], w_ref[0])).astype(f32))
+        recv[...] = mm(h_ref[...], w_ref[1]).astype(bf)
+        to_pairs(table, 0, h_ref[...].astype(f32))
+        to_pairs(table, nodes, left_ref[...].astype(f32))
+        to_pairs(table, nodes + halo, right_ref[...].astype(f32))
 
     for e in range(edges):
         taken[2 * e : 2 * e + 2, :] = table[pair(src_ref[t * edges + e]), :]
     rows = pl.ds(pl.multiple_of(t * TILE, TILE), TILE)
     hot = hot_rows(row_form(dst_ref, t * per, per), TILE)
-    z = from_pairs(taken, 0, edges) + mm_tn(hot, q_ref[rows, :]) + b_ref[0:1, :]
+    he = from_pairs(taken, 0, edges).astype(bf)
+    he_ref[...] = he
+    sent = as_bf(mm(he, w_ref[0])).astype(f32)
+    z = sent + mm_tn(hot, recv[rows, :]) + b_ref[0:1, :]
     m, d = silu_parts(z)
     d_ref[...] = d.astype(bf)
     agg_ref[rows, :] = mm(hot, m.astype(bf)).astype(bf)
@@ -227,9 +225,29 @@
     part_ref[...] = ghc_ref[...] + mm_nt(du, w_ref[3]) + mm_nt(dq, w_ref[1])
 
 
+def by_core(core_ref, mine_ref, other_ref, half0, half1):
+    core = core_ref[0]
+
+    def write(ref, half):
+        at = 0
+        for piece in half:
+            ref[at : at + piece.shape[0], :] = piece
+            at += piece.shape[0]
+
+    @pl.when(core == 0)
+    def _():
+        write(mine_ref, half0)
+        write(other_ref, half1)
+
+    @pl.when(core != 0)
+    def _():
+        write(mine_ref, half1)
+        write(other_ref, half0)
+
+
 def node_back_kernel(
-    own_ref, ret_ref, send_ref, part_ref, wc_ref, count_ref, pool_ref, cot_ref, dsu_ref, w_ref,
-    h_ref, agg_ref, g_ref, du_ref, dagg_ref, gw_ref,
+    core_ref, own_ref, ret_ref, send_ref, part_ref, wc_ref, count_ref, pool_ref, cot_ref, dsu_ref,
+    w_ref, h_ref, agg_ref, gwc_ref, g_ref, du_ref, dagg_ref, mine_ref, other_ref,
 ):
     coarse = own_ref.shape[0]
     width = h_ref.shape[1]
@@ -244,33 +262,56 @@
     du = (g * dsu_ref[...].astype(f32)).astype(bf)
     du_ref[...] = du
     dagg_ref[...] = mm_nt(du, w_ref[2]).astype(bf)
-    gw_ref[0:width, :] = mm_tn(agg_ref[...], du).astype(bf)
-    gw_ref[width : 2 * width, :] = mm_tn(h_ref[...], du).astype(bf)
+    gw2 = mm_tn(agg_ref[...], du).astype(bf)
+    gw3 = mm_tn(h_ref[...], du).astype(bf)
+    by_core(
+        core_ref, mine_ref, other_ref,
+        [gwc_ref[0 : 3 * width, :]], [gwc_ref[3 * width : 4 * width, :], gw2, gw3],
+    )
 
 
 def edge_back_kernel(
-    per, tiles, src_ref, d_ref, dagg_ref, h_ref, left_ref, right_ref, dst_ref, gbc_ref,
-    own_ref, gl_ref, gr_ref, dq_ref, gw_ref, gb, dzs, *accs,
+    per, tiles, core_ref, d_ref, he_ref, dagg_ref, h_ref, dst_ref, gbc_ref,
+    dz_ref, dq_ref, mine_ref, other_ref, gb, gw0,
 ):
     t = pl.program_id(0)
     nodes, width = h_ref.shape
-    halo = left_ref.shape[0]
-    edges = per * LANES
 
     @pl.when(t == 0)
     def _():
         gb[...] = jnp.zeros_like(gb)
-        for acc in accs:
-            acc[...] = jnp.zeros_like(acc)
+        gw0[...] = jnp.zeros_like(gw0)
 
     hot = hot_rows(row_form(dst_ref, t * per, per), TILE)
     rows = pl.ds(pl.multiple_of(t * TILE, TILE), TILE)
     gm = mm_tn(hot, dagg_ref[rows, :])
     dz = (gm * d_ref[...].astype(f32)).astype(bf)
+    dz_ref[...] = dz
     dq = mm(hot, dz)
     gb[...] += jnp.sum(dq, axis=0, keepdims=True)
     dq_ref[rows, :] = dq.astype(bf)
-    to_pairs(dzs, 0, dz.astype(f32))
+    gw0[...] += mm_tn(he_ref[...], dz)
+
+    @pl.when(t == tiles - 1)
+    def _():
+        gbf = jnp.broadcast_to(gb[0:1, :], (16, width)).astype(bf)
+        gbc = jnp.broadcast_to(gbc_ref[0:1, :], (16, width)).astype(bf)
+        gw1 = mm_tn(h_ref[...], dq_ref[...]).astype(bf)
+        by_core(core_ref, mine_ref, other_ref, [gw0[...].astype(bf), gbf], [gw1, gbc])
+
+
+def scatter_kernel(per, tiles, src_ref, dz_ref, own_ref, gl_ref, gr_ref, dzs, *accs):
+    t = pl.program_id(0)
+    nodes = own_ref.shape[0]
+    halo = gl_ref.shape[0]
+    edges = per * LANES
+
+    @pl.when(t == 0)
+    def _():
+        for acc in accs:
+            acc[...] = jnp.zeros_like(acc)
+
+    to_pairs(dzs, 0, dz_ref[...].astype(f32))
     for e in range(edges):
         acc = accs[e % len(accs)]
         at = pair(src_ref[t * edges + e])
@@ -284,18 +325,9 @@
                 total = total + from_pairs(acc, first, n)
             return total.astype(bf)
 
-        own = summed(0, nodes)
-        gl = summed(nodes, halo)
-        gr = summed(nodes + halo, halo)
-        own_ref[...] = own
-        gl_ref[...] = gl
-        gr_ref[...] = gr
-        gw_ref[0:width, :] = (
-            mm_tn(h_ref[...], own) + mm_tn(left_ref[...], gl) + mm_tn(right_ref[...], gr)
-        ).astype(bf)
-        gw_ref[width : width + 16, :] = jnp.broadcast_to(gb[0:1, :], (16, width)).astype(bf)
-        gw_ref[width + 16 : 2 * width + 16, :] = mm_tn(h_ref[...], dq_ref[...]).astype(bf)
-        gw_ref[2 * width + 16 :, :] = jnp.broadcast_to(gbc_ref[0:1, :], (16, width)).astype(bf)
+        own_ref[...] = summed(0, nodes)
+        gl_ref[...] = summed(nodes, halo)
+        gr_ref[...] = summed(nodes + halo, halo)
 
 
 def part_kernel(dq_ref, du_ref, g_ref, w_ref, part_ref):
@@ -360,13 +392,6 @@
         block.reshape(parts, rows // parts, width), "dom", split_axis=0, concat_axis=0, tiled=True
     )
     return got
-
-
-def halves(block, core):
-    two = block.reshape((2, block.shape[0] // 2) + block.shape[1:])
-    mine = lax.dynamic_index_in_dim(two, core, 0, keepdims=False)
-    other = lax.dynamic_index_in_dim(two, 1 - core, 0, keepdims=False)
-    return mine, other
 
 
 def add(a, b):
@@ -398,17 +423,12 @@
     h_left = shifted(to_right, "dom", 1)
     h_right = shifted(to_left, "dom", -1)
     edge_tile = pl.BlockSpec((edges, width), lambda t: (t, 0))
-    proj, recv = call(
-        project_kernel,
-        [sds((nodes, width), bf)] * 2,
-        [features, w_fine],
-        cost=(3e9, 10e6),
-    )
     smem = pl.BlockSpec(memory_space=pltpu.SMEM)
     ext_pairs = 2 * (nodes + 2 * halo)
-    d_edge, agg, dsu, pooled, outgoing, count = call(
+    d_edge, he, agg, dsu, pooled, outgoing, count = call(
         part(fine_kernel, per, tiles),
         [
+            sds((tiles * edges, width), bf),
             sds((tiles * edges, width), bf),
             sds((nodes, width), bf),
             sds((nodes, width), bf),
@@ -416,11 +436,15 @@
             sds((crows, width), bf),
             sds((coarse, LANES), f32),
         ],
-        [fine_src, proj, recv, h_left, h_right, features, w_fine, bias, fdst, pool, csend],
+        [fine_src, h_left, h_right, features, w_fine, bias, fdst, pool, csend],
         grid=(tiles,),
         specs={0: smem},
-        out_specs={0: edge_tile},
-        scratch=[pltpu.VMEM((ext_pairs, LANES), f32), pltpu.VMEM((2 * edges, LANES), f32)],
+        out_specs={0: edge_tile, 1: edge_tile},
+        scratch=[
+            pltpu.VMEM((nodes, width), bf),
+            pltpu.VMEM((ext_pairs, LANES), f32),
+            pltpu.VMEM((2 * edges, LANES), f32),
+        ],
     )
     incoming = exchange(outgoing, parts).reshape(crows, width)
     cedges = coarse_src.shape[0]
@@ -449,51 +473,61 @@
         [pooled, incoming, ghc, w_coarse, cdst, own_c, back_c, dz_c, du_c, agg_c],
         cost=(4e9, 10e6),
     )
-    g, du, dagg, gw_n = call(
+    core = (lax.axis_index("dom") % 2).astype(jnp.int32).reshape(1)
+    same_core = [list(range(c, parts, 2)) for c in range(2)]
+    chips = parts // 2
+    g, du, dagg, mine, other = call(
         node_back_kernel,
         [
             sds((nodes, width), f32),
             sds((nodes, width), bf),
             sds((nodes, width), bf),
-            sds((2 * width, width), bf),
+            sds((3 * width, width), bf),
+            sds((3 * width, width), bf),
         ],
         [
-            own_c, returned, csend, part_c, w_coarse, count, pool, cotangent, dsu, w_fine,
-            features, agg,
-        ],
-    )
-    core = lax.axis_index("dom") % 2
-    same_core = [list(range(c, parts, 2)) for c in range(2)]
-    chips = parts // 2
-    mine, other = halves(jnp.concatenate([gw_c, gw_n], axis=0), core)
+            core, own_c, returned, csend, part_c, w_coarse, count, pool, cotangent, dsu, w_fine,
+            features, agg, gw_c,
+        ],
+        specs={0: smem},
+    )
     early = add(mine, swapped(other, parts, 1))
     early, dagg = lax.optimization_barrier((early, dagg))
     early = lax.all_to_all(
         early.reshape(chips, -1, width), "dom", 0, 0, axis_index_groups=same_core, tiled=True
     )
-    own_f, gl, gr, dq, gw_e = call(
+    dz, dq, mine, other = call(
         part(edge_back_kernel, per, tiles),
         [
+            sds((tiles * edges, width), bf),
             sds((nodes, width), bf),
-            sds((halo, width), bf),
-            sds((halo, width), bf),
-            sds((nodes, width), bf),
-            sds((2 * (width + 16), width), bf),
-        ],
-        [fine_src, d_edge, dagg, features, h_left, h_right, fdst, gb_c],
+            sds((width + 16, width), bf),
+            sds((width + 16, width), bf),
+        ],
+        [core, d_edge, he, dagg, features, fdst, gb_c],
         grid=(tiles,),
-        specs={0: smem, 1: edge_tile},
-        scratch=[pltpu.VMEM((8, width), f32), pltpu.VMEM((2 * edges, LANES), f32)]
-        + [pltpu.VMEM((ext_pairs, LANES), f32)] * 8,
-        cost=(30e9, 10e6),
-    )
-    mine, other = halves(gw_e, core)
+        specs={0: smem, 1: edge_tile, 2: edge_tile},
+        out_specs={0: edge_tile},
+        scratch=[pltpu.VMEM((8, width), f32), pltpu.VMEM((width, width), f32)],
+        cost=(15e9, 10e6),
+    )
+    early, dz, dq, mine, other = lax.optimization_barrier((early, dz, dq, mine, other))
     late = add(mine, swapped(other, parts, 1))
     early = jnp.sum(early.astype(f32), axis=0).astype(bf)
     early = lax.all_to_all(
         jnp.broadcast_to(early[None], (chips,) + early.shape),
         "dom", 0, 0, axis_index_groups=same_core, tiled=True,
     ).reshape(-1, width)
+    own_f, gl, gr = call(
+        part(scatter_kernel, per, tiles),
+        [sds((nodes, width), bf), sds((halo, width), bf), sds((halo, width), bf)],
+        [fine_src, dz],
+        grid=(tiles,),
+        specs={0: smem, 1: edge_tile},
+        scratch=[pltpu.VMEM((2 * edges, LANES), f32)]
+        + [pltpu.VMEM((ext_pairs, LANES), f32)] * 8,
+        cost=(15e9, 10e6),
+    )
     bit = 2
     while bit < parts:
         late = add(late, swapped(late, parts, bit))
@@ -514,8 +548,7 @@
         part(finish_kernel, scale),
         [sds((4 * width, width), f32), sds((4 * width, width), f32), sds((2, width), f32)],
         [
-            core.astype(jnp.int32).reshape(1), early, swapped(early, parts, 1),
-            late, swapped(late, parts, 1),
+            core, early, swapped(early, parts, 1), late, swapped(late, parts, 1),
         ],
         specs={0: smem},
     )

time: 157 us -> 164 us (1.045)
  the two profiles are of different devices: /device:TPU:1 before, /device:TPU:0 now
where the time goes in v3:
time: 164 us; the launch traced here: 162 us
  Pallas kernels  95.8 us (58%)
  starting transfers between devices  36.3 us (22%)
  waiting for transfers between devices  20.3 us (12%)
  local copies, waits for them, and re-layouts  6.28 us (4%)
  other arithmetic  2.97 us (2%)
    pallas_call x11, Pallas kernels, call(): pl.pallas_call(kernel, grid=grid or (1,), in_specs=in_specs, out_specs=o_...  95.8 us
    all_to_all x2, starting transfers between devices, exchange(): lax.all_to_all(block.reshape(parts, rows // parts, width), 'dom', split_a...  12.7 us
    all_to_all x2, waiting for transfers between devices, exchange(): lax.all_to_all(block.reshape(parts, rows // parts, width), 'dom', split_a...  11.2 us
    ppermute x4, starting transfers between devices, shifted(): return lax.ppermute(block, axis, route)  7.96 us
    ppermute x7, starting transfers between devices, swapped(): return lax.ppermute(block, 'dom', [(i, i ^ bit) for i in range(parts)])  7.65 us
    ppermute x7, waiting for transfers between devices, swapped(): return lax.ppermute(block, 'dom', [(i, i ^ bit) for i in range(parts)])  6.14 us
    all_to_all x1, starting transfers between devices, shards(): lax.all_to_all(jnp.broadcast_to(early[None], (chips,) + early.shape), 'do...  4.58 us
    unnamed x20, local copies, waits for them, and re-layouts  4.14 us
  transfers between devices with their start and end apart: 15, of which 6 were waited for; matrix products, arithmetic and copies ran while one was open for 1% of the time, Pallas kernels for 32%

profile of v3, /device:TPU:0, one launch (start us, length us, event | category | flops | bytes accessed | tf_op | source)
XLA Modules:
  0.0 162.4 jit_solution(18015362192434173184)
XLA Ops:
  0.6 2.7 %shard_map.156 = (bf16[256,256]{1,0:T(8,128)(2,1)}, bf16[256,256]{1,0:T(8,128)(2,1)}) custom-call(bf16[2048,256]{1,0:T(8,128)(2,1)} %h_ref.7, s32[2,128]{1,0:T(2,128)} %bitcast.32, s32[2,128]{1,0:T(2,128)} %bitcast.34), custom_call_target="tpu_custom_call" | custom-call | tf_op jit(solution)/shard_map/pallas_call | solution.py:80
  3.3 2.4 %collective-permute-start = (bf16[256,256]{1,0:T(8,128)(2,1)}, bf16[256,256]{1,0:T(8,128)(2,1)S(1)}, u32[]{:S(2)}, u32[]{:S(2)}) collective-permute-start(bf16[256,256]{1,0:T(8,128)(2,1)} %get-tuple-element.46), channel_id=1, source_target_pairs={{0,1},{1,2},{2,3},{3,4},{4,5},{5,6},{6,7},{7,8},{8,9},{9,10},{10,1... | collective-permute-start | bytes 393224 | tf_op jit(solution)/shard_map/ppermute | solution.py:382
  5.7 1.3 collective-permute-start.1
  7.0 1.4 reshape.62.send_ref
  8.4 2.9 %collective-permute-done.1.right_ref = bf16[256,256]{1,0:T(8,128)(2,1)S(1)} collective-permute-done((bf16[256,256]{1,0:T(8,128)(2,1)}, bf16[256,256]{1,0:T(8,128)(2,1)S(1)}, u32[]{:S(2)}, u32[]{:S(2)}) %collective-permute-start.1) | collective-permute-done | bytes 131104 | tf_op jit(solution)/shard_map/ppermute | solution.py:382
  11.9 23.7 %shard_map.157 = (bf16[8192,256]{1,0:T(8,128)(2,1)}, bf16[8192,256]{1,0:T(8,128)(2,1)}, bf16[2048,256]{1,0:T(8,128)(2,1)}, bf16[2048,256]{1,0:T(8,128)(2,1)}, bf...) custom-call(s32[8192]{0:T(1024)} %src_ref.3, bf16[256,256]{1,0:T(8,128)(2,1)} %copy-done.6, ...), custom_call_target="tpu_custom_call" | custom-call | tf_op jit(solution)/shard_map/pallas_call | solution.py:80
  35.6 9.0 %all-to-all-start = ((bf16[16,32,256]{2,1,0:T(8,128)(2,1)}), bf16[16,32,256]{2,1,0:T(8,128)(2,1)S(1)}, u32[]{:S(2)}, u32[]{:S(2)}) async-start(bf16[16,32,256]{2,1,0:T(8,128)(2,1)} %bitcast.21), calls=%async_computation | async-start | bytes 524288 | tf_op jit(solution)/shard_map/all_to_all | solution.py:391
  44.6 4.9 %shard_map.158 = (f32[2048,256]{1,0:T(8,128)}, f32[512,256]{1,0:T(8,128)}, f32[512,256]{1,0:T(8,128)}) custom-call(bf16[512,256]{1,0:T(8,128)(2,1)} %get-tuple-element.48.pooled_ref, bf16[4,256,256]{2,1,0:T(8,128)(2,1)} %wc_ref.1, f32[2,256]{1,0:T(2,128)} %b_ref.3, s32[16,128]{1,0:T(8,128)} %bitcast.27, s32[16,128]{1,0:T(8,128)} %bitcast.29, ...), custom_call_target="tpu_custom_call" | custom-call | flops 4000000000 | bytes 10000000 | tf_op jit(solution)/shard_map/pallas_call | solution.py:80
  49.5 5.2 %all-to-all-done = bf16[16,32,256]{2,1,0:T(8,128)(2,1)S(1)} async-done(((bf16[16,32,256]{2,1,0:T(8,128)(2,1)}), bf16[16,32,256]{2,1,0:T(8,128)(2,1)S(1)}, u32[]{:S(2)}, u32[]{:S(2)}) %all-to-all-start) | async-done | bytes 262176 | tf_op jit(solution)/shard_map/all_to_all | solution.py:391
  55.3 7.9 %shard_map.159 = (bf16[512,256]{1,0:T(8,128)(2,1)}, bf16[512,256]{1,0:T(8,128)(2,1)}, bf16[2048,256]{1,0:T(8,128)(2,1)}, bf16[512,256]{1,0:T(8,128)(2,1)}, bf16[512,256]{1,0:T(8,128)(2,1)}) custom-call(f32[2048,256]{1,0:T(8,128)} %get-tuple-element.49.z_ref, bf16[512,256]{1,0:T(8,128)(2,1)} %bitcast.18, f32[512,256]{1,0:T(8,128)} %get-tuple-element.51.ghc_ref, ...), custom_call_target="tpu_custom_call" | custom-call | tf_op jit(solution)/shard_map/pallas_call | solution.py:80
  63.3 3.7 %all-to-all-start.1 = ((bf16[16,32,256]{2,1,0:T(8,128)(2,1)}), bf16[16,32,256]{2,1,0:T(8,128)(2,1)S(1)}, u32[]{:S(2)}, u32[]{:S(2)}) async-start(bf16[16,32,256]{2,1,0:T(8,128)(2,1)} %bitcast.20), calls=%async_computation.1 | async-start | bytes 524288 | tf_op jit(solution)/shard_map/all_to_all | solution.py:391
  67.0 3.8 %shard_map.160 = (bf16[1024,256]{1,0:T(8,128)(2,1)}, f32[8,256]{1,0:T(8,128)}, f32[512,256]{1,0:T(8,128)}) custom-call(bf16[512,256]{1,0:T(8,128)(2,1)} %get-tuple-element.48.pooled_ref, bf16[512,256]{1,0:T(8,128)(2,1)} %bitcast.19, f32[512,256]{1,0:T(8,128)} %get-tuple-element.51.ghc_ref, bf16[4,256,256]{2,1,0:T(8,128)(2,1)} %wc_ref.1, s32[16,128]{1,0:T(8,128)} %bitcast.31, ...), custom_call_target="tpu_custom_call" | custom-call | flops 4000000000 | bytes 10000000 | tf_op jit(solution)/shard_map/pallas_call | solution.py:80
  70.8 6.0 %all-to-all-done.1 = bf16[16,32,256]{2,1,0:T(8,128)(2,1)S(1)} async-done(((bf16[16,32,256]{2,1,0:T(8,128)(2,1)}), bf16[16,32,256]{2,1,0:T(8,128)(2,1)S(1)}, u32[]{:S(2)}, u32[]{:S(2)}) %all-to-all-start.1) | async-done | bytes 262176 | tf_op jit(solution)/shard_map/all_to_all | solution.py:391
  77.5 7.5 %shard_map.161 = (f32[2048,256]{1,0:T(8,128)}, bf16[2048,256]{1,0:T(8,128)(2,1)}, bf16[2048,256]{1,0:T(8,128)(2,1)}, bf16[768,256]{1,0:T(8,128)(2,1)}, bf16[768,256]{1,0:T(8,128)(2,1)}) custom-call(s32[1]{0:T(128)} %bitcast.core_ref, bf16[512,256]{1,0:T(8,128)(2,1)} %get-tuple-element.53.own_ref, bf16[512,256]{1,0:T(8,128)(2,1)} %bitcast.17, ...), custom_call_target="tpu_custom_call" | custom-call | tf_op jit(solution)/shard_map/pallas_call | solution.py:80
  85.0 1.9 %collective-permute-done.2 = bf16[768,256]{1,0:T(8,128)(2,1)S(1)} collective-permute-done((bf16[768,256]{1,0:T(8,128)(2,1)}, bf16[768,256]{1,0:T(8,128)(2,1)S(1)}, u32[]{:S(2)}, u32[]{:S(2)}) %collective-permute-start.2) | collective-permute-done | bytes 393248 | tf_op jit(solution)/shard_map/ppermute | solution.py:386
  86.9 1.8 %add_convert_fusion = bf16[768,256]{1,0:T(8,128)(2,1)} fusion(bf16[768,256]{1,0:T(8,128)(2,1)S(1)} %collective-permute-done.2, bf16[768,256]{1,0:T(8,128)(2,1)} %get-tuple-element.63), kind=kLoop, calls=%fused_computation | loop fusion | flops 786432 | bytes 1179648 | tf_op jit(solution)/shard_map/convert_element_type | solution.py:398
  88.8 3.5 %all-to-all-start.2 = ((bf16[8,96,256]{2,1,0:T(8,128)(2,1)}), bf16[8,96,256]{2,1,0:T(8,128)(2,1)S(1)}, u32[]{:S(2)}, u32[]{:S(2)}) async-start(bf16[8,96,256]{2,1,0:T(8,128)(2,1)} %bitcast.11), calls=%async_computation.2 | async-start | bytes 786432 | tf_op jit(solution)/shard_map/all_to_all | solution.py:496
  92.3 16.9 %shard_map.162 = (bf16[8192,256]{1,0:T(8,128)(2,1)}, bf16[2048,256]{1,0:T(8,128)(2,1)}, bf16[272,256]{1,0:T(8,128)(2,1)}, bf16[272,256]{1,0:T(8,128)(2,1)}) custom-call(s32[1]{0:T(128)} %bitcast.core_ref, bf16[8192,256]{1,0:T(8,128)(2,1)} %get-tuple-element.67.d_ref, bf16[8192,256]{1,0:T(8,128)(2,1)} %get-tuple-element.68.he_ref, ...), custom_call_target="tpu_custom_call" | custom-call | flops 15000000512 | bytes 10000000 | tf_op jit(solution)/shard_map/pallas_call | solution.py:80
  109.3 1.4 collective-permute-done.6
  110.8 1.0 add_convert_fusion.4
  111.7 2.0 %collective-permute-start.7 = (bf16[272,256]{1,0:T(8,128)(2,1)S(1)}, bf16[272,256]{1,0:T(8,128)(2,1)S(1)}, u32[]{:S(2)}, u32[]{:S(2)}) collective-permute-start(bf16[272,256]{1,0:T(8,128)(2,1)S(1)} %add_convert_fusion.4), channel_id=1, source_target_pairs={{0,2},{1,3},{2,0},{3,1},{4,6},{5,7},{6,4},{7,5},{8,10},{9,11},{10,... | collective-permute-start | bytes 417800 | tf_op jit(solution)/shard_map/ppermute | solution.py:386
  114.6 4.6 %all-to-all-start.3 = ((bf16[8,96,256]{2,1,0:T(8,128)(2,1)}), bf16[8,96,256]{2,1,0:T(8,128)(2,1)S(1)}, u32[]{:S(2)}, u32[]{:S(2)}) async-start(bf16[8,96,256]{2,1,0:T(8,128)(2,1)} %broadcast_in_dim.2), calls=%async_computation.3 | async-start | bytes 786432 | tf_op jit(solution)/shard_map/all_to_all | solution.py:517
  119.2 2.1 %collective-permute-start.8 = (bf16[272,256]{1,0:T(8,128)(2,1)S(1)}, bf16[272,256]{1,0:T(8,128)(2,1)S(1)}, u32[]{:S(2)}, u32[]{:S(2)}) collective-permute-start(bf16[272,256]{1,0:T(8,128)(2,1)S(1)} %add_convert_fusion.3), channel_id=1, source_target_pairs={{0,4},{1,5},{2,6},{3,7},{4,0},{5,1},{6,2},{7,3},{8,12},{9,13},{10,... | collective-permute-start | bytes 417800 | tf_op jit(solution)/shard_map/ppermute | solution.py:386
  121.3 16.8 %shard_map.163 = (bf16[2048,256]{1,0:T(8,128)(2,1)}, bf16[256,256]{1,0:T(8,128)(2,1)}, bf16[256,256]{1,0:T(8,128)(2,1)}) custom-call(s32[8192]{0:T(1024)} %src_ref.3, bf16[8192,256]{1,0:T(8,128)(2,1)} %get-tuple-element.75.dz_ref), custom_call_target="tpu_custom_call" | custom-call | flops 15000000512 | bytes 10000000 | tf_op jit(solution)/shard_map/pallas_call | solution.py:80
  138.1 1.3 collective-permute-start.3
  139.4 3.0 %collective-permute-start.4 = (bf16[256,256]{1,0:T(8,128)(2,1)}, bf16[256,256]{1,0:T(8,128)(2,1)S(1)}, u32[]{:S(2)}, u32[]{:S(2)}) collective-permute-start(bf16[256,256]{1,0:T(8,128)(2,1)} %get-tuple-element.78), channel_id=1, source_target_pairs={{0,1},{1,2},{2,3},{3,4},{4,5},{5,6},{6,7},{7,8},{8,9},{9,10},{10,1... | collective-permute-start | bytes 393224 | tf_op jit(solution)/shard_map/ppermute | solution.py:382
  142.5 2.4 %collective-permute-start.9 = (bf16[272,256]{1,0:T(8,128)(2,1)S(1)}, bf16[272,256]{1,0:T(8,128)(2,1)S(1)}, u32[]{:S(2)}, u32[]{:S(2)}) collective-permute-start(bf16[272,256]{1,0:T(8,128)(2,1)S(1)} %add_convert_fusion.2), channel_id=1, source_target_pairs={{0,8},{1,9},{2,10},{3,11},{4,12},{5,13},{6,14},{7,15},{8,0},{9,1},... | collective-permute-start | bytes 417800 | tf_op jit(solution)/shard_map/ppermute | solution.py:386
  144.9 4.4 %shard_map.164.part_ref = f32[2048,256]{1,0:T(8,128)} custom-call(bf16[2048,256]{1,0:T(8,128)(2,1)} %get-tuple-element.79.dq_ref, bf16[2048,256]{1,0:T(8,128)(2,1)} %get-tuple-element.80.du_ref, f32[2048,256]{1,0:T(8,128)} %get-tuple-element.81.g_ref, bf16[4,256,256]{2,1,0:T(8,128)(2,1)} %w_ref.13), custom_call_target="tpu_custom_call" | custom-call | flops 4000000000 | bytes 10000000 | tf_op jit(solution)/shard_map/pallas_call | solution.py:80
  149.3 0.8 collective-permute-start.5
  150.1 2.8 %collective-permute-done.9 = bf16[272,256]{1,0:T(8,128)(2,1)S(1)} collective-permute-done((bf16[272,256]{1,0:T(8,128)(2,1)S(1)}, bf16[272,256]{1,0:T(8,128)(2,1)S(1)}, u32[]{:S(2)}, u32[]{:S(2)}) %collective-permute-start.9) | collective-permute-done | bytes 139296 | tf_op jit(solution)/shard_map/ppermute | solution.py:386
  153.8 4.5 %shard_map.165 = f32[2048,256]{1,0:T(8,128)} custom-call(bf16[2048,256]{1,0:T(8,128)(2,1)} %get-tuple-element.76.own_ref, bf16[256,256]{1,0:T(8,128)(2,1)} %copy-done.8, bf16[256,256]{1,0:T(8,128)(2,1)} %copy-done.9, s32[2,128]{1,0:T(2,128)} %bitcast.33, s32[2,128]{1,0:T(2,128)} %bitcast.35, f32[2048,256]{1,0:T(8,128)} %shard_map.164.part_ref, ...), custom_call_target="tpu_custom_call" | custom-call | flops 4000000000 | bytes 10000000 | tf_op jit(solution)/shard_map/pallas_call | solution.py:80
  159.8 2.6 %shard_map.166 = (f32[1024,256]{1,0:T(8,128)}, f32[1024,256]{1,0:T(8,128)}, f32[2,256]{1,0:T(2,128)}) custom-call(s32[1]{0:T(128)} %bitcast.core_ref, bf16[768,256]{1,0:T(8,128)(2,1)} %bitcast.16, bf16[768,256]{1,0:T(8,128)(2,1)} %copy-done.4, bf16[272,256]{1,0:T(8,128)(2,1)} %copy-done.3, bf16[272,256]{1,0:T(8,128)(2,1)} %copy-done.5), custom_call_target="tpu_custom_call" | custom-call | tf_op jit(solution)/shard_map/pallas_call | solution.py:80
  (37 shorter events, 5.5 us)
Async XLA Ops:
  3.3 5.0 %collective-permute-start = (bf16[256,256]{1,0:T(8,128)(2,1)}, bf16[256,256]{1,0:T(8,128)(2,1)S(1)}, u32[]{:S(2)}, u32[]{:S(2)}) collective-permute-start(bf16[256,256]{1,0:T(8,128)(2,1)} %get-tuple-element.46), channel_id=1, source_target_pairs={{0,1},{1,2},{2,3},{3,4},{4,5},{5,6},{6,7},{7,8},{8,9},{9,10},{10,1... | collective-permute-start | bytes 393224 | tf_op jit(solution)/shard_map/ppermute | solution.py:382
  5.7 5.6 %collective-permute-start.1 = (bf16[256,256]{1,0:T(8,128)(2,1)}, bf16[256,256]{1,0:T(8,128)(2,1)S(1)}, u32[]{:S(2)}, u32[]{:S(2)}) collective-permute-start(bf16[256,256]{1,0:T(8,128)(2,1)} %get-tuple-element.47), channel_id=1, source_target_pairs={{1,0},{2,1},{3,2},{4,3},{5,4},{6,5},{7,6},{8,7},{9,8},{10,9},{11,1... | collective-permute-start | bytes 393224 | tf_op jit(solution)/shard_map/ppermute | solution.py:382
  8.4 2.9 %copy-start.6 = (bf16[256,256]{1,0:T(8,128)(2,1)}, bf16[256,256]{1,0:T(8,128)(2,1)S(1)}, u32[]{:S(2)}) copy-start(bf16[256,256]{1,0:T(8,128)(2,1)S(1)} %collective-permute-done.left_ref) | copy-start | bytes 393220
  11.3 0.6 copy-start.7
  35.6 19.0 %all-to-all-start = ((bf16[16,32,256]{2,1,0:T(8,128)(2,1)}), bf16[16,32,256]{2,1,0:T(8,128)(2,1)S(1)}, u32[]{:S(2)}, u32[]{:S(2)}) async-start(bf16[16,32,256]{2,1,0:T(8,128)(2,1)} %bitcast.21), calls=%async_computation | async-start | bytes 524288 | tf_op jit(solution)/shard_map/all_to_all | solution.py:391
  54.6 0.7 copy-start.2
  63.3 13.5 %all-to-all-start.1 = ((bf16[16,32,256]{2,1,0:T(8,128)(2,1)}), bf16[16,32,256]{2,1,0:T(8,128)(2,1)S(1)}, u32[]{:S(2)}, u32[]{:S(2)}) async-start(bf16[16,32,256]{2,1,0:T(8,128)(2,1)} %bitcast.20), calls=%async_computation.1 | async-start | bytes 524288 | tf_op jit(solution)/shard_map/all_to_all | solution.py:391
  76.8 0.7 copy-start.1
  85.0 1.9 %collective-permute-start.2 = (bf16[768,256]{1,0:T(8,128)(2,1)}, bf16[768,256]{1,0:T(8,128)(2,1)S(1)}, u32[]{:S(2)}, u32[]{:S(2)}) collective-permute-start(bf16[768,256]{1,0:T(8,128)(2,1)} %get-tuple-element.64), channel_id=1, source_target_pairs={{0,1},{1,0},{2,3},{3,2},{4,5},{5,4},{6,7},{7,6},{8,9},{9,8},{10,11... | collective-permute-start | bytes 1179656 | tf_op jit(solution)/shard_map/ppermute | solution.py:386
  88.8 20.3 %all-to-all-start.2 = ((bf16[8,96,256]{2,1,0:T(8,128)(2,1)}), bf16[8,96,256]{2,1,0:T(8,128)(2,1)S(1)}, u32[]{:S(2)}, u32[]{:S(2)}) async-start(bf16[8,96,256]{2,1,0:T(8,128)(2,1)} %bitcast.11), calls=%async_computation.2 | async-start | bytes 786432 | tf_op jit(solution)/shard_map/all_to_all | solution.py:496
  109.1 1.6 %collective-permute-start.6 = (bf16[272,256]{1,0:T(8,128)(2,1)}, bf16[272,256]{1,0:T(8,128)(2,1)S(1)}, u32[]{:S(2)}, u32[]{:S(2)}) collective-permute-start(bf16[272,256]{1,0:T(8,128)(2,1)} %get-tuple-element.84), channel_id=1, source_target_pairs={{0,1},{1,0},{2,3},{3,2},{4,5},{5,4},{6,7},{7,6},{8,9},{9,8},{10,11... | collective-permute-start | bytes 417800 | tf_op jit(solution)/shard_map/ppermute | solution.py:386
  111.7 7.4 %collective-permute-start.7 = (bf16[272,256]{1,0:T(8,128)(2,1)S(1)}, bf16[272,256]{1,0:T(8,128)(2,1)S(1)}, u32[]{:S(2)}, u32[]{:S(2)}) collective-permute-start(bf16[272,256]{1,0:T(8,128)(2,1)S(1)} %add_convert_fusion.4), channel_id=1, source_target_pairs={{0,2},{1,3},{2,0},{3,1},{4,6},{5,7},{6,4},{7,5},{8,10},{9,11},{10,... | collective-permute-start | bytes 417800 | tf_op jit(solution)/shard_map/ppermute | solution.py:386
  114.6 34.7 %all-to-all-start.3 = ((bf16[8,96,256]{2,1,0:T(8,128)(2,1)}), bf16[8,96,256]{2,1,0:T(8,128)(2,1)S(1)}, u32[]{:S(2)}, u32[]{:S(2)}) async-start(bf16[8,96,256]{2,1,0:T(8,128)(2,1)} %broadcast_in_dim.2), calls=%async_computation.3 | async-start | bytes 786432 | tf_op jit(solution)/shard_map/all_to_all | solution.py:517
  119.2 23.2 %collective-permute-start.8 = (bf16[272,256]{1,0:T(8,128)(2,1)S(1)}, bf16[272,256]{1,0:T(8,128)(2,1)S(1)}, u32[]{:S(2)}, u32[]{:S(2)}) collective-permute-start(bf16[272,256]{1,0:T(8,128)(2,1)S(1)} %add_convert_fusion.3), channel_id=1, source_target_pairs={{0,4},{1,5},{2,6},{3,7},{4,0},{5,1},{6,2},{7,3},{8,12},{9,13},{10,... | collective-permute-start | bytes 417800 | tf_op jit(solution)/shard_map/ppermute | solution.py:386
  138.1 15.0 %collective-permute-start.3 = (bf16[256,256]{1,0:T(8,128)(2,1)}, bf16[256,256]{1,0:T(8,128)(2,1)S(1)}, u32[]{:S(2)}, u32[]{:S(2)}) collective-permute-start(bf16[256,256]{1,0:T(8,128)(2,1)} %get-tuple-element.77), channel_id=1, source_target_pairs={{1,0},{2,1},{3,2},{4,3},{5,4},{6,5},{7,6},{8,7},{9,8},{10,9},{11,1... | collective-permute-start | bytes 393224 | tf_op jit(solution)/shard_map/ppermute | solution.py:382
  139.4 13.7 %collective-permute-start.4 = (bf16[256,256]{1,0:T(8,128)(2,1)}, bf16[256,256]{1,0:T(8,128)(2,1)S(1)}, u32[]{:S(2)}, u32[]{:S(2)}) collective-permute-start(bf16[256,256]{1,0:T(8,128)(2,1)} %get-tuple-element.78), channel_id=1, source_target_pairs={{0,1},{1,2},{2,3},{3,4},{4,5},{5,6},{6,7},{7,8},{8,9},{9,10},{10,1... | collective-permute-start | bytes 393224 | tf_op jit(solution)/shard_map/ppermute | solution.py:382
  142.5 10.4 %collective-permute-start.9 = (bf16[272,256]{1,0:T(8,128)(2,1)S(1)}, bf16[272,256]{1,0:T(8,128)(2,1)S(1)}, u32[]{:S(2)}, u32[]{:S(2)}) collective-permute-start(bf16[272,256]{1,0:T(8,128)(2,1)S(1)} %add_convert_fusion.2), channel_id=1, source_target_pairs={{0,8},{1,9},{2,10},{3,11},{4,12},{5,13},{6,14},{7,15},{8,0},{9,1},... | collective-permute-start | bytes 417800 | tf_op jit(solution)/shard_map/ppermute | solution.py:386
  149.3 9.1 %copy-start = (bf16[8,96,256]{2,1,0:T(8,128)(2,1)}, bf16[8,96,256]{2,1,0:T(8,128)(2,1)S(1)}, u32[]{:S(2)}) copy-start(bf16[8,96,256]{2,1,0:T(8,128)(2,1)S(1)} %all-to-all-done.3) | copy-start | bytes 1179652
  149.3 9.1 %collective-permute-start.5 = (bf16[768,256]{1,0:T(8,128)(2,1)S(1)}, bf16[768,256]{1,0:T(8,128)(2,1)S(1)}, u32[]{:S(2)}, u32[]{:S(2)}) collective-permute-start(bf16[768,256]{1,0:T(8,128)(2,1)S(1)} %bitcast.15), channel_id=1, source_target_pairs={{0,1},{1,0},{2,3},{3,2},{4,5},{5,4},{6,7},{7,6},{8,9},{9,8},{10,11... | collective-permute-start | bytes 1179656 | tf_op jit(solution)/shard_map/ppermute | solution.py:386
  152.9 5.5 %copy-start.3 = (bf16[272,256]{1,0:T(8,128)(2,1)}, bf16[272,256]{1,0:T(8,128)(2,1)S(1)}, u32[]{:S(2)}) copy-start(bf16[272,256]{1,0:T(8,128)(2,1)S(1)} %add_convert_fusion.1.b_ref) | copy-start | bytes 417796
  152.9 5.5 %collective-permute-start.10 = (bf16[272,256]{1,0:T(8,128)(2,1)S(1)}, bf16[272,256]{1,0:T(8,128)(2,1)S(1)}, u32[]{:S(2)}, u32[]{:S(2)}) collective-permute-start(bf16[272,256]{1,0:T(8,128)(2,1)S(1)} %add_convert_fusion.1.b_ref), channel_id=1, source_target_pairs={{0,1},{1,0},{2,3},{3,2},{4,5},{5,4},{6,7},{7,6},{8,9},{9,8},{10,11... | collective-permute-start | bytes 417800 | tf_op jit(solution)/shard_map/ppermute | solution.py:386
  153.1 0.7 copy-start.8
  153.1 0.7 copy-start.9
  158.4 0.7 copy-start.5
  159.0 0.7 copy-start.4

commit v4 on v3

--- a/solution.py
+++ b/solution.py
@@ -45,6 +45,22 @@
     return jnp.concatenate(
         [jnp.where(high == bf(k), base, bf(0)) for k in range(rows // 256)], axis=0
     )
+
+
+def tile_loop(group, body):
+    if group == 1:
+        body(0)
+    else:
+
+        def step(k, carry):
+            body(k)
+            return carry
+
+        lax.fori_loop(0, group, step, 0)
+
+
+def tile_rows(index, size):
+    return pl.ds(pl.multiple_of(index * size, size), size)
 
 
 def silu_parts(v):
@@ -103,34 +119,38 @@
 
 
 def fine_kernel(
-    per, tiles, src_ref, left_ref, right_ref, h_ref, w_ref, b_ref, dst_ref, pool_ref, send_ref,
+    per, group, src_ref, left_ref, right_ref, h_ref, w_ref, b_ref, dst_ref, pool_ref, send_ref,
     d_ref, he_ref, agg_ref, dsu_ref, pooled_ref, out_ref, count_ref, recv, table, taken,
 ):
-    t = pl.program_id(0)
+    step = pl.program_id(0)
     nodes = h_ref.shape[0]
     halo = left_ref.shape[0]
     edges = per * LANES
 
-    @pl.when(t == 0)
+    @pl.when(step == 0)
     def _():
         recv[...] = mm(h_ref[...], w_ref[1]).astype(bf)
         to_pairs(table, 0, h_ref[...].astype(f32))
         to_pairs(table, nodes, left_ref[...].astype(f32))
         to_pairs(table, nodes + halo, right_ref[...].astype(f32))
 
-    for e in range(edges):
-        taken[2 * e : 2 * e + 2, :] = table[pair(src_ref[t * edges + e]), :]
-    rows = pl.ds(pl.multiple_of(t * TILE, TILE), TILE)
-    hot = hot_rows(row_form(dst_ref, t * per, per), TILE)
-    he = from_pairs(taken, 0, edges).astype(bf)
-    he_ref[...] = he
-    sent = as_bf(mm(he, w_ref[0])).astype(f32)
-    z = sent + mm_tn(hot, recv[rows, :]) + b_ref[0:1, :]
-    m, d = silu_parts(z)
-    d_ref[...] = d.astype(bf)
-    agg_ref[rows, :] = mm(hot, m.astype(bf)).astype(bf)
-
-    @pl.when(t == tiles - 1)
+    def tile(k):
+        t = step * group + k
+        for e in range(edges):
+            taken[2 * e : 2 * e + 2, :] = table[pair(src_ref[t * edges + e]), :]
+        rows = tile_rows(t, TILE)
+        hot = hot_rows(row_form(dst_ref, t * per, per), TILE)
+        he = from_pairs(taken, 0, edges).astype(bf)
+        he_ref[tile_rows(k, edges), :] = he
+        sent = as_bf(mm(he, w_ref[0])).astype(f32)
+        z = sent + mm_tn(hot, recv[rows, :]) + b_ref[0:1, :]
+        m, d = silu_parts(z)
+        d_ref[tile_rows(k, edges), :] = d.astype(bf)
+        agg_ref[rows, :] = mm(hot, m.astype(bf)).astype(bf)
+
+    tile_loop(group, tile)
+
+    @pl.when(step == pl.num_programs(0) - 1)
     def _():
         h = h_ref[...]
         u = mm(h, w_ref[3]) + mm(agg_ref[...], w_ref[2])
@@ -201,6 +221,26 @@
     back_ref[...] = total[coarse:].astype(bf)
 
 
+def by_core(core_ref, mine_ref, other_ref, half0, half1):
+    core = core_ref[0]
+
+    def write(ref, half):
+        at = 0
+        for piece in half:
+            ref[at : at + piece.shape[0], :] = piece
+            at += piece.shape[0]
+
+    @pl.when(core == 0)
+    def _():
+        write(mine_ref, half0)
+        write(other_ref, half1)
+
+    @pl.when(core != 0)
+    def _():
+        write(mine_ref, half1)
+        write(other_ref, half0)
+
+
 def coarse_grad_kernel(
     per, pooled_ref, in_ref, ghc_ref, w_ref, dst_ref, own_ref, back_ref, dz_ref, du_ref, agg_ref,
     gw_ref, gb_ref, part_ref,
@@ -225,32 +265,11 @@
     part_ref[...] = ghc_ref[...] + mm_nt(du, w_ref[3]) + mm_nt(dq, w_ref[1])
 
 
-def by_core(core_ref, mine_ref, other_ref, half0, half1):
-    core = core_ref[0]
-
-    def write(ref, half):
-        at = 0
-        for piece in half:
-            ref[at : at + piece.shape[0], :] = piece
-            at += piece.shape[0]
-
-    @pl.when(core == 0)
-    def _():
-        write(mine_ref, half0)
-        write(other_ref, half1)
-
-    @pl.when(core != 0)
-    def _():
-        write(mine_ref, half1)
-        write(other_ref, half0)
-
-
 def node_back_kernel(
-    core_ref, own_ref, ret_ref, send_ref, part_ref, wc_ref, count_ref, pool_ref, cot_ref, dsu_ref,
-    w_ref, h_ref, agg_ref, gwc_ref, g_ref, du_ref, dagg_ref, mine_ref, other_ref,
+    own_ref, ret_ref, send_ref, part_ref, wc_ref, count_ref, pool_ref, cot_ref, dsu_ref, w_ref,
+    g_ref, du_ref, dagg_ref,
 ):
     coarse = own_ref.shape[0]
-    width = h_ref.shape[1]
     sends = hot_rows(row_form(send_ref, 0, send_ref.shape[0]), coarse)
     dp = (own_ref[...].astype(f32) + mm(sends, ret_ref[...])).astype(bf)
     dc = part_ref[...] + mm_nt(dp, wc_ref[0])
@@ -262,62 +281,71 @@
     du = (g * dsu_ref[...].astype(f32)).astype(bf)
     du_ref[...] = du
     dagg_ref[...] = mm_nt(du, w_ref[2]).astype(bf)
-    gw2 = mm_tn(agg_ref[...], du).astype(bf)
-    gw3 = mm_tn(h_ref[...], du).astype(bf)
-    by_core(
-        core_ref, mine_ref, other_ref,
-        [gwc_ref[0 : 3 * width, :]], [gwc_ref[3 * width : 4 * width, :], gw2, gw3],
-    )
 
 
 def edge_back_kernel(
-    per, tiles, core_ref, d_ref, he_ref, dagg_ref, h_ref, dst_ref, gbc_ref,
+    per, group, core_ref, d_ref, he_ref, dagg_ref, h_ref, dst_ref, gwc_ref, gbc_ref, agg_ref, du_ref,
     dz_ref, dq_ref, mine_ref, other_ref, gb, gw0,
 ):
-    t = pl.program_id(0)
-    nodes, width = h_ref.shape
-
-    @pl.when(t == 0)
+    step = pl.program_id(0)
+    width = h_ref.shape[1]
+    edges = per * LANES
+
+    @pl.when(step == 0)
     def _():
         gb[...] = jnp.zeros_like(gb)
         gw0[...] = jnp.zeros_like(gw0)
 
-    hot = hot_rows(row_form(dst_ref, t * per, per), TILE)
-    rows = pl.ds(pl.multiple_of(t * TILE, TILE), TILE)
-    gm = mm_tn(hot, dagg_ref[rows, :])
-    dz = (gm * d_ref[...].astype(f32)).astype(bf)
-    dz_ref[...] = dz
-    dq = mm(hot, dz)
-    gb[...] += jnp.sum(dq, axis=0, keepdims=True)
-    dq_ref[rows, :] = dq.astype(bf)
-    gw0[...] += mm_tn(he_ref[...], dz)
-
-    @pl.when(t == tiles - 1)
+    def tile(k):
+        t = step * group + k
+        hot = hot_rows(row_form(dst_ref, t * per, per), TILE)
+        rows = tile_rows(t, TILE)
+        here = tile_rows(k, edges)
+        gm = mm_tn(hot, dagg_ref[rows, :])
+        dz = (gm * d_ref[here, :].astype(f32)).astype(bf)
+        dz_ref[here, :] = dz
+        dq = mm(hot, dz)
+        gb[...] += jnp.sum(dq, axis=0, keepdims=True)
+        dq_ref[rows, :] = dq.astype(bf)
+
+    tile_loop(group, tile)
+    gw0[...] += mm_tn(he_ref[...], dz_ref[...])
+
+    @pl.when(step == pl.num_programs(0) - 1)
     def _():
         gbf = jnp.broadcast_to(gb[0:1, :], (16, width)).astype(bf)
         gbc = jnp.broadcast_to(gbc_ref[0:1, :], (16, width)).astype(bf)
-        gw1 = mm_tn(h_ref[...], dq_ref[...]).astype(bf)
-        by_core(core_ref, mine_ref, other_ref, [gw0[...].astype(bf), gbf], [gw1, gbc])
-
-
-def scatter_kernel(per, tiles, src_ref, dz_ref, own_ref, gl_ref, gr_ref, dzs, *accs):
-    t = pl.program_id(0)
+        h = h_ref[...]
+        gw1 = mm_tn(h, dq_ref[...]).astype(bf)
+        gw2 = mm_tn(agg_ref[...], du_ref[...]).astype(bf)
+        gw3 = mm_tn(h, du_ref[...]).astype(bf)
+        half0 = [gwc_ref[0 : 2 * width, :], gw0[...].astype(bf), gw1] + [gbf] * 4
+        half1 = [gwc_ref[2 * width : 4 * width, :], gw2, gw3] + [gbc] * 4
+        by_core(core_ref, mine_ref, other_ref, half0, half1)
+
+
+def scatter_kernel(per, group, src_ref, dz_ref, own_ref, gl_ref, gr_ref, dzs, *accs):
+    step = pl.program_id(0)
     nodes = own_ref.shape[0]
     halo = gl_ref.shape[0]
     edges = per * LANES
 
-    @pl.when(t == 0)
+    @pl.when(step == 0)
     def _():
         for acc in accs:
             acc[...] = jnp.zeros_like(acc)
 
-    to_pairs(dzs, 0, dz_ref[...].astype(f32))
-    for e in range(edges):
-        acc = accs[e % len(accs)]
-        at = pair(src_ref[t * edges + e])
-        acc[at, :] = acc[at, :] + dzs[2 * e : 2 * e + 2, :]
-
-    @pl.when(t == tiles - 1)
+    def tile(k):
+        t = step * group + k
+        to_pairs(dzs, 0, dz_ref[tile_rows(k, edges), :].astype(f32))
+        for e in range(edges):
+            acc = accs[e % len(accs)]
+            at = pair(src_ref[t * edges + e])
+            acc[at, :] = acc[at, :] + dzs[2 * e : 2 * e + 2, :]
+
+    tile_loop(group, tile)
+
+    @pl.when(step == pl.num_programs(0) - 1)
     def _():
         def summed(first, n):
             total = from_pairs(accs[0], first, n)
@@ -346,34 +374,26 @@
     o_ref[...] = part_ref[...] + mm_nt(dp, w_ref[0])
 
 
-def finish_kernel(scale, core_ref, a_ref, ax_ref, b_ref, bx_ref, gf_ref, gc_ref, gb_ref):
-    width = a_ref.shape[1]
-
-    def write(a0, a1, b0, b1):
-        def put(ref, k, src, at):
-            ref[k * width : (k + 1) * width, :] = (
-                src[at * width : (at + 1) * width, :].astype(f32) * scale
-            )
-
-        for k in range(3):
-            put(gc_ref, k, a0, k)
-        put(gc_ref, 3, a1, 0)
-        put(gf_ref, 2, a1, 1)
-        put(gf_ref, 3, a1, 2)
-        put(gf_ref, 0, b0, 0)
-        put(gf_ref, 1, b1, 0)
-        gb_ref[0:1, :] = b0[width : width + 1, :].astype(f32) * scale
-        gb_ref[1:2, :] = b1[width : width + 1, :].astype(f32) * scale
+def finish_kernel(scale, core_ref, a_ref, ax_ref, gf_ref, gc_ref, gb_ref):
+    two = gf_ref.shape[0] // 2
+
+    def write(half, src):
+        rows = slice(half * two, (half + 1) * two)
+        gc_ref[rows, :] = src[0:two, :].astype(f32) * scale
+        gf_ref[rows, :] = src[two : 2 * two, :].astype(f32) * scale
+        gb_ref[half : half + 1, :] = src[2 * two : 2 * two + 16, :].astype(f32)[0:1] * scale
 
     core = core_ref[0]
 
     @pl.when(core == 0)
     def _():
-        write(a_ref, ax_ref, b_ref, bx_ref)
+        write(0, a_ref)
+        write(1, ax_ref)
 
     @pl.when(core != 0)
     def _():
-        write(ax_ref, a_ref, bx_ref, b_ref)
+        write(1, a_ref)
+        write(0, ax_ref)
 
 
 def shifted(block, axis, distance):
@@ -396,6 +416,10 @@
 
 def add(a, b):
     return (a.astype(f32) + b.astype(f32)).astype(bf)
+
+
+def over_chips(blocks, groups):
+    return lax.all_to_all(blocks, "dom", 0, 0, axis_index_groups=groups, tiled=True)
 
 
 def shards(
@@ -416,17 +440,22 @@
     csend = coarse_send.reshape(-1, LANES)
     crows = coarse_send.shape[0] * coarse_send.shape[1]
     part = functools.partial
+    core = (lax.axis_index("dom") % 2).astype(jnp.int32).reshape(1)
+    same_core = [list(range(c, parts, 2)) for c in range(2)]
+    chips = parts // 2
+    group = 4
+    steps = tiles // group
 
     to_right, to_left = call(
         halo_kernel, [sds((halo, width), bf)] * 2, [features, right, left]
     )
     h_left = shifted(to_right, "dom", 1)
     h_right = shifted(to_left, "dom", -1)
-    edge_tile = pl.BlockSpec((edges, width), lambda t: (t, 0))
+    edge_tile = pl.BlockSpec((group * edges, width), lambda t: (t, 0))
     smem = pl.BlockSpec(memory_space=pltpu.SMEM)
     ext_pairs = 2 * (nodes + 2 * halo)
     d_edge, he, agg, dsu, pooled, outgoing, count = call(
-        part(fine_kernel, per, tiles),
+        part(fine_kernel, per, group),
         [
             sds((tiles * edges, width), bf),
             sds((tiles * edges, width), bf),
@@ -437,7 +466,7 @@
             sds((coarse, LANES), f32),
         ],
         [fine_src, h_left, h_right, features, w_fine, bias, fdst, pool, csend],
-        grid=(tiles,),
+        grid=(steps,),
         specs={0: smem},
         out_specs={0: edge_tile, 1: edge_tile},
         scratch=[
@@ -473,65 +502,44 @@
         [pooled, incoming, ghc, w_coarse, cdst, own_c, back_c, dz_c, du_c, agg_c],
         cost=(4e9, 10e6),
     )
-    core = (lax.axis_index("dom") % 2).astype(jnp.int32).reshape(1)
-    same_core = [list(range(c, parts, 2)) for c in range(2)]
-    chips = parts // 2
-    g, du, dagg, mine, other = call(
+    g, du, dagg = call(
         node_back_kernel,
-        [
-            sds((nodes, width), f32),
-            sds((nodes, width), bf),
-            sds((nodes, width), bf),
-            sds((3 * width, width), bf),
-            sds((3 * width, width), bf),
-        ],
-        [
-            core, own_c, returned, csend, part_c, w_coarse, count, pool, cotangent, dsu, w_fine,
-            features, agg, gw_c,
-        ],
-        specs={0: smem},
-    )
-    early = add(mine, swapped(other, parts, 1))
-    early, dagg = lax.optimization_barrier((early, dagg))
-    early = lax.all_to_all(
-        early.reshape(chips, -1, width), "dom", 0, 0, axis_index_groups=same_core, tiled=True
-    )
+        [sds((nodes, width), f32), sds((nodes, width), bf), sds((nodes, width), bf)],
+        [own_c, returned, csend, part_c, w_coarse, count, pool, cotangent, dsu, w_fine],
+        cost=(6e9, 10e6),
+    )
+    half_rows = 4 * width + 64
     dz, dq, mine, other = call(
-        part(edge_back_kernel, per, tiles),
+        part(edge_back_kernel, per, group),
         [
             sds((tiles * edges, width), bf),
             sds((nodes, width), bf),
-            sds((width + 16, width), bf),
-            sds((width + 16, width), bf),
+            sds((half_rows, width), bf),
+            sds((half_rows, width), bf),
         ],
-        [core, d_edge, he, dagg, features, fdst, gb_c],
-        grid=(tiles,),
+        [core, d_edge, he, dagg, features, fdst, gw_c, gb_c, agg, du],
+        grid=(steps,),
         specs={0: smem, 1: edge_tile, 2: edge_tile},
         out_specs={0: edge_tile},
         scratch=[pltpu.VMEM((8, width), f32), pltpu.VMEM((width, width), f32)],
         cost=(15e9, 10e6),
     )
-    early, dz, dq, mine, other = lax.optimization_barrier((early, dz, dq, mine, other))
-    late = add(mine, swapped(other, parts, 1))
-    early = jnp.sum(early.astype(f32), axis=0).astype(bf)
-    early = lax.all_to_all(
-        jnp.broadcast_to(early[None], (chips,) + early.shape),
-        "dom", 0, 0, axis_index_groups=same_core, tiled=True,
-    ).reshape(-1, width)
+    sums = add(mine, swapped(other, parts, 1)).reshape(chips, -1, width)
+    sums, dz = lax.optimization_barrier((sums, dz))
+    sums = over_chips(sums, same_core)
     own_f, gl, gr = call(
-        part(scatter_kernel, per, tiles),
+        part(scatter_kernel, per, group),
         [sds((nodes, width), bf), sds((halo, width), bf), sds((halo, width), bf)],
         [fine_src, dz],
-        grid=(tiles,),
+        grid=(steps,),
         specs={0: smem, 1: edge_tile},
         scratch=[pltpu.VMEM((2 * edges, LANES), f32)]
         + [pltpu.VMEM((ext_pairs, LANES), f32)] * 8,
         cost=(15e9, 10e6),
     )
-    bit = 2
-    while bit < parts:
-        late = add(late, swapped(late, parts, bit))
-        bit *= 2
+    sums, own_f, gl, gr = lax.optimization_barrier((sums, own_f, gl, gr))
+    sums = jnp.sum(sums.astype(f32), axis=0).astype(bf)
+    sums = over_chips(jnp.broadcast_to(sums[None], (chips,) + sums.shape), same_core)
     from_right = shifted(gl, "dom", -1)
     from_left = shifted(gr, "dom", 1)
     (part_f,) = call(
@@ -543,13 +551,13 @@
         [own_f, from_right, from_left, right, left, part_f, w_fine],
         cost=(4e9, 10e6),
     )
+    sums, grad_input = lax.optimization_barrier((sums, grad_input))
+    sums = sums.reshape(half_rows, width)
     scale = 1.0 / float(nodes * parts // 256)
     grad_fine, grad_coarse, grad_bias = call(
         part(finish_kernel, scale),
         [sds((4 * width, width), f32), sds((4 * width, width), f32), sds((2, width), f32)],
-        [
-            core, early, swapped(early, parts, 1), late, swapped(late, parts, 1),
-        ],
+        [core, sums, swapped(sums, parts, 1)],
         specs={0: smem},
     )
     shape = (4, width, width)

time: 164 us -> 153 us (0.933)
  the two profiles are of different devices: /device:TPU:0 before, /device:TPU:13 now
where the time goes in v4:
time: 153 us; the launch traced here: 152 us
  Pallas kernels  89 us (58%)
  starting transfers between devices  33.7 us (22%)
  waiting for transfers between devices  20.1 us (13%)
  local copies, waits for them, and re-layouts  6.43 us (4%)
  other arithmetic  2.08 us (1%)
    pallas_call x11, Pallas kernels, call(): pl.pallas_call(kernel, grid=grid or (1,), in_specs=in_specs, out_specs=o_...  89 us
    ppermute x4, starting transfers between devices, shifted(): return lax.ppermute(block, axis, route)  12.1 us
    all_to_all x2, starting transfers between devices, over_chips(): lax.all_to_all(blocks, 'dom', 0, 0, axis_index_groups=groups, tiled=True)  10.8 us
    all_to_all x2, starting transfers between devices, exchange(): lax.all_to_all(block.reshape(parts, rows // parts, width), 'dom', split_a...  10.5 us
    ppermute x4, waiting for transfers between devices, shifted(): return lax.ppermute(block, axis, route)  8.91 us
    all_to_all x2, waiting for transfers between devices, exchange(): lax.all_to_all(block.reshape(parts, rows // parts, width), 'dom', split_a...  7.26 us
    unnamed x20, local copies, waits for them, and re-layouts  4.23 us
    ppermute x2, waiting for transfers between devices, swapped(): return lax.ppermute(block, 'dom', [(i, i ^ bit) for i in range(parts)])  3.92 us
  transfers between devices with their start and end apart: 10, of which 6 were waited for; matrix products, arithmetic and copies ran while one was open for 1% of the time, Pallas kernels for 21%

profile of v4, /device:TPU:13, one launch (start us, length us, event | category | flops | bytes accessed | tf_op | source)
XLA Modules:
  0.0 152.1 jit_solution(9516924500069261192)
XLA Ops:
  0.6 2.7 %shard_map.156 = (bf16[256,256]{1,0:T(8,128)(2,1)}, bf16[256,256]{1,0:T(8,128)(2,1)}) custom-call(bf16[2048,256]{1,0:T(8,128)(2,1)} %h_ref.5, s32[2,128]{1,0:T(2,128)} %bitcast.32, s32[2,128]{1,0:T(2,128)} %bitcast.34), custom_call_target="tpu_custom_call" | custom-call | tf_op jit(solution)/shard_map/pallas_call | solution.py:96
  3.3 3.7 %collective-permute-start = (bf16[256,256]{1,0:T(8,128)(2,1)}, bf16[256,256]{1,0:T(8,128)(2,1)S(1)}, u32[]{:S(2)}, u32[]{:S(2)}) collective-permute-start(bf16[256,256]{1,0:T(8,128)(2,1)} %get-tuple-element.45), channel_id=1, source_target_pairs={{0,1},{1,2},{2,3},{3,4},{4,5},{5,6},{6,7},{7,8},{8,9},{9,10},{10,1... | collective-permute-start | bytes 393224 | tf_op jit(solution)/shard_map/ppermute | solution.py:402
  7.0 1.9 %collective-permute-start.1 = (bf16[256,256]{1,0:T(8,128)(2,1)}, bf16[256,256]{1,0:T(8,128)(2,1)S(1)}, u32[]{:S(2)}, u32[]{:S(2)}) collective-permute-start(bf16[256,256]{1,0:T(8,128)(2,1)} %get-tuple-element.46), channel_id=1, source_target_pairs={{1,0},{2,1},{3,2},{4,3},{5,4},{6,5},{7,6},{8,7},{9,8},{10,9},{11,1... | collective-permute-start | bytes 393224 | tf_op jit(solution)/shard_map/ppermute | solution.py:402
  9.0 1.4 reshape.62.send_ref
  10.3 4.1 %collective-permute-done.1.right_ref = bf16[256,256]{1,0:T(8,128)(2,1)S(1)} collective-permute-done((bf16[256,256]{1,0:T(8,128)(2,1)}, bf16[256,256]{1,0:T(8,128)(2,1)S(1)}, u32[]{:S(2)}, u32[]{:S(2)}) %collective-permute-start.1) | collective-permute-done | bytes 131104 | tf_op jit(solution)/shard_map/ppermute | solution.py:402
  14.4 0.7 copy-done.5
  15.1 23.2 %shard_map.157 = (bf16[8192,256]{1,0:T(8,128)(2,1)}, bf16[8192,256]{1,0:T(8,128)(2,1)}, bf16[2048,256]{1,0:T(8,128)(2,1)}, bf16[2048,256]{1,0:T(8,128)(2,1)}, bf...) custom-call(s32[8192]{0:T(1024)} %src_ref.3, bf16[256,256]{1,0:T(8,128)(2,1)} %copy-done.4, ...), custom_call_target="tpu_custom_call" | custom-call | tf_op jit(solution)/shard_map/pallas_call | solution.py:96
  38.3 5.0 %all-to-all-start = ((bf16[16,32,256]{2,1,0:T(8,128)(2,1)}), bf16[16,32,256]{2,1,0:T(8,128)(2,1)S(1)}, u32[]{:S(2)}, u32[]{:S(2)}) async-start(bf16[16,32,256]{2,1,0:T(8,128)(2,1)} %bitcast.21), calls=%async_computation | async-start | bytes 524288 | tf_op jit(solution)/shard_map/all_to_all | solution.py:411
  43.3 4.9 %shard_map.158 = (f32[2048,256]{1,0:T(8,128)}, f32[512,256]{1,0:T(8,128)}, f32[512,256]{1,0:T(8,128)}) custom-call(bf16[512,256]{1,0:T(8,128)(2,1)} %get-tuple-element.49.pooled_ref, bf16[4,256,256]{2,1,0:T(8,128)(2,1)} %wc_ref.1, f32[2,256]{1,0:T(2,128)} %b_ref.3, s32[16,128]{1,0:T(8,128)} %bitcast.24, s32[16,128]{1,0:T(8,128)} %bitcast.26, ...), custom_call_target="tpu_custom_call" | custom-call | flops 4000000000 | bytes 10000000 | tf_op jit(solution)/shard_map/pallas_call | solution.py:96
  48.2 3.1 %all-to-all-done = bf16[16,32,256]{2,1,0:T(8,128)(2,1)S(1)} async-done(((bf16[16,32,256]{2,1,0:T(8,128)(2,1)}), bf16[16,32,256]{2,1,0:T(8,128)(2,1)S(1)}, u32[]{:S(2)}, u32[]{:S(2)}) %all-to-all-start) | async-done | bytes 262176 | tf_op jit(solution)/shard_map/all_to_all | solution.py:411
  51.2 0.7 copy-done.1
  52.0 7.9 %shard_map.159 = (bf16[512,256]{1,0:T(8,128)(2,1)}, bf16[512,256]{1,0:T(8,128)(2,1)}, bf16[2048,256]{1,0:T(8,128)(2,1)}, bf16[512,256]{1,0:T(8,128)(2,1)}, bf16[512,256]{1,0:T(8,128)(2,1)}) custom-call(f32[2048,256]{1,0:T(8,128)} %get-tuple-element.50.z_ref, bf16[512,256]{1,0:T(8,128)(2,1)} %bitcast.17, f32[512,256]{1,0:T(8,128)} %get-tuple-element.52.ghc_ref, ...), custom_call_target="tpu_custom_call" | custom-call | tf_op jit(solution)/shard_map/pallas_call | solution.py:96
  59.9 5.5 %all-to-all-start.1 = ((bf16[16,32,256]{2,1,0:T(8,128)(2,1)}), bf16[16,32,256]{2,1,0:T(8,128)(2,1)S(1)}, u32[]{:S(2)}, u32[]{:S(2)}) async-start(bf16[16,32,256]{2,1,0:T(8,128)(2,1)} %bitcast.20), calls=%async_computation.1 | async-start | bytes 524288 | tf_op jit(solution)/shard_map/all_to_all | solution.py:411
  65.4 3.8 %shard_map.160 = (bf16[1024,256]{1,0:T(8,128)(2,1)}, f32[8,256]{1,0:T(8,128)}, f32[512,256]{1,0:T(8,128)}) custom-call(bf16[512,256]{1,0:T(8,128)(2,1)} %get-tuple-element.49.pooled_ref, bf16[512,256]{1,0:T(8,128)(2,1)} %bitcast.18, f32[512,256]{1,0:T(8,128)} %get-tuple-element.52.ghc_ref, bf16[4,256,256]{2,1,0:T(8,128)(2,1)} %wc_ref.1, s32[16,128]{1,0:T(8,128)} %bitcast.28, ...), custom_call_target="tpu_custom_call" | custom-call | flops 4000000000 | bytes 10000000 | tf_op jit(solution)/shard_map/pallas_call | solution.py:96
  69.2 4.2 %all-to-all-done.1 = bf16[16,32,256]{2,1,0:T(8,128)(2,1)S(1)} async-done(((bf16[16,32,256]{2,1,0:T(8,128)(2,1)}), bf16[16,32,256]{2,1,0:T(8,128)(2,1)S(1)}, u32[]{:S(2)}, u32[]{:S(2)}) %all-to-all-start.1) | async-done | bytes 262176 | tf_op jit(solution)/shard_map/all_to_all | solution.py:411
  73.4 0.7 copy-done.3
  74.1 5.8 %shard_map.161 = (f32[2048,256]{1,0:T(8,128)}, bf16[2048,256]{1,0:T(8,128)(2,1)}, bf16[2048,256]{1,0:T(8,128)(2,1)}) custom-call(bf16[512,256]{1,0:T(8,128)(2,1)} %get-tuple-element.54.own_ref, bf16[512,256]{1,0:T(8,128)(2,1)} %bitcast.19, s32[4,128]{1,0:T(4,128)} %reshape.62.send_ref, f32[512,256]{1,0:T(8,128)} %get-tuple-element.59.part_ref, ...), custom_call_target="tpu_custom_call" | custom-call | flops 6000000000 | bytes 10000000 | tf_op jit(solution)/shard_map/pallas_call | solution.py:96
  79.9 15.2 %shard_map.162 = (bf16[8192,256]{1,0:T(8,128)(2,1)}, bf16[2048,256]{1,0:T(8,128)(2,1)}, bf16[1088,256]{1,0:T(8,128)(2,1)}, bf16[1088,256]{1,0:T(8,128)(2,1)}) custom-call(s32[1]{0:T(128)} %bitcast.core_ref, bf16[8192,256]{1,0:T(8,128)(2,1)} %get-tuple-element.47.d_ref, bf16[8192,256]{1,0:T(8,128)(2,1)} %get-tuple-element.48.he_ref, ...), custom_call_target="tpu_custom_call" | custom-call | flops 15000000512 | bytes 10000000 | tf_op jit(solution)/shard_map/pallas_call | solution.py:96
  95.4 2.0 %collective-permute-done.2 = bf16[1088,256]{1,0:T(8,128)(2,1)S(1)} collective-permute-done((bf16[1088,256]{1,0:T(8,128)(2,1)}, bf16[1088,256]{1,0:T(8,128)(2,1)S(1)}, u32[]{:S(2)}, u32[]{:S(2)}) %collective-permute-start.2) | collective-permute-done | bytes 557088 | tf_op jit(solution)/shard_map/ppermute | solution.py:406
  97.4 2.0 %add_convert_fusion = bf16[1088,256]{1,0:T(8,128)(2,1)} fusion(bf16[1088,256]{1,0:T(8,128)(2,1)S(1)} %collective-permute-done.2, bf16[1088,256]{1,0:T(8,128)(2,1)} %get-tuple-element.67), kind=kLoop, calls=%fused_computation | loop fusion | flops 1114112 | bytes 1671168 | tf_op jit(solution)/shard_map/convert_element_type | solution.py:418
  99.4 5.4 %all-to-all-start.2 = ((bf16[8,136,256]{2,1,0:T(8,128)(2,1)}), bf16[8,136,256]{2,1,0:T(8,128)(2,1)S(1)}, u32[]{:S(2)}, u32[]{:S(2)}) async-start(bf16[8,136,256]{2,1,0:T(8,128)(2,1)} %bitcast.11), calls=%async_computation.2 | async-start | bytes 1114112 | tf_op jit(solution)/shard_map/all_to_all | solution.py:422
  104.7 13.9 %shard_map.163 = (bf16[2048,256]{1,0:T(8,128)(2,1)}, bf16[256,256]{1,0:T(8,128)(2,1)}, bf16[256,256]{1,0:T(8,128)(2,1)}) custom-call(s32[8192]{0:T(1024)} %src_ref.3, bf16[8192,256]{1,0:T(8,128)(2,1)} %get-tuple-element.71.dz_ref), custom_call_target="tpu_custom_call" | custom-call | flops 15000000512 | bytes 10000000 | tf_op jit(solution)/shard_map/pallas_call | solution.py:96
  118.8 0.9 broadcast_in_dim.2
  119.6 5.5 %all-to-all-start.3 = ((bf16[8,136,256]{2,1,0:T(8,128)(2,1)}), bf16[8,136,256]{2,1,0:T(8,128)(2,1)S(1)}, u32[]{:S(2)}, u32[]{:S(2)}) async-start(bf16[8,136,256]{2,1,0:T(8,128)(2,1)} %broadcast_in_dim.2), calls=%async_computation.3 | async-start | bytes 1114112 | tf_op jit(solution)/shard_map/all_to_all | solution.py:422
  125.1 3.1 %collective-permute-start.3 = (bf16[256,256]{1,0:T(8,128)(2,1)S(1)}, bf16[256,256]{1,0:T(8,128)(2,1)S(1)}, u32[]{:S(2)}, u32[]{:S(2)}) collective-permute-start(bf16[256,256]{1,0:T(8,128)(2,1)S(1)} %copy-done.7), channel_id=1, source_target_pairs={{1,0},{2,1},{3,2},{4,3},{5,4},{6,5},{7,6},{8,7},{9,8},{10,9},{11,1... | collective-permute-start | bytes 393224 | tf_op jit(solution)/shard_map/ppermute | solution.py:402
  128.2 3.3 %collective-permute-start.4 = (bf16[256,256]{1,0:T(8,128)(2,1)S(1)}, bf16[256,256]{1,0:T(8,128)(2,1)S(1)}, u32[]{:S(2)}, u32[]{:S(2)}) collective-permute-start(bf16[256,256]{1,0:T(8,128)(2,1)S(1)} %copy-done.6), channel_id=1, source_target_pairs={{0,1},{1,2},{2,3},{3,4},{4,5},{5,6},{6,7},{7,8},{8,9},{9,10},{10,1... | collective-permute-start | bytes 393224 | tf_op jit(solution)/shard_map/ppermute | solution.py:402
  131.5 4.4 %shard_map.164.part_ref = f32[2048,256]{1,0:T(8,128)} custom-call(bf16[2048,256]{1,0:T(8,128)(2,1)} %get-tuple-element.79.dq_ref, bf16[2048,256]{1,0:T(8,128)(2,1)} %get-tuple-element.66.du_ref, f32[2048,256]{1,0:T(8,128)} %get-tuple-element.80.g_ref, bf16[4,256,256]{2,1,0:T(8,128)(2,1)} %w_ref.13), custom_call_target="tpu_custom_call" | custom-call | flops 4000000000 | bytes 10000000 | tf_op jit(solution)/shard_map/pallas_call | solution.py:96
  136.0 4.8 %collective-permute-done.3.from_right_ref = bf16[256,256]{1,0:T(8,128)(2,1)S(1)} collective-permute-done((bf16[256,256]{1,0:T(8,128)(2,1)S(1)}, bf16[256,256]{1,0:T(8,128)(2,1)S(1)}, u32[]{:S(2)}, u32[]{:S(2)}) %collective-permute-start.3) | collective-permute-done | bytes 131104 | tf_op jit(solution)/shard_map/ppermute | solution.py:402
  142.1 4.5 %shard_map.165 = f32[2048,256]{1,0:T(8,128)} custom-call(bf16[2048,256]{1,0:T(8,128)(2,1)} %get-tuple-element.76.own_ref, bf16[256,256]{1,0:T(8,128)(2,1)} %copy-done.8, bf16[256,256]{1,0:T(8,128)(2,1)} %copy-done.9, s32[2,128]{1,0:T(2,128)} %bitcast.33, s32[2,128]{1,0:T(2,128)} %bitcast.35, f32[2048,256]{1,0:T(8,128)} %shard_map.164.part_ref, ...), custom_call_target="tpu_custom_call" | custom-call | flops 4000000000 | bytes 10000000 | tf_op jit(solution)/shard_map/pallas_call | solution.py:96
  146.6 1.9 %collective-permute-done.5.ax_ref = bf16[1088,256]{1,0:T(8,128)(2,1)S(1)} collective-permute-done((bf16[1088,256]{1,0:T(8,128)(2,1)S(1)}, bf16[1088,256]{1,0:T(8,128)(2,1)S(1)}, u32[]{:S(2)}, u32[]{:S(2)}) %collective-permute-start.5) | collective-permute-done | bytes 557088 | tf_op jit(solution)/shard_map/ppermute | solution.py:406
  148.6 0.8 copy-done.2
  149.4 2.7 %shard_map.166 = (f32[1024,256]{1,0:T(8,128)}, f32[1024,256]{1,0:T(8,128)}, f32[2,256]{1,0:T(2,128)}) custom-call(s32[1]{0:T(128)} %bitcast.core_ref, bf16[1088,256]{1,0:T(8,128)(2,1)} %bitcast.16, bf16[1088,256]{1,0:T(8,128)(2,1)} %copy-done.2), custom_call_target="tpu_custom_call" | custom-call | tf_op jit(solution)/shard_map/pallas_call | solution.py:96
  (23 shorter events, 1.7 us)
Async XLA Ops:
  3.3 7.0 %collective-permute-start = (bf16[256,256]{1,0:T(8,128)(2,1)}, bf16[256,256]{1,0:T(8,128)(2,1)S(1)}, u32[]{:S(2)}, u32[]{:S(2)}) collective-permute-start(bf16[256,256]{1,0:T(8,128)(2,1)} %get-tuple-element.45), channel_id=1, source_target_pairs={{0,1},{1,2},{2,3},{3,4},{4,5},{5,6},{6,7},{7,8},{8,9},{9,10},{10,1... | collective-permute-start | bytes 393224 | tf_op jit(solution)/shard_map/ppermute | solution.py:402
  7.0 7.4 %collective-permute-start.1 = (bf16[256,256]{1,0:T(8,128)(2,1)}, bf16[256,256]{1,0:T(8,128)(2,1)S(1)}, u32[]{:S(2)}, u32[]{:S(2)}) collective-permute-start(bf16[256,256]{1,0:T(8,128)(2,1)} %get-tuple-element.46), channel_id=1, source_target_pairs={{1,0},{2,1},{3,2},{4,3},{5,4},{6,5},{7,6},{8,7},{9,8},{10,9},{11,1... | collective-permute-start | bytes 393224 | tf_op jit(solution)/shard_map/ppermute | solution.py:402
  10.3 4.1 %copy-start.4 = (bf16[256,256]{1,0:T(8,128)(2,1)}, bf16[256,256]{1,0:T(8,128)(2,1)S(1)}, u32[]{:S(2)}) copy-start(bf16[256,256]{1,0:T(8,128)(2,1)S(1)} %collective-permute-done.left_ref) | copy-start | bytes 393220
  14.4 0.7 copy-start.5
  38.3 13.0 %all-to-all-start = ((bf16[16,32,256]{2,1,0:T(8,128)(2,1)}), bf16[16,32,256]{2,1,0:T(8,128)(2,1)S(1)}, u32[]{:S(2)}, u32[]{:S(2)}) async-start(bf16[16,32,256]{2,1,0:T(8,128)(2,1)} %bitcast.21), calls=%async_computation | async-start | bytes 524288 | tf_op jit(solution)/shard_map/all_to_all | solution.py:411
  51.2 0.7 copy-start.1
  59.9 13.5 %all-to-all-start.1 = ((bf16[16,32,256]{2,1,0:T(8,128)(2,1)}), bf16[16,32,256]{2,1,0:T(8,128)(2,1)S(1)}, u32[]{:S(2)}, u32[]{:S(2)}) async-start(bf16[16,32,256]{2,1,0:T(8,128)(2,1)} %bitcast.20), calls=%async_computation.1 | async-start | bytes 524288 | tf_op jit(solution)/shard_map/all_to_all | solution.py:411
  73.4 0.7 copy-start.3
  95.1 2.2 %collective-permute-start.2 = (bf16[1088,256]{1,0:T(8,128)(2,1)}, bf16[1088,256]{1,0:T(8,128)(2,1)S(1)}, u32[]{:S(2)}, u32[]{:S(2)}) collective-permute-start(bf16[1088,256]{1,0:T(8,128)(2,1)} %get-tuple-element.68), channel_id=1, source_target_pairs={{0,1},{1,0},{2,3},{3,2},{4,5},{5,4},{6,7},{7,6},{8,9},{9,8},{10,11... | collective-permute-start | bytes 1671176 | tf_op jit(solution)/shard_map/ppermute | solution.py:406
  99.4 19.3 %all-to-all-start.2 = ((bf16[8,136,256]{2,1,0:T(8,128)(2,1)}), bf16[8,136,256]{2,1,0:T(8,128)(2,1)S(1)}, u32[]{:S(2)}, u32[]{:S(2)}) async-start(bf16[8,136,256]{2,1,0:T(8,128)(2,1)} %bitcast.11), calls=%async_computation.2 | async-start | bytes 1114112 | tf_op jit(solution)/shard_map/all_to_all | solution.py:422
  118.7 6.4 %copy-start.7 = (bf16[256,256]{1,0:T(8,128)(2,1)S(1)}, bf16[256,256]{1,0:T(8,128)(2,1)}, u32[]{:S(2)}) copy-start(bf16[256,256]{1,0:T(8,128)(2,1)} %get-tuple-element.77) | copy-start | bytes 393220
  118.7 9.5 %copy-start.6 = (bf16[256,256]{1,0:T(8,128)(2,1)S(1)}, bf16[256,256]{1,0:T(8,128)(2,1)}, u32[]{:S(2)}) copy-start(bf16[256,256]{1,0:T(8,128)(2,1)} %get-tuple-element.78) | copy-start | bytes 393220
  119.6 27.0 %all-to-all-start.3 = ((bf16[8,136,256]{2,1,0:T(8,128)(2,1)}), bf16[8,136,256]{2,1,0:T(8,128)(2,1)S(1)}, u32[]{:S(2)}, u32[]{:S(2)}) async-start(bf16[8,136,256]{2,1,0:T(8,128)(2,1)} %broadcast_in_dim.2), calls=%async_computation.3 | async-start | bytes 1114112 | tf_op jit(solution)/shard_map/all_to_all | solution.py:422
  125.1 15.7 %collective-permute-start.3 = (bf16[256,256]{1,0:T(8,128)(2,1)S(1)}, bf16[256,256]{1,0:T(8,128)(2,1)S(1)}, u32[]{:S(2)}, u32[]{:S(2)}) collective-permute-start(bf16[256,256]{1,0:T(8,128)(2,1)S(1)} %copy-done.7), channel_id=1, source_target_pairs={{1,0},{2,1},{3,2},{4,3},{5,4},{6,5},{7,6},{8,7},{9,8},{10,9},{11,1... | collective-permute-start | bytes 393224 | tf_op jit(solution)/shard_map/ppermute | solution.py:402
  128.2 12.6 %collective-permute-start.4 = (bf16[256,256]{1,0:T(8,128)(2,1)S(1)}, bf16[256,256]{1,0:T(8,128)(2,1)S(1)}, u32[]{:S(2)}, u32[]{:S(2)}) collective-permute-start(bf16[256,256]{1,0:T(8,128)(2,1)S(1)} %copy-done.6), channel_id=1, source_target_pairs={{0,1},{1,2},{2,3},{3,4},{4,5},{5,6},{6,7},{7,8},{8,9},{9,10},{10,1... | collective-permute-start | bytes 393224 | tf_op jit(solution)/shard_map/ppermute | solution.py:402
  140.8 0.7 copy-start.8
  141.4 0.6 copy-start.9
  146.6 2.0 %copy-start = (bf16[8,136,256]{2,1,0:T(8,128)(2,1)}, bf16[8,136,256]{2,1,0:T(8,128)(2,1)S(1)}, u32[]{:S(2)}) copy-start(bf16[8,136,256]{2,1,0:T(8,128)(2,1)S(1)} %all-to-all-done.3) | copy-start | bytes 1671172
  146.6 2.0 %collective-permute-start.5 = (bf16[1088,256]{1,0:T(8,128)(2,1)S(1)}, bf16[1088,256]{1,0:T(8,128)(2,1)S(1)}, u32[]{:S(2)}, u32[]{:S(2)}) collective-permute-start(bf16[1088,256]{1,0:T(8,128)(2,1)S(1)} %bitcast.15), channel_id=1, source_target_pairs={{0,1},{1,0},{2,3},{3,2},{4,5},{5,4},{6,7},{7,6},{8,9},{9,8},{10,11... | collective-permute-start | bytes 1671176 | tf_op jit(solution)/shard_map/ppermute | solution.py:406
  148.6 0.8 copy-start.2

commit v5 on v4

--- a/solution.py
+++ b/solution.py
@@ -11,6 +11,8 @@
 f32 = jnp.float32
 TILE = 128
 LANES = 128
+FINE_UNROLL = 4
+EDGE_UNROLL = 4
 
 
 def mm(a, b):
@@ -47,16 +49,18 @@
     )
 
 
-def tile_loop(group, body):
-    if group == 1:
-        body(0)
+def tile_loop(group, unroll, body):
+    if group == unroll:
+        for k in range(group):
+            body(k, k)
     else:
 
-        def step(k, carry):
-            body(k)
+        def step(j, carry):
+            for k in range(unroll):
+                body(j * unroll + k, k)
             return carry
 
-        lax.fori_loop(0, group, step, 0)
+        lax.fori_loop(0, group // unroll, step, 0)
 
 
 def tile_rows(index, size):
@@ -100,7 +104,7 @@
         out_specs=o_specs,
         out_shape=outs,
         scratch_shapes=list(scratch),
-        compiler_params=pltpu.CompilerParams(vmem_limit_bytes=56 << 20),
+        compiler_params=pltpu.CompilerParams(vmem_limit_bytes=24 << 20),
         cost_estimate=pl.CostEstimate(
             flops=int(cost[0]), bytes_accessed=int(cost[1]), transcendentals=0
         ),
@@ -134,13 +138,14 @@
         to_pairs(table, nodes, left_ref[...].astype(f32))
         to_pairs(table, nodes + halo, right_ref[...].astype(f32))
 
-    def tile(k):
+    def tile(k, slot):
         t = step * group + k
         for e in range(edges):
-            taken[2 * e : 2 * e + 2, :] = table[pair(src_ref[t * edges + e]), :]
+            at = 2 * (slot * edges + e)
+            taken[at : at + 2, :] = table[pair(src_ref[t * edges + e]), :]
         rows = tile_rows(t, TILE)
         hot = hot_rows(row_form(dst_ref, t * per, per), TILE)
-        he = from_pairs(taken, 0, edges).astype(bf)
+        he = from_pairs(taken, slot * edges, edges).astype(bf)
         he_ref[tile_rows(k, edges), :] = he
         sent = as_bf(mm(he, w_ref[0])).astype(f32)
         z = sent + mm_tn(hot, recv[rows, :]) + b_ref[0:1, :]
@@ -148,7 +153,7 @@
         d_ref[tile_rows(k, edges), :] = d.astype(bf)
         agg_ref[rows, :] = mm(hot, m.astype(bf)).astype(bf)
 
-    tile_loop(group, tile)
+    tile_loop(group, FINE_UNROLL, tile)
 
     @pl.when(step == pl.num_programs(0) - 1)
     def _():
@@ -296,7 +301,7 @@
         gb[...] = jnp.zeros_like(gb)
         gw0[...] = jnp.zeros_like(gw0)
 
-    def tile(k):
+    def tile(k, slot):
         t = step * group + k
         hot = hot_rows(row_form(dst_ref, t * per, per), TILE)
         rows = tile_rows(t, TILE)
@@ -308,7 +313,7 @@
         gb[...] += jnp.sum(dq, axis=0, keepdims=True)
         dq_ref[rows, :] = dq.astype(bf)
 
-    tile_loop(group, tile)
+    tile_loop(group, EDGE_UNROLL, tile)
     gw0[...] += mm_tn(he_ref[...], dz_ref[...])
 
     @pl.when(step == pl.num_programs(0) - 1)
@@ -335,7 +340,7 @@
         for acc in accs:
             acc[...] = jnp.zeros_like(acc)
 
-    def tile(k):
+    def tile(k, slot):
         t = step * group + k
         to_pairs(dzs, 0, dz_ref[tile_rows(k, edges), :].astype(f32))
         for e in range(edges):
@@ -343,7 +348,7 @@
             at = pair(src_ref[t * edges + e])
             acc[at, :] = acc[at, :] + dzs[2 * e : 2 * e + 2, :]
 
-    tile_loop(group, tile)
+    tile_loop(group, 1, tile)
 
     @pl.when(step == pl.num_programs(0) - 1)
     def _():
@@ -472,7 +477,7 @@
         scratch=[
             pltpu.VMEM((nodes, width), bf),
             pltpu.VMEM((ext_pairs, LANES), f32),
-            pltpu.VMEM((2 * edges, LANES), f32),
+            pltpu.VMEM((2 * FINE_UNROLL * edges, LANES), f32),
         ],
     )
     incoming = exchange(outgoing, parts).reshape(crows, width)
@@ -534,7 +539,7 @@
         grid=(steps,),
         specs={0: smem, 1: edge_tile},
         scratch=[pltpu.VMEM((2 * edges, LANES), f32)]
-        + [pltpu.VMEM((ext_pairs, LANES), f32)] * 8,
+        + [pltpu.VMEM((ext_pairs, LANES), f32)] * 6,
         cost=(15e9, 10e6),
     )
     sums, own_f, gl, gr = lax.optimization_barrier((sums, own_f, gl, gr))

time: 153 us -> 156 us (1.020)
  local copies, waits for them, and re-layouts: 6.43 us -> 47.8 us
  Pallas kernels: 89 us -> 52.5 us
  waiting for transfers between devices: 20.1 us -> 17 us
    unnamed x20 -> x124, local copies, waits for them, and re-layouts: 4.23 us -> 46.1 us
    pallas_call x11, Pallas kernels: 89 us -> 52.5 us  [call(): pl.pallas_call(kernel, grid=grid or (1,), in_specs=in_specs, out_specs=o_...]
    all_to_all x2, waiting for transfers between devices: 7.26 us -> 2.93 us  [exchange(): lax.all_to_all(block.reshape(parts, rows // parts, width), 'dom', split_a...]
    ppermute x4, waiting for transfers between devices: 8.91 us -> 10.5 us  [shifted(): return lax.ppermute(block, axis, route)]
  transfers between devices with their start and end apart: 10 -> 10, of which waited for: 6 -> 5; matrix products, arithmetic and copies ran while one was open for 1% -> 1% of each run, Pallas kernels for 21% -> 12%
where the time goes in v5:
time: 156 us; the launch traced here: 154 us
  Pallas kernels  52.5 us (34%)
  local copies, waits for them, and re-layouts  47.8 us (31%)
  starting transfers between devices  33.9 us (22%)
  waiting for transfers between devices  17 us (11%)
  other arithmetic  2.27 us (1%)
    pallas_call x11, Pallas kernels, call(): pl.pallas_call(kernel, grid=grid or (1,), in_specs=in_specs, out_specs=o_...  52.5 us
    unnamed x124, local copies, waits for them, and re-layouts  46.1 us
    ppermute x4, starting transfers between devices, shifted(): return lax.ppermute(block, axis, route)  12.1 us
    all_to_all x2, starting transfers between devices, over_chips(): lax.all_to_all(blocks, 'dom', 0, 0, axis_index_groups=groups, tiled=True)  10.9 us
    all_to_all x2, starting transfers between devices, exchange(): lax.all_to_all(block.reshape(parts, rows // parts, width), 'dom', split_a...  10.5 us
    ppermute x4, waiting for transfers between devices, shifted(): return lax.ppermute(block, axis, route)  10.5 us
    ppermute x2, waiting for transfers between devices, swapped(): return lax.ppermute(block, 'dom', [(i, i ^ bit) for i in range(parts)])  3.55 us
  transfers between devices with their start and end apart: 10, of which 5 were waited for; matrix products, arithmetic and copies ran while one was open for 1% of the time, Pallas kernels for 12%

profile of v5, /device:TPU:13, one launch (start us, length us, event | category | flops | bytes accessed | tf_op | source)
XLA Modules:
  0.0 154.4 jit_solution(2195809109112063963)
XLA Ops:
  0.7 1.2 copy-done
  4.0 3.7 %collective-permute-start = (bf16[256,256]{1,0:T(8,128)(2,1)S(1)}, bf16[256,256]{1,0:T(8,128)(2,1)S(1)}, u32[]{:S(2)}, u32[]{:S(2)}) collective-permute-start(bf16[256,256]{1,0:T(8,128)(2,1)S(1)} %get-tuple-element.45), channel_id=1, source_target_pairs={{0,1},{1,2},{2,3},{3,4},{4,5},{5,6},{6,7},{7,8},{8,9},{9,10},{10,1... | collective-permute-start | bytes 393224 | tf_op jit(solution)/shard_map/ppermute | solution.py:407
  7.7 1.9 %collective-permute-start.1 = (bf16[256,256]{1,0:T(8,128)(2,1)S(1)}, bf16[256,256]{1,0:T(8,128)(2,1)S(1)}, u32[]{:S(2)}, u32[]{:S(2)}) collective-permute-start(bf16[256,256]{1,0:T(8,128)(2,1)S(1)} %get-tuple-element.46), channel_id=1, source_target_pairs={{1,0},{2,1},{3,2},{4,3},{5,4},{6,5},{7,6},{8,7},{9,8},{10,9},{11,1... | collective-permute-start | bytes 393224 | tf_op jit(solution)/shard_map/ppermute | solution.py:407
  10.4 4.5 %collective-permute-done.1.right_ref = bf16[256,256]{1,0:T(8,128)(2,1)S(1)} collective-permute-done((bf16[256,256]{1,0:T(8,128)(2,1)S(1)}, bf16[256,256]{1,0:T(8,128)(2,1)S(1)}, u32[]{:S(2)}, u32[]{:S(2)}) %collective-permute-start.1) | collective-permute-done | bytes 131104 | tf_op jit(solution)/shard_map/ppermute | solution.py:407
  14.9 1.2 copy-done.1
  20.1 17.7 %shard_map.157 = (bf16[8192,256]{1,0:T(8,128)(2,1)S(1)}, bf16[8192,256]{1,0:T(8,128)(2,1)S(1)}, bf16[2048,256]{1,0:T(8,128)(2,1)S(1)}, bf16[2048,256]{1,0:T(8,12...) custom-call(s32[8192]{0:T(1024)S(1)} %copy-done.12, ...), custom_call_target="tpu_custom_call" | custom-call | tf_op jit(solution)/shard_map/pallas_call | solution.py:100
  37.8 2.0 %copy-done.24 = bf16[8192,256]{1,0:T(8,128)(2,1)} copy-done((bf16[8192,256]{1,0:T(8,128)(2,1)}, bf16[8192,256]{1,0:T(8,128)(2,1)S(1)}, u32[]{:S(2)}) %copy-start.24) | copy-done | bytes 4194328
  39.8 2.0 %copy-done.26 = bf16[8192,256]{1,0:T(8,128)(2,1)} copy-done((bf16[8192,256]{1,0:T(8,128)(2,1)}, bf16[8192,256]{1,0:T(8,128)(2,1)S(1)}, u32[]{:S(2)}) %copy-start.26) | copy-done | bytes 4194328
  45.1 5.0 %all-to-all-start = ((bf16[16,32,256]{2,1,0:T(8,128)(2,1)}), bf16[16,32,256]{2,1,0:T(8,128)(2,1)S(1)}, u32[]{:S(2)}, u32[]{:S(2)}) async-start(bf16[16,32,256]{2,1,0:T(8,128)(2,1)} %bitcast.7), calls=%async_computation | async-start | bytes 524288 | tf_op jit(solution)/shard_map/all_to_all | solution.py:416
  52.4 2.0 %shard_map.158 = (f32[2048,256]{1,0:T(8,128)S(1)}, f32[512,256]{1,0:T(8,128)S(1)}, f32[512,256]{1,0:T(8,128)S(1)}) custom-call(bf16[512,256]{1,0:T(8,128)(2,1)S(1)} %copy-done.39, bf16[4,256,256]{2,1,0:T(8,128)(2,1)S(1)} %copy-done.3, f32[2,256]{1,0:T(2,128)S(1)} %copy-done.19, s32[16,128]{1,0:T(8,128)S(1)} %bitcast.23, s32[16,128]{1,0:T(8,128)S(1)} %bitcast.25, ...), custom_call_target="tpu_custom_call" | custom-call | flops 4000000000 | bytes 10000000 | tf_op jit(solution)/shard_map/pallas_call | solution.py:100
  55.2 2.9 %all-to-all-done = bf16[16,32,256]{2,1,0:T(8,128)(2,1)S(1)} async-done(((bf16[16,32,256]{2,1,0:T(8,128)(2,1)}), bf16[16,32,256]{2,1,0:T(8,128)(2,1)S(1)}, u32[]{:S(2)}, u32[]{:S(2)}) %all-to-all-start) | async-done | bytes 262176 | tf_op jit(solution)/shard_map/all_to_all | solution.py:416
  59.1 4.7 %shard_map.159 = (bf16[512,256]{1,0:T(8,128)(2,1)S(1)}, bf16[512,256]{1,0:T(8,128)(2,1)S(1)}, bf16[2048,256]{1,0:T(8,128)(2,1)S(1)}, bf16[512,256]{1,0:T(8,128)(2,1)S(1)}, bf16[512,256]{1,0:T(8,128)(2,1)S(1)}) custom-call(f32[2048,256]{1,0:T(8,128)S(1)} %get-tuple-element.50.z_ref, bf16[512,256]{1,0:T(8,128)(2,1)S(1)} %bitcast.17, ...), custom_call_target="tpu_custom_call" | custom-call | tf_op jit(solution)/shard_map/pallas_call | solution.py:100
  67.6 5.5 %all-to-all-start.1 = ((bf16[16,32,256]{2,1,0:T(8,128)(2,1)}), bf16[16,32,256]{2,1,0:T(8,128)(2,1)S(1)}, u32[]{:S(2)}, u32[]{:S(2)}) async-start(bf16[16,32,256]{2,1,0:T(8,128)(2,1)} %bitcast.20), calls=%async_computation.1 | async-start | bytes 524288 | tf_op jit(solution)/shard_map/all_to_all | solution.py:416
  74.2 1.2 copy-done.35
  83.0 1.2 copy-done.33
  86.2 1.6 %shard_map.161 = (f32[2048,256]{1,0:T(8,128)S(1)}, bf16[2048,256]{1,0:T(8,128)(2,1)S(1)}, bf16[2048,256]{1,0:T(8,128)(2,1)S(1)}) custom-call(bf16[512,256]{1,0:T(8,128)(2,1)S(1)} %copy-done.43, bf16[512,256]{1,0:T(8,128)(2,1)S(1)} %bitcast.19, s32[4,128]{1,0:T(4,128)S(1)} %reshape.62.send_ref, f32[512,256]{1,0:T(8,128)S(1)} %copy-done.59, ...), custom_call_target="tpu_custom_call" | custom-call | flops 6000000000 | bytes 10000000 | tf_op jit(solution)/shard_map/pallas_call | solution.py:100
  88.7 2.4 %copy-done.27 = bf16[8192,256]{1,0:T(8,128)(2,1)S(1)} copy-done((bf16[8192,256]{1,0:T(8,128)(2,1)S(1)}, bf16[8192,256]{1,0:T(8,128)(2,1)}, u32[]{:S(2)}) %copy-start.27) | copy-done | bytes 4194328
  91.4 8.1 %shard_map.162 = (bf16[8192,256]{1,0:T(8,128)(2,1)S(1)}, bf16[2048,256]{1,0:T(8,128)(2,1)S(1)}, bf16[1088,256]{1,0:T(8,128)(2,1)S(1)}, bf16[1088,256]{1,0:T(8,128)(2,1)S(1)}) custom-call(s32[1]{0:T(128)} %bitcast.core_ref, bf16[8192,256]{1,0:T(8,128)(2,1)S(1)} %copy-done.25, bf16[8192,256]{1,0:T(8,128)(2,1)S(1)} %copy-done.27, ...), custom_call_target="tpu_custom_call" | custom-call | flops 15000000512 | bytes 10000000 | tf_op jit(solution)/shard_map/pallas_call | solution.py:100
  99.6 2.0 %copy-done.60 = bf16[8192,256]{1,0:T(8,128)(2,1)} copy-done((bf16[8192,256]{1,0:T(8,128)(2,1)}, bf16[8192,256]{1,0:T(8,128)(2,1)S(1)}, u32[]{:S(2)}) %copy-start.60) | copy-done | bytes 4194328
  101.9 1.6 %collective-permute-done.2 = bf16[1088,256]{1,0:T(8,128)(2,1)S(1)} collective-permute-done((bf16[1088,256]{1,0:T(8,128)(2,1)S(1)}, bf16[1088,256]{1,0:T(8,128)(2,1)S(1)}, u32[]{:S(2)}, u32[]{:S(2)}) %collective-permute-start.2) | collective-permute-done | bytes 557088 | tf_op jit(solution)/shard_map/ppermute | solution.py:411
  104.5 5.5 %all-to-all-start.2 = ((bf16[8,136,256]{2,1,0:T(8,128)(2,1)}), bf16[8,136,256]{2,1,0:T(8,128)(2,1)}, u32[]{:S(2)}, u32[]{:S(2)}) async-start(bf16[8,136,256]{2,1,0:T(8,128)(2,1)} %bitcast.11), calls=%async_computation.2 | async-start | bytes 1114112 | tf_op jit(solution)/shard_map/all_to_all | solution.py:427
  110.0 2.2 %copy-done.61 = bf16[8192,256]{1,0:T(8,128)(2,1)S(1)} copy-done((bf16[8192,256]{1,0:T(8,128)(2,1)S(1)}, bf16[8192,256]{1,0:T(8,128)(2,1)}, u32[]{:S(2)}) %copy-start.61) | copy-done | bytes 4194328
  112.2 12.1 %shard_map.163 = (bf16[2048,256]{1,0:T(8,128)(2,1)S(1)}, bf16[256,256]{1,0:T(8,128)(2,1)S(1)}, bf16[256,256]{1,0:T(8,128)(2,1)S(1)}) custom-call(s32[8192]{0:T(1024)S(1)} %copy-done.13, bf16[8192,256]{1,0:T(8,128)(2,1)S(1)} %copy-done.61), custom_call_target="tpu_custom_call" | custom-call | flops 15000000512 | bytes 10000000 | tf_op jit(solution)/shard_map/pallas_call | solution.py:100
  125.2 1.3 reduce_sum.12
  127.4 5.4 %all-to-all-start.3 = ((bf16[8,136,256]{2,1,0:T(8,128)(2,1)}), bf16[8,136,256]{2,1,0:T(8,128)(2,1)S(1)}, u32[]{:S(2)}, u32[]{:S(2)}) async-start(bf16[8,136,256]{2,1,0:T(8,128)(2,1)} %broadcast_in_dim.2), calls=%async_computation.3 | async-start | bytes 1114112 | tf_op jit(solution)/shard_map/all_to_all | solution.py:427
  132.8 3.4 %collective-permute-start.3 = (bf16[256,256]{1,0:T(8,128)(2,1)S(1)}, bf16[256,256]{1,0:T(8,128)(2,1)S(1)}, u32[]{:S(2)}, u32[]{:S(2)}) collective-permute-start(bf16[256,256]{1,0:T(8,128)(2,1)S(1)} %get-tuple-element.77), channel_id=1, source_target_pairs={{1,0},{2,1},{3,2},{4,3},{5,4},{6,5},{7,6},{8,7},{9,8},{10,9},{11,1... | collective-permute-start | bytes 393224 | tf_op jit(solution)/shard_map/ppermute | solution.py:407
  136.2 3.1 %collective-permute-start.4 = (bf16[256,256]{1,0:T(8,128)(2,1)S(1)}, bf16[256,256]{1,0:T(8,128)(2,1)S(1)}, u32[]{:S(2)}, u32[]{:S(2)}) collective-permute-start(bf16[256,256]{1,0:T(8,128)(2,1)S(1)} %get-tuple-element.78), channel_id=1, source_target_pairs={{0,1},{1,2},{2,3},{3,4},{4,5},{5,6},{6,7},{7,8},{8,9},{9,10},{10,1... | collective-permute-start | bytes 393224 | tf_op jit(solution)/shard_map/ppermute | solution.py:407
  140.5 1.2 copy-done.53
  142.5 6.0 %collective-permute-done.3.from_right_ref = bf16[256,256]{1,0:T(8,128)(2,1)S(1)} collective-permute-done((bf16[256,256]{1,0:T(8,128)(2,1)S(1)}, bf16[256,256]{1,0:T(8,128)(2,1)S(1)}, u32[]{:S(2)}, u32[]{:S(2)}) %collective-permute-start.3) | collective-permute-done | bytes 131104 | tf_op jit(solution)/shard_map/ppermute | solution.py:407
  148.6 2.4 %shard_map.165 = f32[2048,256]{1,0:T(8,128)} custom-call(bf16[2048,256]{1,0:T(8,128)(2,1)S(1)} %copy-done.55, bf16[256,256]{1,0:T(8,128)(2,1)S(1)} %collective-permute-done.3.from_right_ref, bf16[256,256]{1,0:T(8,128)(2,1)S(1)} %collective-permute-done.4.from_left_ref, s32[2,128]{1,0:T(2,128)S(1)} %bitcast.32, s32[2,128]{1,0:T(2,128)S(1)} %bitcast.34, ...), custom_call_target="tpu_custom_call" | custom-call | flops 4000000000 | bytes 10000000 | tf_op jit(solution)/shard_map/pallas_call | solution.py:100
  151.0 2.0 %collective-permute-done.5.ax_ref = bf16[1088,256]{1,0:T(8,128)(2,1)S(1)} collective-permute-done((bf16[1088,256]{1,0:T(8,128)(2,1)S(1)}, bf16[1088,256]{1,0:T(8,128)(2,1)S(1)}, u32[]{:S(2)}, u32[]{:S(2)}) %collective-permute-start.5) | collective-permute-done | bytes 557088 | tf_op jit(solution)/shard_map/ppermute | solution.py:411
  153.0 1.5 shard_map.166
  (127 shorter events, 34.9 us)
Async XLA Ops:
  0.6 49.5 %copy-start.19 = (f32[2,256]{1,0:T(2,128)S(1)}, f32[2,256]{1,0:T(2,128)}, u32[]{:S(2)}) copy-start(f32[2,256]{1,0:T(2,128)} %b_ref.3) | copy-start | bytes 6148
  3.2 46.9 %copy-start.3 = (bf16[4,256,256]{2,1,0:T(8,128)(2,1)S(1)}, bf16[4,256,256]{2,1,0:T(8,128)(2,1)}, u32[]{:S(2)}) copy-start(bf16[4,256,256]{2,1,0:T(8,128)(2,1)} %wc_ref.1) | copy-start | bytes 1572868
  3.2 46.9 %copy-start.14 = (s32[2048]{0:T(1024)S(1)}, s32[2048]{0:T(1024)}, u32[]{:S(2)}) copy-start(s32[2048]{0:T(1024)} %param.23) | copy-start | bytes 24580
  3.2 46.9 %copy-start.15 = (s32[2048]{0:T(1024)S(1)}, s32[2048]{0:T(1024)}, u32[]{:S(2)}) copy-start(s32[2048]{0:T(1024)} %param.24) | copy-start | bytes 24580
  3.2 46.9 %copy-start.17 = (s32[2048]{0:T(1024)S(1)}, s32[2048]{0:T(1024)}, u32[]{:S(2)}) copy-start(s32[2048]{0:T(1024)} %param.22) | copy-start | bytes 24580
  4.0 6.4 %collective-permute-start = (bf16[256,256]{1,0:T(8,128)(2,1)S(1)}, bf16[256,256]{1,0:T(8,128)(2,1)S(1)}, u32[]{:S(2)}, u32[]{:S(2)}) collective-permute-start(bf16[256,256]{1,0:T(8,128)(2,1)S(1)} %get-tuple-element.45), channel_id=1, source_target_pairs={{0,1},{1,2},{2,3},{3,4},{4,5},{5,6},{6,7},{7,8},{8,9},{9,10},{10,1... | collective-permute-start | bytes 393224 | tf_op jit(solution)/shard_map/ppermute | solution.py:407
  7.7 7.2 %collective-permute-start.1 = (bf16[256,256]{1,0:T(8,128)(2,1)S(1)}, bf16[256,256]{1,0:T(8,128)(2,1)S(1)}, u32[]{:S(2)}, u32[]{:S(2)}) collective-permute-start(bf16[256,256]{1,0:T(8,128)(2,1)S(1)} %get-tuple-element.46), channel_id=1, source_target_pairs={{1,0},{2,1},{3,2},{4,3},{5,4},{6,5},{7,6},{8,7},{9,8},{10,9},{11,1... | collective-permute-start | bytes 393224 | tf_op jit(solution)/shard_map/ppermute | solution.py:407
  39.8 2.0 %copy-start.26 = (bf16[8192,256]{1,0:T(8,128)(2,1)}, bf16[8192,256]{1,0:T(8,128)(2,1)S(1)}, u32[]{:S(2)}) copy-start(bf16[8192,256]{1,0:T(8,128)(2,1)S(1)} %get-tuple-element.48.he_ref) | copy-start | bytes 12582916
  45.1 12.9 %all-to-all-start = ((bf16[16,32,256]{2,1,0:T(8,128)(2,1)}), bf16[16,32,256]{2,1,0:T(8,128)(2,1)S(1)}, u32[]{:S(2)}, u32[]{:S(2)}) async-start(bf16[16,32,256]{2,1,0:T(8,128)(2,1)} %bitcast.7), calls=%async_computation | async-start | bytes 524288 | tf_op jit(solution)/shard_map/all_to_all | solution.py:416
  67.6 14.1 %all-to-all-start.1 = ((bf16[16,32,256]{2,1,0:T(8,128)(2,1)}), bf16[16,32,256]{2,1,0:T(8,128)(2,1)S(1)}, u32[]{:S(2)}, u32[]{:S(2)}) async-start(bf16[16,32,256]{2,1,0:T(8,128)(2,1)} %bitcast.20), calls=%async_computation.1 | async-start | bytes 524288 | tf_op jit(solution)/shard_map/all_to_all | solution.py:416
  79.2 2.5 %copy-start.7 = (bf16[4,256,256]{2,1,0:T(8,128)(2,1)S(1)}, bf16[4,256,256]{2,1,0:T(8,128)(2,1)}, u32[]{:S(2)}) copy-start(bf16[4,256,256]{2,1,0:T(8,128)(2,1)} %w_ref.13) | copy-start | bytes 1572868
  79.2 2.5 %copy-start.37 = (f32[512,128]{1,0:T(8,128)S(1)}, f32[512,128]{1,0:T(8,128)}, u32[]{:S(2)}) copy-start(f32[512,128]{1,0:T(8,128)} %copy-done.36) | copy-start | bytes 786436
  86.2 2.5 %copy-start.25 = (bf16[8192,256]{1,0:T(8,128)(2,1)S(1)}, bf16[8192,256]{1,0:T(8,128)(2,1)}, u32[]{:S(2)}) copy-start(bf16[8192,256]{1,0:T(8,128)(2,1)} %copy-done.24) | copy-start | bytes 12582916
  86.2 4.9 %copy-start.27 = (bf16[8192,256]{1,0:T(8,128)(2,1)S(1)}, bf16[8192,256]{1,0:T(8,128)(2,1)}, u32[]{:S(2)}) copy-start(bf16[8192,256]{1,0:T(8,128)(2,1)} %copy-done.26) | copy-start | bytes 12582916
  86.2 5.1 %copy-start.31 = (bf16[2048,256]{1,0:T(8,128)(2,1)S(1)}, bf16[2048,256]{1,0:T(8,128)(2,1)}, u32[]{:S(2)}) copy-start(bf16[2048,256]{1,0:T(8,128)(2,1)} %copy-done.30) | copy-start | bytes 3145732
  86.2 5.2 %copy-start.57 = (bf16[1024,256]{1,0:T(8,128)(2,1)S(1)}, bf16[1024,256]{1,0:T(8,128)(2,1)}, u32[]{:S(2)}) copy-start(bf16[1024,256]{1,0:T(8,128)(2,1)} %copy-done.56) | copy-start | bytes 1572868
  87.8 11.7 %copy-start.48 = (f32[2048,256]{1,0:T(8,128)}, f32[2048,256]{1,0:T(8,128)S(1)}, u32[]{:S(2)}) copy-start(f32[2048,256]{1,0:T(8,128)S(1)} %get-tuple-element.80.g_ref) | copy-start | bytes 6291460
  87.8 11.7 %copy-start.50 = (bf16[2048,256]{1,0:T(8,128)(2,1)}, bf16[2048,256]{1,0:T(8,128)(2,1)S(1)}, u32[]{:S(2)}) copy-start(bf16[2048,256]{1,0:T(8,128)(2,1)S(1)} %get-tuple-element.66.du_ref) | copy-start | bytes 3145732
  99.6 2.0 %copy-start.60 = (bf16[8192,256]{1,0:T(8,128)(2,1)}, bf16[8192,256]{1,0:T(8,128)(2,1)S(1)}, u32[]{:S(2)}) copy-start(bf16[8192,256]{1,0:T(8,128)(2,1)S(1)} %get-tuple-element.71.dz_ref) | copy-start | bytes 12582916
  101.5 3.0 %copy-start.52 = (bf16[2048,256]{1,0:T(8,128)(2,1)}, bf16[2048,256]{1,0:T(8,128)(2,1)S(1)}, u32[]{:S(2)}) copy-start(bf16[2048,256]{1,0:T(8,128)(2,1)S(1)} %get-tuple-element.79.dq_ref) | copy-start | bytes 3145732
  101.6 8.4 %copy-start.13 = (s32[8192]{0:T(1024)S(1)}, s32[8192]{0:T(1024)}, u32[]{:S(2)}) copy-start(s32[8192]{0:T(1024)} %src_ref.3) | copy-start | bytes 98308
  101.6 2.0 %collective-permute-start.2 = (bf16[1088,256]{1,0:T(8,128)(2,1)S(1)}, bf16[1088,256]{1,0:T(8,128)(2,1)S(1)}, u32[]{:S(2)}, u32[]{:S(2)}) collective-permute-start(bf16[1088,256]{1,0:T(8,128)(2,1)S(1)} %get-tuple-element.68), channel_id=1, source_target_pairs={{0,1},{1,0},{2,3},{3,2},{4,5},{5,4},{6,7},{7,6},{8,9},{9,8},{10,11... | collective-permute-start | bytes 1671176 | tf_op jit(solution)/shard_map/ppermute | solution.py:411
  104.5 20.7 %all-to-all-start.2 = ((bf16[8,136,256]{2,1,0:T(8,128)(2,1)}), bf16[8,136,256]{2,1,0:T(8,128)(2,1)}, u32[]{:S(2)}, u32[]{:S(2)}) async-start(bf16[8,136,256]{2,1,0:T(8,128)(2,1)} %bitcast.11), calls=%async_computation.2 | async-start | bytes 1114112 | tf_op jit(solution)/shard_map/all_to_all | solution.py:427
  110.0 2.2 %copy-start.61 = (bf16[8192,256]{1,0:T(8,128)(2,1)S(1)}, bf16[8192,256]{1,0:T(8,128)(2,1)}, u32[]{:S(2)}) copy-start(bf16[8192,256]{1,0:T(8,128)(2,1)} %copy-done.60) | copy-start | bytes 12582916
  125.2 14.1 %copy-start.49 = (f32[2048,256]{1,0:T(8,128)S(1)}, f32[2048,256]{1,0:T(8,128)}, u32[]{:S(2)}) copy-start(f32[2048,256]{1,0:T(8,128)} %copy-done.48) | copy-start | bytes 6291460
  127.4 23.6 %all-to-all-start.3 = ((bf16[8,136,256]{2,1,0:T(8,128)(2,1)}), bf16[8,136,256]{2,1,0:T(8,128)(2,1)S(1)}, u32[]{:S(2)}, u32[]{:S(2)}) async-start(bf16[8,136,256]{2,1,0:T(8,128)(2,1)} %broadcast_in_dim.2), calls=%async_computation.3 | async-start | bytes 1114112 | tf_op jit(solution)/shard_map/all_to_all | solution.py:427
  132.8 15.7 %collective-permute-start.3 = (bf16[256,256]{1,0:T(8,128)(2,1)S(1)}, bf16[256,256]{1,0:T(8,128)(2,1)S(1)}, u32[]{:S(2)}, u32[]{:S(2)}) collective-permute-start(bf16[256,256]{1,0:T(8,128)(2,1)S(1)} %get-tuple-element.77), channel_id=1, source_target_pairs={{1,0},{2,1},{3,2},{4,3},{5,4},{6,5},{7,6},{8,7},{9,8},{10,9},{11,1... | collective-permute-start | bytes 393224 | tf_op jit(solution)/shard_map/ppermute | solution.py:407
  136.2 12.3 %collective-permute-start.4 = (bf16[256,256]{1,0:T(8,128)(2,1)S(1)}, bf16[256,256]{1,0:T(8,128)(2,1)S(1)}, u32[]{:S(2)}, u32[]{:S(2)}) collective-permute-start(bf16[256,256]{1,0:T(8,128)(2,1)S(1)} %get-tuple-element.78), channel_id=1, source_target_pairs={{0,1},{1,2},{2,3},{3,4},{4,5},{5,6},{6,7},{7,8},{8,9},{9,10},{10,1... | collective-permute-start | bytes 393224 | tf_op jit(solution)/shard_map/ppermute | solution.py:407
  141.8 6.8 %copy-start.21 = (s32[256]{0:T(256)S(1)}, s32[256]{0:T(256)}, u32[]{:S(2)}) copy-start(s32[256]{0:T(256)} %param.21) | copy-start | bytes 3076
  141.8 6.8 %copy-start.23 = (s32[256]{0:T(256)S(1)}, s32[256]{0:T(256)}, u32[]{:S(2)}) copy-start(s32[256]{0:T(256)} %param.20) | copy-start | bytes 3076
  141.8 6.8 %copy-start.55 = (bf16[2048,256]{1,0:T(8,128)(2,1)S(1)}, bf16[2048,256]{1,0:T(8,128)(2,1)}, u32[]{:S(2)}) copy-start(bf16[2048,256]{1,0:T(8,128)(2,1)} %copy-done.54) | copy-start | bytes 3145732
  151.0 2.0 %collective-permute-start.5 = (bf16[1088,256]{1,0:T(8,128)(2,1)S(1)}, bf16[1088,256]{1,0:T(8,128)(2,1)S(1)}, u32[]{:S(2)}, u32[]{:S(2)}) collective-permute-start(bf16[1088,256]{1,0:T(8,128)(2,1)S(1)} %bitcast.15), channel_id=1, source_target_pairs={{0,1},{1,0},{2,3},{3,2},{4,5},{5,4},{6,7},{7,6},{8,9},{9,8},{10,11... | collective-permute-start | bytes 1671176 | tf_op jit(solution)/shard_map/ppermute | solution.py:411
  (40 other events, 39.8 us)

commit v6 on v5

--- a/solution.py
+++ b/solution.py
@@ -87,13 +87,20 @@
     return pl.ds(pl.multiple_of(index * 2, 2), 2)
 
 
-def call(kernel, outs, args, grid=(), specs=None, out_specs=None, scratch=(), cost=(0, 0)):
+def call(kernel, outs, args, grid=(), specs=None, out_specs=None, scratch=(), us=1.0, near=(), near_out=()):
+    specs = specs or {}
+    args = [
+        a
+        if k in near or getattr(specs.get(k), "memory_space", None) == pltpu.SMEM
+        else pltpu.with_memory_space_constraint(a, pltpu.HBM)
+        for k, a in enumerate(args)
+    ]
     def whole(a):
         return pl.BlockSpec(a.shape, lambda *_: (0,) * len(a.shape))
 
     in_specs = [whole(a) for a in args]
     o_specs = [whole(o) for o in outs]
-    for k, s in (specs or {}).items():
+    for k, s in specs.items():
         in_specs[k] = s
     for k, s in (out_specs or {}).items():
         o_specs[k] = s
@@ -102,11 +109,11 @@
         grid=grid or (1,),
         in_specs=in_specs,
         out_specs=o_specs,
-        out_shape=outs,
+        out_shape=[o if k in near_out else pltpu.HBM(o.shape, o.dtype) for k, o in enumerate(outs)],
         scratch_shapes=list(scratch),
         compiler_params=pltpu.CompilerParams(vmem_limit_bytes=24 << 20),
         cost_estimate=pl.CostEstimate(
-            flops=int(cost[0]), bytes_accessed=int(cost[1]), transcendentals=0
+            flops=int(us * 1e9), bytes_accessed=1 << 20, transcendentals=0
         ),
     )(*args)
 
@@ -452,7 +459,8 @@
     steps = tiles // group
 
     to_right, to_left = call(
-        halo_kernel, [sds((halo, width), bf)] * 2, [features, right, left]
+        halo_kernel, [sds((halo, width), bf)] * 2, [features, right, left],
+        us=0.8, near_out=(0, 1),
     )
     h_left = shifted(to_right, "dom", 1)
     h_right = shifted(to_left, "dom", -1)
@@ -479,6 +487,7 @@
             pltpu.VMEM((ext_pairs, LANES), f32),
             pltpu.VMEM((2 * FINE_UNROLL * edges, LANES), f32),
         ],
+        us=18, near=(1, 2), near_out=(5,),
     )
     incoming = exchange(outgoing, parts).reshape(crows, width)
     cedges = coarse_src.shape[0]
@@ -486,7 +495,7 @@
         part(coarse_own_kernel, per),
         [sds((cedges, width), f32), sds((coarse, width), f32), sds((coarse, width), f32)],
         [pooled, w_coarse, bias, csrc, cdst, pool, cotangent],
-        cost=(4e9, 10e6),
+        us=2, near_out=(1, 2),
     )
     own_c, back_c, dz_c, du_c, agg_c = call(
         part(coarse_kernel, per),
@@ -499,19 +508,20 @@
         ],
         [zc, incoming, ghc, uc, w_coarse, csrc, cdst],
         scratch=[pltpu.VMEM((cedges, width), f32)],
+        us=4.7, near=(1, 2, 3), near_out=(1,),
     )
     returned = exchange(back_c, parts).reshape(crows, width)
     gw_c, gb_c, part_c = call(
         part(coarse_grad_kernel, per),
         [sds((4 * width, width), bf), sds((8, width), f32), sds((coarse, width), f32)],
         [pooled, incoming, ghc, w_coarse, cdst, own_c, back_c, dz_c, du_c, agg_c],
-        cost=(4e9, 10e6),
+        us=1, near=(1, 2), near_out=(1,),
     )
     g, du, dagg = call(
         node_back_kernel,
         [sds((nodes, width), f32), sds((nodes, width), bf), sds((nodes, width), bf)],
         [own_c, returned, csend, part_c, w_coarse, count, pool, cotangent, dsu, w_fine],
-        cost=(6e9, 10e6),
+        us=1.6, near=(1,), near_out=(2,),
     )
     half_rows = 4 * width + 64
     dz, dq, mine, other = call(
@@ -527,7 +537,7 @@
         specs={0: smem, 1: edge_tile, 2: edge_tile},
         out_specs={0: edge_tile},
         scratch=[pltpu.VMEM((8, width), f32), pltpu.VMEM((width, width), f32)],
-        cost=(15e9, 10e6),
+        us=8, near=(3,), near_out=(2, 3),
     )
     sums = add(mine, swapped(other, parts, 1)).reshape(chips, -1, width)
     sums, dz = lax.optimization_barrier((sums, dz))
@@ -540,7 +550,7 @@
         specs={0: smem, 1: edge_tile},
         scratch=[pltpu.VMEM((2 * edges, LANES), f32)]
         + [pltpu.VMEM((ext_pairs, LANES), f32)] * 6,
-        cost=(15e9, 10e6),
+        us=12, near_out=(1, 2),
     )
     sums, own_f, gl, gr = lax.optimization_barrier((sums, own_f, gl, gr))
     sums = jnp.sum(sums.astype(f32), axis=0).astype(bf)
@@ -548,13 +558,14 @@
     from_right = shifted(gl, "dom", -1)
     from_left = shifted(gr, "dom", 1)
     (part_f,) = call(
-        part_kernel, [sds((nodes, width), f32)], [dq, du, g, w_fine], cost=(4e9, 10e6)
+        part_kernel, [sds((nodes, width), f32)], [dq, du, g, w_fine],
+        us=0.8, near_out=(0,),
     )
     (grad_input,) = call(
         input_kernel,
         [sds((nodes, width), f32)],
         [own_f, from_right, from_left, right, left, part_f, w_fine],
-        cost=(4e9, 10e6),
+        us=2.4, near=(1, 2, 5), near_out=(0,),
     )
     sums, grad_input = lax.optimization_barrier((sums, grad_input))
     sums = sums.reshape(half_rows, width)
@@ -564,6 +575,7 @@
         [sds((4 * width, width), f32), sds((4 * width, width), f32), sds((2, width), f32)],
         [core, sums, swapped(sums, parts, 1)],
         specs={0: smem},
+        us=1.5, near=(1, 2), near_out=(0, 1, 2),
     )
     shape = (4, width, width)
     return (grad_input, grad_fine.reshape(shape), grad_coarse.reshape(shape), grad_bias)

time: 156 us -> 138 us (0.88)
  local copies, waits for them, and re-layouts: 47.8 us -> 2.1 us
  Pallas kernels: 52.5 us -> 76.7 us
  waiting for transfers between devices: 17 us -> 21.8 us
    unnamed x124 -> x6, local copies, waits for them, and re-layouts: 46.1 us -> 0.6 us
    pallas_call x11, Pallas kernels: 52.5 us -> 76.7 us  [call(): pl.pallas_call(kernel, grid=grid or (1,), in_specs=in_specs, out_specs=o_...]
    all_to_all x2, waiting for transfers between devices: 2.93 us -> 7.28 us  [exchange(): lax.all_to_all(block.reshape(parts, rows // parts, width), 'dom', split_a...]
  transfers between devices with their start and end apart: 10 -> 10, of which waited for: 5 -> 6; matrix products, arithmetic and copies ran while one was open for 1% -> 0% of each run, Pallas kernels for 12% -> 21%
where the time goes in v6:
time: 138 us; the launch traced here: 136 us
  Pallas kernels  76.7 us (56%)
  starting transfers between devices  34.2 us (25%)
  waiting for transfers between devices  21.8 us (16%)
  local copies, waits for them, and re-layouts  2.1 us (2%)
    pallas_call x11, Pallas kernels, call(): pl.pallas_call(kernel, grid=grid or (1,), in_specs=in_specs, out_specs=o_...  76.7 us
    ppermute x4, starting transfers between devices, shifted(): return lax.ppermute(block, axis, route)  12.1 us
    all_to_all x2, starting transfers between devices, over_chips(): lax.all_to_all(blocks, 'dom', 0, 0, axis_index_groups=groups, tiled=True)  11.2 us
    ppermute x4, waiting for transfers between devices, shifted(): return lax.ppermute(block, axis, route)  10.8 us
    all_to_all x2, starting transfers between devices, exchange(): lax.all_to_all(block.reshape(parts, rows // parts, width), 'dom', split_a...  10.7 us
    all_to_all x2, waiting for transfers between devices, exchange(): lax.all_to_all(block.reshape(parts, rows // parts, width), 'dom', split_a...  7.28 us
    ppermute x2, waiting for transfers between devices, swapped(): return lax.ppermute(block, 'dom', [(i, i ^ bit) for i in range(parts)])  3.71 us
  transfers between devices with their start and end apart: 10, of which 6 were waited for; matrix products, arithmetic and copies ran while one was open for 0% of the time, Pallas kernels for 21%

profile of v6, /device:TPU:13, one launch (start us, length us, event | category | flops | bytes accessed | tf_op | source)
XLA Modules:
  0.0 136.5 jit_solution(9148305944673107531)
XLA Ops:
  0.7 2.0 %shard_map.156 = (bf16[256,256]{1,0:T(8,128)(2,1)S(1)}, bf16[256,256]{1,0:T(8,128)(2,1)S(1)}) custom-call(bf16[2048,256]{1,0:T(8,128)(2,1)} %h_ref.5, s32[2,128]{1,0:T(2,128)} %bitcast.30, s32[2,128]{1,0:T(2,128)} %bitcast.32), custom_call_target="tpu_custom_call" | custom-call | flops 800000000 | bytes 1048576 | tf_op jit(solution)/shard_map/pallas_call | solution.py:107
  2.7 3.7 %collective-permute-start = (bf16[256,256]{1,0:T(8,128)(2,1)S(1)}, bf16[256,256]{1,0:T(8,128)(2,1)S(1)}, u32[]{:S(2)}, u32[]{:S(2)}) collective-permute-start(bf16[256,256]{1,0:T(8,128)(2,1)S(1)} %get-tuple-element.45), channel_id=1, source_target_pairs={{0,1},{1,2},{2,3},{3,4},{4,5},{5,6},{6,7},{7,8},{8,9},{9,10},{10,1... | collective-permute-start | bytes 393224 | tf_op jit(solution)/shard_map/ppermute | solution.py:414
  6.4 1.9 %collective-permute-start.1 = (bf16[256,256]{1,0:T(8,128)(2,1)S(1)}, bf16[256,256]{1,0:T(8,128)(2,1)S(1)}, u32[]{:S(2)}, u32[]{:S(2)}) collective-permute-start(bf16[256,256]{1,0:T(8,128)(2,1)S(1)} %get-tuple-element.46), channel_id=1, source_target_pairs={{1,0},{2,1},{3,2},{4,3},{5,4},{6,5},{7,6},{8,7},{9,8},{10,9},{11,1... | collective-permute-start | bytes 393224 | tf_op jit(solution)/shard_map/ppermute | solution.py:414
  8.3 0.7 reshape.62.send_ref
  9.0 4.6 %collective-permute-done.1.right_ref = bf16[256,256]{1,0:T(8,128)(2,1)S(1)} collective-permute-done((bf16[256,256]{1,0:T(8,128)(2,1)S(1)}, bf16[256,256]{1,0:T(8,128)(2,1)S(1)}, u32[]{:S(2)}, u32[]{:S(2)}) %collective-permute-start.1) | collective-permute-done | bytes 131104 | tf_op jit(solution)/shard_map/ppermute | solution.py:414
  13.6 19.7 %shard_map.157 = (bf16[8192,256]{1,0:T(8,128)(2,1)}, bf16[8192,256]{1,0:T(8,128)(2,1)}, bf16[2048,256]{1,0:T(8,128)(2,1)}, bf16[2048,256]{1,0:T(8,128)(2,1)}, bf...) custom-call(s32[8192]{0:T(1024)S(1)} %copy-done, ...), custom_call_target="tpu_custom_call" | custom-call | flops 17999998976 | bytes 1048576 | tf_op jit(solution)/shard_map/pallas_call | solution.py:107
  33.3 5.0 %all-to-all-start = ((bf16[16,32,256]{2,1,0:T(8,128)(2,1)}), bf16[16,32,256]{2,1,0:T(8,128)(2,1)S(1)}, u32[]{:S(2)}, u32[]{:S(2)}) async-start(bf16[16,32,256]{2,1,0:T(8,128)(2,1)} %bitcast.7), calls=%async_computation | async-start | bytes 524288 | tf_op jit(solution)/shard_map/all_to_all | solution.py:423
  38.3 4.6 %shard_map.158 = (f32[2048,256]{1,0:T(8,128)}, f32[512,256]{1,0:T(8,128)S(1)}, f32[512,256]{1,0:T(8,128)S(1)}) custom-call(bf16[512,256]{1,0:T(8,128)(2,1)} %get-tuple-element.49.pooled_ref, bf16[4,256,256]{2,1,0:T(8,128)(2,1)} %wc_ref.1, f32[2,256]{1,0:T(2,128)} %b_ref.3, s32[16,128]{1,0:T(8,128)} %bitcast.22, s32[16,128]{1,0:T(8,128)} %bitcast.24, ...), custom_call_target="tpu_custom_call" | custom-call | flops 2000000000 | bytes 1048576 | tf_op jit(solution)/shard_map/pallas_call | solution.py:107
  42.8 3.4 %all-to-all-done = bf16[16,32,256]{2,1,0:T(8,128)(2,1)S(1)} async-done(((bf16[16,32,256]{2,1,0:T(8,128)(2,1)}), bf16[16,32,256]{2,1,0:T(8,128)(2,1)S(1)}, u32[]{:S(2)}, u32[]{:S(2)}) %all-to-all-start) | async-done | bytes 262176 | tf_op jit(solution)/shard_map/all_to_all | solution.py:423
  46.2 7.6 %shard_map.159 = (bf16[512,256]{1,0:T(8,128)(2,1)}, bf16[512,256]{1,0:T(8,128)(2,1)}, bf16[2048,256]{1,0:T(8,128)(2,1)}, bf16[512,256]{1,0:T(8,128)(2,1)}, bf16[512,256]{1,0:T(8,128)(2,1)}) custom-call(f32[2048,256]{1,0:T(8,128)} %get-tuple-element.50.z_ref, bf16[512,256]{1,0:T(8,128)(2,1)S(1)} %bitcast.17, f32[512,256]{1,0:T(8,128)S(1)} %get-tuple-element.52.ghc_ref, ...), custom_call_target="tpu_custom_call" | custom-call | flops 4700000256 | bytes 1048576 | tf_op jit(solution)/shard_map/pallas_call | solution.py:107
  53.9 5.7 %all-to-all-start.1 = ((bf16[16,32,256]{2,1,0:T(8,128)(2,1)}), bf16[16,32,256]{2,1,0:T(8,128)(2,1)S(1)}, u32[]{:S(2)}, u32[]{:S(2)}) async-start(bf16[16,32,256]{2,1,0:T(8,128)(2,1)} %bitcast.9), calls=%async_computation.1 | async-start | bytes 524288 | tf_op jit(solution)/shard_map/all_to_all | solution.py:423
  59.6 3.5 %shard_map.160 = (bf16[1024,256]{1,0:T(8,128)(2,1)}, f32[8,256]{1,0:T(8,128)S(1)}, f32[512,256]{1,0:T(8,128)}) custom-call(bf16[512,256]{1,0:T(8,128)(2,1)} %get-tuple-element.49.pooled_ref, bf16[512,256]{1,0:T(8,128)(2,1)S(1)} %bitcast.18, f32[512,256]{1,0:T(8,128)S(1)} %get-tuple-element.52.ghc_ref, bf16[4,256,256]{2,1,0:T(8,128)(2,1)} %wc_ref.1, ...), custom_call_target="tpu_custom_call" | custom-call | flops 1000000000 | bytes 1048576 | tf_op jit(solution)/shard_map/pallas_call | solution.py:107
  63.1 0.6 copy-done.1
  63.7 3.9 %all-to-all-done.1 = bf16[16,32,256]{2,1,0:T(8,128)(2,1)S(1)} async-done(((bf16[16,32,256]{2,1,0:T(8,128)(2,1)}), bf16[16,32,256]{2,1,0:T(8,128)(2,1)S(1)}, u32[]{:S(2)}, u32[]{:S(2)}) %all-to-all-start.1) | async-done | bytes 262176 | tf_op jit(solution)/shard_map/all_to_all | solution.py:423
  67.6 5.4 %shard_map.161 = (f32[2048,256]{1,0:T(8,128)}, bf16[2048,256]{1,0:T(8,128)(2,1)}, bf16[2048,256]{1,0:T(8,128)(2,1)S(1)}) custom-call(bf16[512,256]{1,0:T(8,128)(2,1)} %get-tuple-element.54.own_ref, bf16[512,256]{1,0:T(8,128)(2,1)S(1)} %bitcast.19, s32[4,128]{1,0:T(4,128)} %reshape.62.send_ref, f32[512,256]{1,0:T(8,128)} %get-tuple-element.59.part_ref, ...), custom_call_target="tpu_custom_call" | custom-call | flops 1600000000 | bytes 1048576 | tf_op jit(solution)/shard_map/pallas_call | solution.py:107
  73.0 12.3 %shard_map.162 = (bf16[8192,256]{1,0:T(8,128)(2,1)}, bf16[2048,256]{1,0:T(8,128)(2,1)}, bf16[1088,256]{1,0:T(8,128)(2,1)S(1)}, bf16[1088,256]{1,0:T(8,128)(2,1)S(1)}) custom-call(s32[1]{0:T(128)} %bitcast.core_ref, bf16[8192,256]{1,0:T(8,128)(2,1)} %get-tuple-element.47.d_ref, bf16[8192,256]{1,0:T(8,128)(2,1)} %get-tuple-element.48.he_ref, ...), custom_call_target="tpu_custom_call" | custom-call | flops 8000000000 | bytes 1048576 | tf_op jit(solution)/shard_map/pallas_call | solution.py:107
  85.3 0.2 collective-permute-start.2
  85.5 1.8 %collective-permute-done.2 = bf16[1088,256]{1,0:T(8,128)(2,1)S(1)} collective-permute-done((bf16[1088,256]{1,0:T(8,128)(2,1)S(1)}, bf16[1088,256]{1,0:T(8,128)(2,1)S(1)}, u32[]{:S(2)}, u32[]{:S(2)}) %collective-permute-start.2) | collective-permute-done | bytes 557088 | tf_op jit(solution)/shard_map/ppermute | solution.py:418
  87.3 1.0 add_convert_fusion
  88.2 5.4 %all-to-all-start.2 = ((bf16[8,136,256]{2,1,0:T(8,128)(2,1)}), bf16[8,136,256]{2,1,0:T(8,128)(2,1)S(1)}, u32[]{:S(2)}, u32[]{:S(2)}) async-start(bf16[8,136,256]{2,1,0:T(8,128)(2,1)} %bitcast.11), calls=%async_computation.2 | async-start | bytes 1114112 | tf_op jit(solution)/shard_map/all_to_all | solution.py:434
  93.6 13.2 %shard_map.163 = (bf16[2048,256]{1,0:T(8,128)(2,1)}, bf16[256,256]{1,0:T(8,128)(2,1)S(1)}, bf16[256,256]{1,0:T(8,128)(2,1)S(1)}) custom-call(s32[8192]{0:T(1024)S(1)} %copy-done, bf16[8192,256]{1,0:T(8,128)(2,1)} %get-tuple-element.71.dz_ref), custom_call_target="tpu_custom_call" | custom-call | flops 12000000000 | bytes 1048576 | tf_op jit(solution)/shard_map/pallas_call | solution.py:107
  106.8 0.0 all-to-all-done.2
  106.8 0.1 reduce_sum.12
  106.9 0.8 broadcast_in_dim.2
  107.8 5.8 %all-to-all-start.3 = ((bf16[8,136,256]{2,1,0:T(8,128)(2,1)}), bf16[8,136,256]{2,1,0:T(8,128)(2,1)S(1)}, u32[]{:S(2)}, u32[]{:S(2)}) async-start(bf16[8,136,256]{2,1,0:T(8,128)(2,1)} %broadcast_in_dim.2), calls=%async_computation.3 | async-start | bytes 1114112 | tf_op jit(solution)/shard_map/all_to_all | solution.py:434
  113.6 2.9 %collective-permute-start.3 = (bf16[256,256]{1,0:T(8,128)(2,1)S(1)}, bf16[256,256]{1,0:T(8,128)(2,1)S(1)}, u32[]{:S(2)}, u32[]{:S(2)}) collective-permute-start(bf16[256,256]{1,0:T(8,128)(2,1)S(1)} %get-tuple-element.77), channel_id=1, source_target_pairs={{1,0},{2,1},{3,2},{4,3},{5,4},{6,5},{7,6},{8,7},{9,8},{10,9},{11,1... | collective-permute-start | bytes 393224 | tf_op jit(solution)/shard_map/ppermute | solution.py:414
  116.5 3.5 %collective-permute-start.4 = (bf16[256,256]{1,0:T(8,128)(2,1)S(1)}, bf16[256,256]{1,0:T(8,128)(2,1)S(1)}, u32[]{:S(2)}, u32[]{:S(2)}) collective-permute-start(bf16[256,256]{1,0:T(8,128)(2,1)S(1)} %get-tuple-element.78), channel_id=1, source_target_pairs={{0,1},{1,2},{2,3},{3,4},{4,5},{5,6},{6,7},{7,8},{8,9},{9,10},{10,1... | collective-permute-start | bytes 393224 | tf_op jit(solution)/shard_map/ppermute | solution.py:414
  120.0 3.0 %shard_map.164.part_ref = f32[2048,256]{1,0:T(8,128)S(1)} custom-call(bf16[2048,256]{1,0:T(8,128)(2,1)} %get-tuple-element.79.dq_ref, bf16[2048,256]{1,0:T(8,128)(2,1)} %get-tuple-element.66.du_ref, f32[2048,256]{1,0:T(8,128)} %get-tuple-element.80.g_ref, bf16[4,256,256]{2,1,0:T(8,128)(2,1)} %w_ref.13), custom_call_target="tpu_custom_call" | custom-call | flops 800000000 | bytes 1048576 | tf_op jit(solution)/shard_map/pallas_call | solution.py:107
  123.1 6.2 %collective-permute-done.3.from_right_ref = bf16[256,256]{1,0:T(8,128)(2,1)S(1)} collective-permute-done((bf16[256,256]{1,0:T(8,128)(2,1)S(1)}, bf16[256,256]{1,0:T(8,128)(2,1)S(1)}, u32[]{:S(2)}, u32[]{:S(2)}) %collective-permute-start.3) | collective-permute-done | bytes 131104 | tf_op jit(solution)/shard_map/ppermute | solution.py:414
  129.3 3.8 %shard_map.165 = f32[2048,256]{1,0:T(8,128)} custom-call(bf16[2048,256]{1,0:T(8,128)(2,1)} %get-tuple-element.76.own_ref, bf16[256,256]{1,0:T(8,128)(2,1)S(1)} %collective-permute-done.3.from_right_ref, bf16[256,256]{1,0:T(8,128)(2,1)S(1)} %collective-permute-done.4.from_left_ref, s32[2,128]{1,0:T(2,128)} %bitcast.31, s32[2,128]{1,0:T(2,128)} %bitcast.33, ...), custom_call_target="tpu_custom_call" | custom-call | flops 2400000000 | bytes 1048576 | tf_op jit(solution)/shard_map/pallas_call | solution.py:107
  133.1 2.0 %collective-permute-done.5.ax_ref = bf16[1088,256]{1,0:T(8,128)(2,1)S(1)} collective-permute-done((bf16[1088,256]{1,0:T(8,128)(2,1)S(1)}, bf16[1088,256]{1,0:T(8,128)(2,1)S(1)}, u32[]{:S(2)}, u32[]{:S(2)}) %collective-permute-start.5) | collective-permute-done | bytes 557088 | tf_op jit(solution)/shard_map/ppermute | solution.py:418
  135.0 1.5 %shard_map.166 = (f32[1024,256]{1,0:T(8,128)}, f32[1024,256]{1,0:T(8,128)}, f32[2,256]{1,0:T(2,128)}) custom-call(s32[1]{0:T(128)} %bitcast.core_ref, bf16[1088,256]{1,0:T(8,128)(2,1)S(1)} %bitcast.16, bf16[1088,256]{1,0:T(8,128)(2,1)S(1)} %collective-permute-done.5.ax_ref), custom_call_target="tpu_custom_call" | custom-call | flops 1500000000 | bytes 1048576 | tf_op jit(solution)/shard_map/pallas_call | solution.py:107
  (9 shorter events, 0.0 us)
Async XLA Ops:
  0.6 7.7 %copy-start.2 = (s32[16,32]{1,0:T(8,128)S(1)}, s32[16,32]{1,0:T(8,128)}, u32[]{:S(2)}) copy-start(s32[16,32]{1,0:T(8,128)} %param.25) | copy-start | bytes 6148
  0.6 12.9 %copy-start = (s32[8192]{0:T(1024)S(1)}, s32[8192]{0:T(1024)}, u32[]{:S(2)}) copy-start(s32[8192]{0:T(1024)} %src_ref.3) | copy-start | bytes 98308
  2.7 6.3 %collective-permute-start = (bf16[256,256]{1,0:T(8,128)(2,1)S(1)}, bf16[256,256]{1,0:T(8,128)(2,1)S(1)}, u32[]{:S(2)}, u32[]{:S(2)}) collective-permute-start(bf16[256,256]{1,0:T(8,128)(2,1)S(1)} %get-tuple-element.45), channel_id=1, source_target_pairs={{0,1},{1,2},{2,3},{3,4},{4,5},{5,6},{6,7},{7,8},{8,9},{9,10},{10,1... | collective-permute-start | bytes 393224 | tf_op jit(solution)/shard_map/ppermute | solution.py:414
  6.4 7.2 %collective-permute-start.1 = (bf16[256,256]{1,0:T(8,128)(2,1)S(1)}, bf16[256,256]{1,0:T(8,128)(2,1)S(1)}, u32[]{:S(2)}, u32[]{:S(2)}) collective-permute-start(bf16[256,256]{1,0:T(8,128)(2,1)S(1)} %get-tuple-element.46), channel_id=1, source_target_pairs={{1,0},{2,1},{3,2},{4,3},{5,4},{6,5},{7,6},{8,7},{9,8},{10,9},{11,1... | collective-permute-start | bytes 393224 | tf_op jit(solution)/shard_map/ppermute | solution.py:414
  33.3 13.0 %all-to-all-start = ((bf16[16,32,256]{2,1,0:T(8,128)(2,1)}), bf16[16,32,256]{2,1,0:T(8,128)(2,1)S(1)}, u32[]{:S(2)}, u32[]{:S(2)}) async-start(bf16[16,32,256]{2,1,0:T(8,128)(2,1)} %bitcast.7), calls=%async_computation | async-start | bytes 524288 | tf_op jit(solution)/shard_map/all_to_all | solution.py:423
  53.9 13.7 %all-to-all-start.1 = ((bf16[16,32,256]{2,1,0:T(8,128)(2,1)}), bf16[16,32,256]{2,1,0:T(8,128)(2,1)S(1)}, u32[]{:S(2)}, u32[]{:S(2)}) async-start(bf16[16,32,256]{2,1,0:T(8,128)(2,1)} %bitcast.9), calls=%async_computation.1 | async-start | bytes 524288 | tf_op jit(solution)/shard_map/all_to_all | solution.py:423
  63.1 0.6 copy-start.1
  85.3 2.0 %collective-permute-start.2 = (bf16[1088,256]{1,0:T(8,128)(2,1)S(1)}, bf16[1088,256]{1,0:T(8,128)(2,1)S(1)}, u32[]{:S(2)}, u32[]{:S(2)}) collective-permute-start(bf16[1088,256]{1,0:T(8,128)(2,1)S(1)} %get-tuple-element.68), channel_id=1, source_target_pairs={{0,1},{1,0},{2,3},{3,2},{4,5},{5,4},{6,7},{7,6},{8,9},{9,8},{10,11... | collective-permute-start | bytes 1671176 | tf_op jit(solution)/shard_map/ppermute | solution.py:418
  88.2 18.6 %all-to-all-start.2 = ((bf16[8,136,256]{2,1,0:T(8,128)(2,1)}), bf16[8,136,256]{2,1,0:T(8,128)(2,1)S(1)}, u32[]{:S(2)}, u32[]{:S(2)}) async-start(bf16[8,136,256]{2,1,0:T(8,128)(2,1)} %bitcast.11), calls=%async_computation.2 | async-start | bytes 1114112 | tf_op jit(solution)/shard_map/all_to_all | solution.py:434
  107.8 25.3 %all-to-all-start.3 = ((bf16[8,136,256]{2,1,0:T(8,128)(2,1)}), bf16[8,136,256]{2,1,0:T(8,128)(2,1)S(1)}, u32[]{:S(2)}, u32[]{:S(2)}) async-start(bf16[8,136,256]{2,1,0:T(8,128)(2,1)} %broadcast_in_dim.2), calls=%async_computation.3 | async-start | bytes 1114112 | tf_op jit(solution)/shard_map/all_to_all | solution.py:434
  113.6 15.7 %collective-permute-start.3 = (bf16[256,256]{1,0:T(8,128)(2,1)S(1)}, bf16[256,256]{1,0:T(8,128)(2,1)S(1)}, u32[]{:S(2)}, u32[]{:S(2)}) collective-permute-start(bf16[256,256]{1,0:T(8,128)(2,1)S(1)} %get-tuple-element.77), channel_id=1, source_target_pairs={{1,0},{2,1},{3,2},{4,3},{5,4},{6,5},{7,6},{8,7},{9,8},{10,9},{11,1... | collective-permute-start | bytes 393224 | tf_op jit(solution)/shard_map/ppermute | solution.py:414
  116.5 12.7 %collective-permute-start.4 = (bf16[256,256]{1,0:T(8,128)(2,1)S(1)}, bf16[256,256]{1,0:T(8,128)(2,1)S(1)}, u32[]{:S(2)}, u32[]{:S(2)}) collective-permute-start(bf16[256,256]{1,0:T(8,128)(2,1)S(1)} %get-tuple-element.78), channel_id=1, source_target_pairs={{0,1},{1,2},{2,3},{3,4},{4,5},{5,6},{6,7},{7,8},{8,9},{9,10},{10,1... | collective-permute-start | bytes 393224 | tf_op jit(solution)/shard_map/ppermute | solution.py:414
  133.1 2.0 %collective-permute-start.5 = (bf16[1088,256]{1,0:T(8,128)(2,1)S(1)}, bf16[1088,256]{1,0:T(8,128)(2,1)S(1)}, u32[]{:S(2)}, u32[]{:S(2)}) collective-permute-start(bf16[1088,256]{1,0:T(8,128)(2,1)S(1)} %bitcast.15), channel_id=1, source_target_pairs={{0,1},{1,0},{2,3},{3,2},{4,5},{5,4},{6,7},{7,6},{8,9},{9,8},{10,11... | collective-permute-start | bytes 1671176 | tf_op jit(solution)/shard_map/ppermute | solution.py:418

commit v7 on v6

--- a/solution.py
+++ b/solution.py
@@ -111,7 +111,7 @@
         out_specs=o_specs,
         out_shape=[o if k in near_out else pltpu.HBM(o.shape, o.dtype) for k, o in enumerate(outs)],
         scratch_shapes=list(scratch),
-        compiler_params=pltpu.CompilerParams(vmem_limit_bytes=24 << 20),
+        compiler_params=pltpu.CompilerParams(vmem_limit_bytes=32 << 20),
         cost_estimate=pl.CostEstimate(
             flops=int(us * 1e9), bytes_accessed=1 << 20, transcendentals=0
         ),
@@ -277,43 +277,44 @@
     part_ref[...] = ghc_ref[...] + mm_nt(du, w_ref[3]) + mm_nt(dq, w_ref[1])
 
 
-def node_back_kernel(
-    own_ref, ret_ref, send_ref, part_ref, wc_ref, count_ref, pool_ref, cot_ref, dsu_ref, w_ref,
-    g_ref, du_ref, dagg_ref,
-):
-    coarse = own_ref.shape[0]
-    sends = hot_rows(row_form(send_ref, 0, send_ref.shape[0]), coarse)
-    dp = (own_ref[...].astype(f32) + mm(sends, ret_ref[...])).astype(bf)
-    dc = part_ref[...] + mm_nt(dp, wc_ref[0])
-    count = count_ref[...]
-    dcs = (dc / jnp.concatenate([count, count], axis=1)).astype(bf)
-    hot = hot_rows(row_form(pool_ref, 0, pool_ref.shape[0]), coarse)
-    g = cot_ref[...].astype(f32) + mm_tn(hot, dcs)
-    g_ref[...] = g
-    du = (g * dsu_ref[...].astype(f32)).astype(bf)
-    du_ref[...] = du
-    dagg_ref[...] = mm_nt(du, w_ref[2]).astype(bf)
-
-
-def edge_back_kernel(
-    per, group, core_ref, d_ref, he_ref, dagg_ref, h_ref, dst_ref, gwc_ref, gbc_ref, agg_ref, du_ref,
-    dz_ref, dq_ref, mine_ref, other_ref, gb, gw0,
+def fine_back_kernel(
+    per, group, core_ref, own_ref, ret_ref, send_ref, part_ref, wc_ref, count_ref, pool_ref,
+    cot_ref, dsu_ref, w_ref, d_ref, he_ref, dst_ref, gwc_ref, gbc_ref, h_hbm, agg_hbm,
+    dz_ref, dq_ref, du_ref, dcs_ref, mine_ref, other_ref, gb, gw0, dagg, h_ref, agg_ref, sems,
 ):
     step = pl.program_id(0)
     width = h_ref.shape[1]
     edges = per * LANES
+    copies = [
+        pltpu.make_async_copy(h_hbm, h_ref, sems.at[0]),
+        pltpu.make_async_copy(agg_hbm, agg_ref, sems.at[1]),
+    ]
 
     @pl.when(step == 0)
     def _():
+        for copy in copies:
+            copy.start()
         gb[...] = jnp.zeros_like(gb)
         gw0[...] = jnp.zeros_like(gw0)
+        coarse = own_ref.shape[0]
+        sends = hot_rows(row_form(send_ref, 0, send_ref.shape[0]), coarse)
+        dp = (own_ref[...].astype(f32) + mm(sends, ret_ref[...])).astype(bf)
+        dc = part_ref[...] + mm_nt(dp, wc_ref[0])
+        count = count_ref[...]
+        dcs = (dc / jnp.concatenate([count, count], axis=1)).astype(bf)
+        dcs_ref[...] = dcs
+        hot = hot_rows(row_form(pool_ref, 0, pool_ref.shape[0]), coarse)
+        g = cot_ref[...].astype(f32) + mm_tn(hot, dcs)
+        du = (g * dsu_ref[...].astype(f32)).astype(bf)
+        du_ref[...] = du
+        dagg[...] = mm_nt(du, w_ref[0]).astype(bf)
 
     def tile(k, slot):
         t = step * group + k
         hot = hot_rows(row_form(dst_ref, t * per, per), TILE)
         rows = tile_rows(t, TILE)
         here = tile_rows(k, edges)
-        gm = mm_tn(hot, dagg_ref[rows, :])
+        gm = mm_tn(hot, dagg[rows, :])
         dz = (gm * d_ref[here, :].astype(f32)).astype(bf)
         dz_ref[here, :] = dz
         dq = mm(hot, dz)
@@ -325,6 +326,8 @@
 
     @pl.when(step == pl.num_programs(0) - 1)
     def _():
+        for copy in copies:
+            copy.wait()
         gbf = jnp.broadcast_to(gb[0:1, :], (16, width)).astype(bf)
         gbc = jnp.broadcast_to(gbc_ref[0:1, :], (16, width)).astype(bf)
         h = h_ref[...]
@@ -370,9 +373,13 @@
         gr_ref[...] = summed(nodes + halo, halo)
 
 
-def part_kernel(dq_ref, du_ref, g_ref, w_ref, part_ref):
+def part_kernel(dq_ref, du_ref, cot_ref, dcs_ref, pool_ref, w3_ref, w1_ref, part_ref):
+    hot = hot_rows(row_form(pool_ref, 0, pool_ref.shape[0]), dcs_ref.shape[0])
     part_ref[...] = (
-        g_ref[...] + mm_nt(du_ref[...], w_ref[3]) + mm_nt(dq_ref[...], w_ref[1])
+        cot_ref[...].astype(f32)
+        + mm_tn(hot, dcs_ref[...])
+        + mm_nt(du_ref[...], w3_ref[0])
+        + mm_nt(dq_ref[...], w1_ref[0])
     )
 
 
@@ -466,6 +473,10 @@
     h_right = shifted(to_left, "dom", -1)
     edge_tile = pl.BlockSpec((group * edges, width), lambda t: (t, 0))
     smem = pl.BlockSpec(memory_space=pltpu.SMEM)
+
+    def weight(k):
+        return pl.BlockSpec((1, width, width), lambda *_: (k, 0, 0))
+
     ext_pairs = 2 * (nodes + 2 * halo)
     d_edge, he, agg, dsu, pooled, outgoing, count = call(
         part(fine_kernel, per, group),
@@ -517,27 +528,36 @@
         [pooled, incoming, ghc, w_coarse, cdst, own_c, back_c, dz_c, du_c, agg_c],
         us=1, near=(1, 2), near_out=(1,),
     )
-    g, du, dagg = call(
-        node_back_kernel,
-        [sds((nodes, width), f32), sds((nodes, width), bf), sds((nodes, width), bf)],
-        [own_c, returned, csend, part_c, w_coarse, count, pool, cotangent, dsu, w_fine],
-        us=1.6, near=(1,), near_out=(2,),
-    )
     half_rows = 4 * width + 64
-    dz, dq, mine, other = call(
-        part(edge_back_kernel, per, group),
+    dz, dq, du, dcs, mine, other = call(
+        part(fine_back_kernel, per, group),
         [
             sds((tiles * edges, width), bf),
             sds((nodes, width), bf),
+            sds((nodes, width), bf),
+            sds((coarse, width), bf),
             sds((half_rows, width), bf),
             sds((half_rows, width), bf),
         ],
-        [core, d_edge, he, dagg, features, fdst, gw_c, gb_c, agg, du],
+        [
+            core, own_c, returned, csend, part_c, w_coarse, count, pool, cotangent, dsu, w_fine,
+            d_edge, he, fdst, gw_c, gb_c, features, agg,
+        ],
         grid=(steps,),
-        specs={0: smem, 1: edge_tile, 2: edge_tile},
+        specs={
+            0: smem, 5: weight(0), 10: weight(2), 11: edge_tile, 12: edge_tile,
+            16: pl.BlockSpec(memory_space=pltpu.HBM), 17: pl.BlockSpec(memory_space=pltpu.HBM),
+        },
         out_specs={0: edge_tile},
-        scratch=[pltpu.VMEM((8, width), f32), pltpu.VMEM((width, width), f32)],
-        us=8, near=(3,), near_out=(2, 3),
+        scratch=[
+            pltpu.VMEM((8, width), f32),
+            pltpu.VMEM((width, width), f32),
+            pltpu.VMEM((nodes, width), bf),
+            pltpu.VMEM((nodes, width), bf),
+            pltpu.VMEM((nodes, width), bf),
+            pltpu.SemaphoreType.DMA((2,)),
+        ],
+        us=10, near=(2, 8, 9), near_out=(4, 5),
     )
     sums = add(mine, swapped(other, parts, 1)).reshape(chips, -1, width)
     sums, dz = lax.optimization_barrier((sums, dz))
@@ -558,13 +578,17 @@
     from_right = shifted(gl, "dom", -1)
     from_left = shifted(gr, "dom", 1)
     (part_f,) = call(
-        part_kernel, [sds((nodes, width), f32)], [dq, du, g, w_fine],
-        us=0.8, near_out=(0,),
+        part_kernel,
+        [sds((nodes, width), f32)],
+        [dq, du, cotangent, dcs, pool, w_fine, w_fine],
+        specs={5: weight(3), 6: weight(1)},
+        us=1.5, near_out=(0,),
     )
     (grad_input,) = call(
         input_kernel,
         [sds((nodes, width), f32)],
         [own_f, from_right, from_left, right, left, part_f, w_fine],
+        specs={6: weight(0)},
         us=2.4, near=(1, 2, 5), near_out=(0,),
     )
     sums, grad_input = lax.optimization_barrier((sums, grad_input))

time: 138 us -> 134 us (0.971)
  Pallas kernels: 76.7 us -> 73 us
    pallas_call x11 -> x10, Pallas kernels: 76.7 us -> 73 us  [call(): pl.pallas_call(kernel, grid=grid or (1,), in_specs=in_specs, out_specs=o_...]
where the time goes in v7:
time: 134 us; the launch traced here: 133 us
  Pallas kernels  73 us (54%)
  starting transfers between devices  34.3 us (26%)
  waiting for transfers between devices  21.4 us (16%)
  local copies, waits for them, and re-layouts  2.11 us (2%)
    pallas_call x10, Pallas kernels, call(): pl.pallas_call(kernel, grid=grid or (1,), in_specs=in_specs, out_specs=o_...  73 us
    ppermute x4, starting transfers between devices, shifted(): return lax.ppermute(block, axis, route)  12.1 us
    all_to_all x2, starting transfers between devices, over_chips(): lax.all_to_all(blocks, 'dom', 0, 0, axis_index_groups=groups, tiled=True)  11.1 us
    all_to_all x2, starting transfers between devices, exchange(): lax.all_to_all(block.reshape(parts, rows // parts, width), 'dom', split_a...  10.9 us
    ppermute x4, waiting for transfers between devices, shifted(): return lax.ppermute(block, axis, route)  10.5 us
    all_to_all x2, waiting for transfers between devices, exchange(): lax.all_to_all(block.reshape(parts, rows // parts, width), 'dom', split_a...  7.19 us
    ppermute x2, waiting for transfers between devices, swapped(): return lax.ppermute(block, 'dom', [(i, i ^ bit) for i in range(parts)])  3.72 us
  transfers between devices with their start and end apart: 10, of which 6 were waited for; matrix products, arithmetic and copies ran while one was open for 0% of the time, Pallas kernels for 21%

profile of v7, /device:TPU:13, one launch (start us, length us, event | category | flops | bytes accessed | tf_op | source)
XLA Modules:
  0.0 132.7 jit_solution(11656332696592091166)
XLA Ops:
  0.7 2.0 %shard_map.156 = (bf16[256,256]{1,0:T(8,128)(2,1)S(1)}, bf16[256,256]{1,0:T(8,128)(2,1)S(1)}) custom-call(bf16[2048,256]{1,0:T(8,128)(2,1)} %h_hbm.1, s32[2,128]{1,0:T(2,128)} %bitcast.31, s32[2,128]{1,0:T(2,128)} %bitcast.33), custom_call_target="tpu_custom_call" | custom-call | flops 800000000 | bytes 1048576 | tf_op jit(solution)/shard_map/pallas_call | solution.py:107
  2.7 3.7 %collective-permute-start = (bf16[256,256]{1,0:T(8,128)(2,1)S(1)}, bf16[256,256]{1,0:T(8,128)(2,1)S(1)}, u32[]{:S(2)}, u32[]{:S(2)}) collective-permute-start(bf16[256,256]{1,0:T(8,128)(2,1)S(1)} %get-tuple-element.44), channel_id=1, source_target_pairs={{0,1},{1,2},{2,3},{3,4},{4,5},{5,6},{6,7},{7,8},{8,9},{9,10},{10,1... | collective-permute-start | bytes 393224 | tf_op jit(solution)/shard_map/ppermute | solution.py:421
  6.4 1.9 %collective-permute-start.1 = (bf16[256,256]{1,0:T(8,128)(2,1)S(1)}, bf16[256,256]{1,0:T(8,128)(2,1)S(1)}, u32[]{:S(2)}, u32[]{:S(2)}) collective-permute-start(bf16[256,256]{1,0:T(8,128)(2,1)S(1)} %get-tuple-element.45), channel_id=1, source_target_pairs={{1,0},{2,1},{3,2},{4,3},{5,4},{6,5},{7,6},{8,7},{9,8},{10,9},{11,1... | collective-permute-start | bytes 393224 | tf_op jit(solution)/shard_map/ppermute | solution.py:421
  8.3 0.7 reshape.62.send_ref
  9.0 0.0 collective-permute-done.left_ref
  9.0 4.6 %collective-permute-done.1.right_ref = bf16[256,256]{1,0:T(8,128)(2,1)S(1)} collective-permute-done((bf16[256,256]{1,0:T(8,128)(2,1)S(1)}, bf16[256,256]{1,0:T(8,128)(2,1)S(1)}, u32[]{:S(2)}, u32[]{:S(2)}) %collective-permute-start.1) | collective-permute-done | bytes 131104 | tf_op jit(solution)/shard_map/ppermute | solution.py:421
  13.6 19.7 %shard_map.157 = (bf16[8192,256]{1,0:T(8,128)(2,1)}, bf16[8192,256]{1,0:T(8,128)(2,1)}, bf16[2048,256]{1,0:T(8,128)(2,1)}, bf16[2048,256]{1,0:T(8,128)(2,1)}, bf...) custom-call(s32[8192]{0:T(1024)S(1)} %copy-done.1, ...), custom_call_target="tpu_custom_call" | custom-call | flops 17999998976 | bytes 1048576 | tf_op jit(solution)/shard_map/pallas_call | solution.py:107
  33.3 5.0 %all-to-all-start = ((bf16[16,32,256]{2,1,0:T(8,128)(2,1)}), bf16[16,32,256]{2,1,0:T(8,128)(2,1)S(1)}, u32[]{:S(2)}, u32[]{:S(2)}) async-start(bf16[16,32,256]{2,1,0:T(8,128)(2,1)} %bitcast.7), calls=%async_computation | async-start | bytes 524288 | tf_op jit(solution)/shard_map/all_to_all | solution.py:430
  38.3 4.6 %shard_map.158 = (f32[2048,256]{1,0:T(8,128)}, f32[512,256]{1,0:T(8,128)S(1)}, f32[512,256]{1,0:T(8,128)S(1)}) custom-call(bf16[512,256]{1,0:T(8,128)(2,1)} %get-tuple-element.46.pooled_ref, bf16[4,256,256]{2,1,0:T(8,128)(2,1)} %wc_ref.1, f32[2,256]{1,0:T(2,128)} %b_ref.3, s32[16,128]{1,0:T(8,128)} %bitcast.26, s32[16,128]{1,0:T(8,128)} %bitcast.28, ...), custom_call_target="tpu_custom_call" | custom-call | flops 2000000000 | bytes 1048576 | tf_op jit(solution)/shard_map/pallas_call | solution.py:107
  42.9 3.4 %all-to-all-done = bf16[16,32,256]{2,1,0:T(8,128)(2,1)S(1)} async-done(((bf16[16,32,256]{2,1,0:T(8,128)(2,1)}), bf16[16,32,256]{2,1,0:T(8,128)(2,1)S(1)}, u32[]{:S(2)}, u32[]{:S(2)}) %all-to-all-start) | async-done | bytes 262176 | tf_op jit(solution)/shard_map/all_to_all | solution.py:430
  46.2 7.6 %shard_map.159 = (bf16[512,256]{1,0:T(8,128)(2,1)}, bf16[512,256]{1,0:T(8,128)(2,1)}, bf16[2048,256]{1,0:T(8,128)(2,1)}, bf16[512,256]{1,0:T(8,128)(2,1)}, bf16[512,256]{1,0:T(8,128)(2,1)}) custom-call(f32[2048,256]{1,0:T(8,128)} %get-tuple-element.47.z_ref, bf16[512,256]{1,0:T(8,128)(2,1)S(1)} %bitcast.18, f32[512,256]{1,0:T(8,128)S(1)} %get-tuple-element.49.ghc_ref, ...), custom_call_target="tpu_custom_call" | custom-call | flops 4700000256 | bytes 1048576 | tf_op jit(solution)/shard_map/pallas_call | solution.py:107
  53.9 5.9 %all-to-all-start.1 = ((bf16[16,32,256]{2,1,0:T(8,128)(2,1)}), bf16[16,32,256]{2,1,0:T(8,128)(2,1)S(1)}, u32[]{:S(2)}, u32[]{:S(2)}) async-start(bf16[16,32,256]{2,1,0:T(8,128)(2,1)} %bitcast.9), calls=%async_computation.1 | async-start | bytes 524288 | tf_op jit(solution)/shard_map/all_to_all | solution.py:430
  59.7 3.6 %shard_map.160 = (bf16[1024,256]{1,0:T(8,128)(2,1)}, f32[8,256]{1,0:T(8,128)S(1)}, f32[512,256]{1,0:T(8,128)}) custom-call(bf16[512,256]{1,0:T(8,128)(2,1)} %get-tuple-element.46.pooled_ref, bf16[512,256]{1,0:T(8,128)(2,1)S(1)} %bitcast.19, f32[512,256]{1,0:T(8,128)S(1)} %get-tuple-element.49.ghc_ref, bf16[4,256,256]{2,1,0:T(8,128)(2,1)} %wc_ref.1, ...), custom_call_target="tpu_custom_call" | custom-call | flops 1000000000 | bytes 1048576 | tf_op jit(solution)/shard_map/pallas_call | solution.py:107
  63.3 0.6 copy-done.2
  63.9 3.8 %all-to-all-done.1 = bf16[16,32,256]{2,1,0:T(8,128)(2,1)S(1)} async-done(((bf16[16,32,256]{2,1,0:T(8,128)(2,1)}), bf16[16,32,256]{2,1,0:T(8,128)(2,1)S(1)}, u32[]{:S(2)}, u32[]{:S(2)}) %all-to-all-start.1) | async-done | bytes 262176 | tf_op jit(solution)/shard_map/all_to_all | solution.py:430
  67.7 13.9 %shard_map.161 = (bf16[8192,256]{1,0:T(8,128)(2,1)}, bf16[2048,256]{1,0:T(8,128)(2,1)}, bf16[2048,256]{1,0:T(8,128)(2,1)}, bf16[512,256]{1,0:T(8,128)(2,1)}, bf1...) custom-call(s32[1]{0:T(128)} %bitcast.core_ref, bf16[512,256]{1,0:T(8,128)(2,1)} %get-tuple-element.51.own_ref, ...), custom_call_target="tpu_custom_call" | custom-call | flops 10000000000 | bytes 1048576 | tf_op jit(solution)/shard_map/pallas_call | solution.py:107
  81.6 0.3 collective-permute-start.2
  81.9 1.8 %collective-permute-done.2 = bf16[1088,256]{1,0:T(8,128)(2,1)S(1)} collective-permute-done((bf16[1088,256]{1,0:T(8,128)(2,1)S(1)}, bf16[1088,256]{1,0:T(8,128)(2,1)S(1)}, u32[]{:S(2)}, u32[]{:S(2)}) %collective-permute-start.2) | collective-permute-done | bytes 557088 | tf_op jit(solution)/shard_map/ppermute | solution.py:425
  83.6 1.0 add_convert_fusion
  84.6 5.4 %all-to-all-start.2 = ((bf16[8,136,256]{2,1,0:T(8,128)(2,1)}), bf16[8,136,256]{2,1,0:T(8,128)(2,1)S(1)}, u32[]{:S(2)}, u32[]{:S(2)}) async-start(bf16[8,136,256]{2,1,0:T(8,128)(2,1)} %bitcast.11), calls=%async_computation.2 | async-start | bytes 1114112 | tf_op jit(solution)/shard_map/all_to_all | solution.py:441
  90.0 13.2 %shard_map.162 = (bf16[2048,256]{1,0:T(8,128)(2,1)}, bf16[256,256]{1,0:T(8,128)(2,1)S(1)}, bf16[256,256]{1,0:T(8,128)(2,1)S(1)}) custom-call(s32[8192]{0:T(1024)S(1)} %copy-done.1, bf16[8192,256]{1,0:T(8,128)(2,1)} %get-tuple-element.68.dz_ref), custom_call_target="tpu_custom_call" | custom-call | flops 12000000000 | bytes 1048576 | tf_op jit(solution)/shard_map/pallas_call | solution.py:107
  103.2 0.0 all-to-all-done.2
  103.2 0.1 reduce_sum.12
  103.3 0.8 broadcast_in_dim.2
  104.1 5.8 %all-to-all-start.3 = ((bf16[8,136,256]{2,1,0:T(8,128)(2,1)}), bf16[8,136,256]{2,1,0:T(8,128)(2,1)S(1)}, u32[]{:S(2)}, u32[]{:S(2)}) async-start(bf16[8,136,256]{2,1,0:T(8,128)(2,1)} %broadcast_in_dim.2), calls=%async_computation.3 | async-start | bytes 1114112 | tf_op jit(solution)/shard_map/all_to_all | solution.py:441
  109.9 2.9 %collective-permute-start.3 = (bf16[256,256]{1,0:T(8,128)(2,1)S(1)}, bf16[256,256]{1,0:T(8,128)(2,1)S(1)}, u32[]{:S(2)}, u32[]{:S(2)}) collective-permute-start(bf16[256,256]{1,0:T(8,128)(2,1)S(1)} %get-tuple-element.74), channel_id=1, source_target_pairs={{1,0},{2,1},{3,2},{4,3},{5,4},{6,5},{7,6},{8,7},{9,8},{10,9},{11,1... | collective-permute-start | bytes 393224 | tf_op jit(solution)/shard_map/ppermute | solution.py:421
  112.8 3.5 %collective-permute-start.4 = (bf16[256,256]{1,0:T(8,128)(2,1)S(1)}, bf16[256,256]{1,0:T(8,128)(2,1)S(1)}, u32[]{:S(2)}, u32[]{:S(2)}) collective-permute-start(bf16[256,256]{1,0:T(8,128)(2,1)S(1)} %get-tuple-element.75), channel_id=1, source_target_pairs={{0,1},{1,2},{2,3},{3,4},{4,5},{5,6},{6,7},{7,8},{8,9},{9,10},{10,1... | collective-permute-start | bytes 393224 | tf_op jit(solution)/shard_map/ppermute | solution.py:421
  116.4 3.3 %shard_map.163.part_ref = f32[2048,256]{1,0:T(8,128)S(1)} custom-call(bf16[2048,256]{1,0:T(8,128)(2,1)} %get-tuple-element.76.dq_ref, bf16[2048,256]{1,0:T(8,128)(2,1)} %get-tuple-element.77.du_ref, bf16[2048,256]{1,0:T(8,128)(2,1)} %cot_ref.5, bf16[512,256]{1,0:T(8,128)(2,1)} %get-tuple-element.78.dcs_ref, s32[16,128]{1,0:T(8,128)} %bitcast.23, ...), custom_call_target="tpu_custom_call" | custom-call | flops 1500000000 | bytes 1048576 | tf_op jit(solution)/shard_map/pallas_call | solution.py:107
  119.7 5.9 %collective-permute-done.3.from_right_ref = bf16[256,256]{1,0:T(8,128)(2,1)S(1)} collective-permute-done((bf16[256,256]{1,0:T(8,128)(2,1)S(1)}, bf16[256,256]{1,0:T(8,128)(2,1)S(1)}, u32[]{:S(2)}, u32[]{:S(2)}) %collective-permute-start.3) | collective-permute-done | bytes 131104 | tf_op jit(solution)/shard_map/ppermute | solution.py:421
  125.6 3.7 %shard_map.164 = f32[2048,256]{1,0:T(8,128)} custom-call(bf16[2048,256]{1,0:T(8,128)(2,1)} %get-tuple-element.73.own_ref, bf16[256,256]{1,0:T(8,128)(2,1)S(1)} %collective-permute-done.3.from_right_ref, bf16[256,256]{1,0:T(8,128)(2,1)S(1)} %collective-permute-done.4.from_left_ref, s32[2,128]{1,0:T(2,128)} %bitcast.32, s32[2,128]{1,0:T(2,128)} %bitcast.34, ...), custom_call_target="tpu_custom_call" | custom-call | flops 2400000000 | bytes 1048576 | tf_op jit(solution)/shard_map/pallas_call | solution.py:107
  129.3 2.0 %collective-permute-done.5.ax_ref = bf16[1088,256]{1,0:T(8,128)(2,1)S(1)} collective-permute-done((bf16[1088,256]{1,0:T(8,128)(2,1)S(1)}, bf16[1088,256]{1,0:T(8,128)(2,1)S(1)}, u32[]{:S(2)}, u32[]{:S(2)}) %collective-permute-start.5) | collective-permute-done | bytes 557088 | tf_op jit(solution)/shard_map/ppermute | solution.py:425
  131.2 1.5 %shard_map.165 = (f32[1024,256]{1,0:T(8,128)}, f32[1024,256]{1,0:T(8,128)}, f32[2,256]{1,0:T(2,128)}) custom-call(s32[1]{0:T(128)} %bitcast.core_ref, bf16[1088,256]{1,0:T(8,128)(2,1)S(1)} %bitcast.16, bf16[1088,256]{1,0:T(8,128)(2,1)S(1)} %collective-permute-done.5.ax_ref), custom_call_target="tpu_custom_call" | custom-call | flops 1500000000 | bytes 1048576 | tf_op jit(solution)/shard_map/pallas_call | solution.py:107
  (12 shorter events, 0.0 us)
Async XLA Ops:
  0.6 7.7 %copy-start.4 = (s32[16,32]{1,0:T(8,128)S(1)}, s32[16,32]{1,0:T(8,128)}, u32[]{:S(2)}) copy-start(s32[16,32]{1,0:T(8,128)} %param.25) | copy-start | bytes 6148
  0.6 12.9 %copy-start.1 = (s32[8192]{0:T(1024)S(1)}, s32[8192]{0:T(1024)}, u32[]{:S(2)}) copy-start(s32[8192]{0:T(1024)} %src_ref.3) | copy-start | bytes 98308
  2.7 6.3 %collective-permute-start = (bf16[256,256]{1,0:T(8,128)(2,1)S(1)}, bf16[256,256]{1,0:T(8,128)(2,1)S(1)}, u32[]{:S(2)}, u32[]{:S(2)}) collective-permute-start(bf16[256,256]{1,0:T(8,128)(2,1)S(1)} %get-tuple-element.44), channel_id=1, source_target_pairs={{0,1},{1,2},{2,3},{3,4},{4,5},{5,6},{6,7},{7,8},{8,9},{9,10},{10,1... | collective-permute-start | bytes 393224 | tf_op jit(solution)/shard_map/ppermute | solution.py:421
  6.4 7.2 %collective-permute-start.1 = (bf16[256,256]{1,0:T(8,128)(2,1)S(1)}, bf16[256,256]{1,0:T(8,128)(2,1)S(1)}, u32[]{:S(2)}, u32[]{:S(2)}) collective-permute-start(bf16[256,256]{1,0:T(8,128)(2,1)S(1)} %get-tuple-element.45), channel_id=1, source_target_pairs={{1,0},{2,1},{3,2},{4,3},{5,4},{6,5},{7,6},{8,7},{9,8},{10,9},{11,1... | collective-permute-start | bytes 393224 | tf_op jit(solution)/shard_map/ppermute | solution.py:421
  33.3 12.9 %all-to-all-start = ((bf16[16,32,256]{2,1,0:T(8,128)(2,1)}), bf16[16,32,256]{2,1,0:T(8,128)(2,1)S(1)}, u32[]{:S(2)}, u32[]{:S(2)}) async-start(bf16[16,32,256]{2,1,0:T(8,128)(2,1)} %bitcast.7), calls=%async_computation | async-start | bytes 524288 | tf_op jit(solution)/shard_map/all_to_all | solution.py:430
  53.9 13.8 %copy-start = (bf16[2048,256]{1,0:T(8,128)(2,1)S(1)}, bf16[2048,256]{1,0:T(8,128)(2,1)}, u32[]{:S(2)}) copy-start(bf16[2048,256]{1,0:T(8,128)(2,1)} %cot_ref.5) | copy-start | bytes 3145732
  53.9 13.9 %copy-start.3 = (bf16[2048,256]{1,0:T(8,128)(2,1)S(1)}, bf16[2048,256]{1,0:T(8,128)(2,1)}, u32[]{:S(2)}) copy-start(bf16[2048,256]{1,0:T(8,128)(2,1)} %get-tuple-element.58.dsu_ref) | copy-start | bytes 3145732
  53.9 13.8 %all-to-all-start.1 = ((bf16[16,32,256]{2,1,0:T(8,128)(2,1)}), bf16[16,32,256]{2,1,0:T(8,128)(2,1)S(1)}, u32[]{:S(2)}, u32[]{:S(2)}) async-start(bf16[16,32,256]{2,1,0:T(8,128)(2,1)} %bitcast.9), calls=%async_computation.1 | async-start | bytes 524288 | tf_op jit(solution)/shard_map/all_to_all | solution.py:430
  63.3 0.6 copy-start.2
  81.6 2.0 %collective-permute-start.2 = (bf16[1088,256]{1,0:T(8,128)(2,1)S(1)}, bf16[1088,256]{1,0:T(8,128)(2,1)S(1)}, u32[]{:S(2)}, u32[]{:S(2)}) collective-permute-start(bf16[1088,256]{1,0:T(8,128)(2,1)S(1)} %get-tuple-element.65), channel_id=1, source_target_pairs={{0,1},{1,0},{2,3},{3,2},{4,5},{5,4},{6,7},{7,6},{8,9},{9,8},{10,11... | collective-permute-start | bytes 1671176 | tf_op jit(solution)/shard_map/ppermute | solution.py:425
  84.6 18.6 %all-to-all-start.2 = ((bf16[8,136,256]{2,1,0:T(8,128)(2,1)}), bf16[8,136,256]{2,1,0:T(8,128)(2,1)S(1)}, u32[]{:S(2)}, u32[]{:S(2)}) async-start(bf16[8,136,256]{2,1,0:T(8,128)(2,1)} %bitcast.11), calls=%async_computation.2 | async-start | bytes 1114112 | tf_op jit(solution)/shard_map/all_to_all | solution.py:441
  104.1 25.1 %all-to-all-start.3 = ((bf16[8,136,256]{2,1,0:T(8,128)(2,1)}), bf16[8,136,256]{2,1,0:T(8,128)(2,1)S(1)}, u32[]{:S(2)}, u32[]{:S(2)}) async-start(bf16[8,136,256]{2,1,0:T(8,128)(2,1)} %broadcast_in_dim.2), calls=%async_computation.3 | async-start | bytes 1114112 | tf_op jit(solution)/shard_map/all_to_all | solution.py:441
  109.9 15.7 %collective-permute-start.3 = (bf16[256,256]{1,0:T(8,128)(2,1)S(1)}, bf16[256,256]{1,0:T(8,128)(2,1)S(1)}, u32[]{:S(2)}, u32[]{:S(2)}) collective-permute-start(bf16[256,256]{1,0:T(8,128)(2,1)S(1)} %get-tuple-element.74), channel_id=1, source_target_pairs={{1,0},{2,1},{3,2},{4,3},{5,4},{6,5},{7,6},{8,7},{9,8},{10,9},{11,1... | collective-permute-start | bytes 393224 | tf_op jit(solution)/shard_map/ppermute | solution.py:421
  112.8 12.7 %collective-permute-start.4 = (bf16[256,256]{1,0:T(8,128)(2,1)S(1)}, bf16[256,256]{1,0:T(8,128)(2,1)S(1)}, u32[]{:S(2)}, u32[]{:S(2)}) collective-permute-start(bf16[256,256]{1,0:T(8,128)(2,1)S(1)} %get-tuple-element.75), channel_id=1, source_target_pairs={{0,1},{1,2},{2,3},{3,4},{4,5},{5,6},{6,7},{7,8},{8,9},{9,10},{10,1... | collective-permute-start | bytes 393224 | tf_op jit(solution)/shard_map/ppermute | solution.py:421
  129.3 2.0 %collective-permute-start.5 = (bf16[1088,256]{1,0:T(8,128)(2,1)S(1)}, bf16[1088,256]{1,0:T(8,128)(2,1)S(1)}, u32[]{:S(2)}, u32[]{:S(2)}) collective-permute-start(bf16[1088,256]{1,0:T(8,128)(2,1)S(1)} %bitcast.15), channel_id=1, source_target_pairs={{0,1},{1,0},{2,3},{3,2},{4,5},{5,4},{6,7},{7,6},{8,9},{9,8},{10,11... | collective-permute-start | bytes 1671176 | tf_op jit(solution)/shard_map/ppermute | solution.py:425

commit v8 on v7

--- a/solution.py
+++ b/solution.py
@@ -279,8 +279,8 @@
 
 def fine_back_kernel(
     per, group, core_ref, own_ref, ret_ref, send_ref, part_ref, wc_ref, count_ref, pool_ref,
-    cot_ref, dsu_ref, w_ref, d_ref, he_ref, dst_ref, gwc_ref, gbc_ref, h_hbm, agg_hbm,
-    dz_ref, dq_ref, du_ref, dcs_ref, mine_ref, other_ref, gb, gw0, dagg, h_ref, agg_ref, sems,
+    cot_ref, dsu_ref, w_ref, d_ref, he_ref, dst_ref, gwc_hbm, gbc_ref, h_hbm, agg_hbm,
+    dz_ref, dq_ref, du_ref, dcs_ref, mine_ref, other_ref, gb, gw0, dagg, h_ref, agg_ref, gwc_ref, sems,
 ):
     step = pl.program_id(0)
     width = h_ref.shape[1]
@@ -288,6 +288,7 @@
     copies = [
         pltpu.make_async_copy(h_hbm, h_ref, sems.at[0]),
         pltpu.make_async_copy(agg_hbm, agg_ref, sems.at[1]),
+        pltpu.make_async_copy(gwc_hbm, gwc_ref, sems.at[2]),
     ]
 
     @pl.when(step == 0)
@@ -546,6 +547,7 @@
         grid=(steps,),
         specs={
             0: smem, 5: weight(0), 10: weight(2), 11: edge_tile, 12: edge_tile,
+            14: pl.BlockSpec(memory_space=pltpu.HBM),
             16: pl.BlockSpec(memory_space=pltpu.HBM), 17: pl.BlockSpec(memory_space=pltpu.HBM),
         },
         out_specs={0: edge_tile},
@@ -555,7 +557,8 @@
             pltpu.VMEM((nodes, width), bf),
             pltpu.VMEM((nodes, width), bf),
             pltpu.VMEM((nodes, width), bf),
-            pltpu.SemaphoreType.DMA((2,)),
+            pltpu.VMEM((4 * width, width), bf),
+            pltpu.SemaphoreType.DMA((3,)),
         ],
         us=10, near=(2, 8, 9), near_out=(4, 5),
     )

time: 134 us -> 134 us (level)
  no operation moved by 1% of the time
where the time goes in v8:
time: 134 us; the launch traced here: 133 us
  Pallas kernels  72.9 us (54%)
  starting transfers between devices  34.3 us (26%)
  waiting for transfers between devices  21.4 us (16%)
  local copies, waits for them, and re-layouts  2.11 us (2%)
    pallas_call x10, Pallas kernels, call(): pl.pallas_call(kernel, grid=grid or (1,), in_specs=in_specs, out_specs=o_...  72.9 us
    ppermute x4, starting transfers between devices, shifted(): return lax.ppermute(block, axis, route)  12.1 us
    all_to_all x2, starting transfers between devices, over_chips(): lax.all_to_all(blocks, 'dom', 0, 0, axis_index_groups=groups, tiled=True)  11.1 us
    all_to_all x2, starting transfers between devices, exchange(): lax.all_to_all(block.reshape(parts, rows // parts, width), 'dom', split_a...  10.9 us
    ppermute x4, waiting for transfers between devices, shifted(): return lax.ppermute(block, axis, route)  10.5 us
    all_to_all x2, waiting for transfers between devices, exchange(): lax.all_to_all(block.reshape(parts, rows // parts, width), 'dom', split_a...  7.19 us
    ppermute x2, waiting for transfers between devices, swapped(): return lax.ppermute(block, 'dom', [(i, i ^ bit) for i in range(parts)])  3.71 us
  transfers between devices with their start and end apart: 10, of which 6 were waited for; matrix products, arithmetic and copies ran while one was open for 0% of the time, Pallas kernels for 21%

profile of v8, /device:TPU:13, one launch (start us, length us, event | category | flops | bytes accessed | tf_op | source)
XLA Modules:
  0.0 132.5 jit_solution(11230549205832625357)
XLA Ops:
  0.7 2.0 %shard_map.156 = (bf16[256,256]{1,0:T(8,128)(2,1)S(1)}, bf16[256,256]{1,0:T(8,128)(2,1)S(1)}) custom-call(bf16[2048,256]{1,0:T(8,128)(2,1)} %h_hbm.1, s32[2,128]{1,0:T(2,128)} %bitcast.31, s32[2,128]{1,0:T(2,128)} %bitcast.33), custom_call_target="tpu_custom_call" | custom-call | flops 800000000 | bytes 1048576 | tf_op jit(solution)/shard_map/pallas_call | solution.py:107
  2.7 3.7 %collective-permute-start = (bf16[256,256]{1,0:T(8,128)(2,1)S(1)}, bf16[256,256]{1,0:T(8,128)(2,1)S(1)}, u32[]{:S(2)}, u32[]{:S(2)}) collective-permute-start(bf16[256,256]{1,0:T(8,128)(2,1)S(1)} %get-tuple-element.44), channel_id=1, source_target_pairs={{0,1},{1,2},{2,3},{3,4},{4,5},{5,6},{6,7},{7,8},{8,9},{9,10},{10,1... | collective-permute-start | bytes 393224 | tf_op jit(solution)/shard_map/ppermute | solution.py:422
  6.4 1.9 %collective-permute-start.1 = (bf16[256,256]{1,0:T(8,128)(2,1)S(1)}, bf16[256,256]{1,0:T(8,128)(2,1)S(1)}, u32[]{:S(2)}, u32[]{:S(2)}) collective-permute-start(bf16[256,256]{1,0:T(8,128)(2,1)S(1)} %get-tuple-element.45), channel_id=1, source_target_pairs={{1,0},{2,1},{3,2},{4,3},{5,4},{6,5},{7,6},{8,7},{9,8},{10,9},{11,1... | collective-permute-start | bytes 393224 | tf_op jit(solution)/shard_map/ppermute | solution.py:422
  8.3 0.7 reshape.62.send_ref
  9.0 0.0 collective-permute-done.left_ref
  9.0 4.6 %collective-permute-done.1.right_ref = bf16[256,256]{1,0:T(8,128)(2,1)S(1)} collective-permute-done((bf16[256,256]{1,0:T(8,128)(2,1)S(1)}, bf16[256,256]{1,0:T(8,128)(2,1)S(1)}, u32[]{:S(2)}, u32[]{:S(2)}) %collective-permute-start.1) | collective-permute-done | bytes 131104 | tf_op jit(solution)/shard_map/ppermute | solution.py:422
  13.6 19.7 %shard_map.157 = (bf16[8192,256]{1,0:T(8,128)(2,1)}, bf16[8192,256]{1,0:T(8,128)(2,1)}, bf16[2048,256]{1,0:T(8,128)(2,1)}, bf16[2048,256]{1,0:T(8,128)(2,1)}, bf...) custom-call(s32[8192]{0:T(1024)S(1)} %copy-done.1, ...), custom_call_target="tpu_custom_call" | custom-call | flops 17999998976 | bytes 1048576 | tf_op jit(solution)/shard_map/pallas_call | solution.py:107
  33.3 5.0 %all-to-all-start = ((bf16[16,32,256]{2,1,0:T(8,128)(2,1)}), bf16[16,32,256]{2,1,0:T(8,128)(2,1)S(1)}, u32[]{:S(2)}, u32[]{:S(2)}) async-start(bf16[16,32,256]{2,1,0:T(8,128)(2,1)} %bitcast.7), calls=%async_computation | async-start | bytes 524288 | tf_op jit(solution)/shard_map/all_to_all | solution.py:431
  38.3 4.6 %shard_map.158 = (f32[2048,256]{1,0:T(8,128)}, f32[512,256]{1,0:T(8,128)S(1)}, f32[512,256]{1,0:T(8,128)S(1)}) custom-call(bf16[512,256]{1,0:T(8,128)(2,1)} %get-tuple-element.46.pooled_ref, bf16[4,256,256]{2,1,0:T(8,128)(2,1)} %wc_ref.1, f32[2,256]{1,0:T(2,128)} %b_ref.3, s32[16,128]{1,0:T(8,128)} %bitcast.26, s32[16,128]{1,0:T(8,128)} %bitcast.28, ...), custom_call_target="tpu_custom_call" | custom-call | flops 2000000000 | bytes 1048576 | tf_op jit(solution)/shard_map/pallas_call | solution.py:107
  42.9 3.4 %all-to-all-done = bf16[16,32,256]{2,1,0:T(8,128)(2,1)S(1)} async-done(((bf16[16,32,256]{2,1,0:T(8,128)(2,1)}), bf16[16,32,256]{2,1,0:T(8,128)(2,1)S(1)}, u32[]{:S(2)}, u32[]{:S(2)}) %all-to-all-start) | async-done | bytes 262176 | tf_op jit(solution)/shard_map/all_to_all | solution.py:431
  46.3 7.6 %shard_map.159 = (bf16[512,256]{1,0:T(8,128)(2,1)}, bf16[512,256]{1,0:T(8,128)(2,1)}, bf16[2048,256]{1,0:T(8,128)(2,1)}, bf16[512,256]{1,0:T(8,128)(2,1)}, bf16[512,256]{1,0:T(8,128)(2,1)}) custom-call(f32[2048,256]{1,0:T(8,128)} %get-tuple-element.47.z_ref, bf16[512,256]{1,0:T(8,128)(2,1)S(1)} %bitcast.18, f32[512,256]{1,0:T(8,128)S(1)} %get-tuple-element.49.ghc_ref, ...), custom_call_target="tpu_custom_call" | custom-call | flops 4700000256 | bytes 1048576 | tf_op jit(solution)/shard_map/pallas_call | solution.py:107
  53.9 5.9 %all-to-all-start.1 = ((bf16[16,32,256]{2,1,0:T(8,128)(2,1)}), bf16[16,32,256]{2,1,0:T(8,128)(2,1)S(1)}, u32[]{:S(2)}, u32[]{:S(2)}) async-start(bf16[16,32,256]{2,1,0:T(8,128)(2,1)} %bitcast.9), calls=%async_computation.1 | async-start | bytes 524288 | tf_op jit(solution)/shard_map/all_to_all | solution.py:431
  59.7 3.6 %shard_map.160 = (bf16[1024,256]{1,0:T(8,128)(2,1)}, f32[8,256]{1,0:T(8,128)S(1)}, f32[512,256]{1,0:T(8,128)}) custom-call(bf16[512,256]{1,0:T(8,128)(2,1)} %get-tuple-element.46.pooled_ref, bf16[512,256]{1,0:T(8,128)(2,1)S(1)} %bitcast.19, f32[512,256]{1,0:T(8,128)S(1)} %get-tuple-element.49.ghc_ref, bf16[4,256,256]{2,1,0:T(8,128)(2,1)} %wc_ref.1, ...), custom_call_target="tpu_custom_call" | custom-call | flops 1000000000 | bytes 1048576 | tf_op jit(solution)/shard_map/pallas_call | solution.py:107
  63.3 0.6 copy-done.2
  63.9 3.8 %all-to-all-done.1 = bf16[16,32,256]{2,1,0:T(8,128)(2,1)S(1)} async-done(((bf16[16,32,256]{2,1,0:T(8,128)(2,1)}), bf16[16,32,256]{2,1,0:T(8,128)(2,1)S(1)}, u32[]{:S(2)}, u32[]{:S(2)}) %all-to-all-start.1) | async-done | bytes 262176 | tf_op jit(solution)/shard_map/all_to_all | solution.py:431
  67.7 13.7 %shard_map.161 = (bf16[8192,256]{1,0:T(8,128)(2,1)}, bf16[2048,256]{1,0:T(8,128)(2,1)}, bf16[2048,256]{1,0:T(8,128)(2,1)}, bf16[512,256]{1,0:T(8,128)(2,1)}, bf1...) custom-call(s32[1]{0:T(128)} %bitcast.core_ref, bf16[512,256]{1,0:T(8,128)(2,1)} %get-tuple-element.51.own_ref, ...), custom_call_target="tpu_custom_call" | custom-call | flops 10000000000 | bytes 1048576 | tf_op jit(solution)/shard_map/pallas_call | solution.py:107
  81.5 0.3 collective-permute-start.2
  81.7 1.8 %collective-permute-done.2 = bf16[1088,256]{1,0:T(8,128)(2,1)S(1)} collective-permute-done((bf16[1088,256]{1,0:T(8,128)(2,1)S(1)}, bf16[1088,256]{1,0:T(8,128)(2,1)S(1)}, u32[]{:S(2)}, u32[]{:S(2)}) %collective-permute-start.2) | collective-permute-done | bytes 557088 | tf_op jit(solution)/shard_map/ppermute | solution.py:426
  83.5 1.0 add_convert_fusion
  84.5 5.4 %all-to-all-start.2 = ((bf16[8,136,256]{2,1,0:T(8,128)(2,1)}), bf16[8,136,256]{2,1,0:T(8,128)(2,1)S(1)}, u32[]{:S(2)}, u32[]{:S(2)}) async-start(bf16[8,136,256]{2,1,0:T(8,128)(2,1)} %bitcast.11), calls=%async_computation.2 | async-start | bytes 1114112 | tf_op jit(solution)/shard_map/all_to_all | solution.py:442
  89.8 13.2 %shard_map.162 = (bf16[2048,256]{1,0:T(8,128)(2,1)}, bf16[256,256]{1,0:T(8,128)(2,1)S(1)}, bf16[256,256]{1,0:T(8,128)(2,1)S(1)}) custom-call(s32[8192]{0:T(1024)S(1)} %copy-done.1, bf16[8192,256]{1,0:T(8,128)(2,1)} %get-tuple-element.68.dz_ref), custom_call_target="tpu_custom_call" | custom-call | flops 12000000000 | bytes 1048576 | tf_op jit(solution)/shard_map/pallas_call | solution.py:107
  103.1 0.1 reduce_sum.12
  103.1 0.8 broadcast_in_dim.2
  104.0 5.8 %all-to-all-start.3 = ((bf16[8,136,256]{2,1,0:T(8,128)(2,1)}), bf16[8,136,256]{2,1,0:T(8,128)(2,1)S(1)}, u32[]{:S(2)}, u32[]{:S(2)}) async-start(bf16[8,136,256]{2,1,0:T(8,128)(2,1)} %broadcast_in_dim.2), calls=%async_computation.3 | async-start | bytes 1114112 | tf_op jit(solution)/shard_map/all_to_all | solution.py:442
  109.8 2.9 %collective-permute-start.3 = (bf16[256,256]{1,0:T(8,128)(2,1)S(1)}, bf16[256,256]{1,0:T(8,128)(2,1)S(1)}, u32[]{:S(2)}, u32[]{:S(2)}) collective-permute-start(bf16[256,256]{1,0:T(8,128)(2,1)S(1)} %get-tuple-element.74), channel_id=1, source_target_pairs={{1,0},{2,1},{3,2},{4,3},{5,4},{6,5},{7,6},{8,7},{9,8},{10,9},{11,1... | collective-permute-start | bytes 393224 | tf_op jit(solution)/shard_map/ppermute | solution.py:422
  112.7 3.5 %collective-permute-start.4 = (bf16[256,256]{1,0:T(8,128)(2,1)S(1)}, bf16[256,256]{1,0:T(8,128)(2,1)S(1)}, u32[]{:S(2)}, u32[]{:S(2)}) collective-permute-start(bf16[256,256]{1,0:T(8,128)(2,1)S(1)} %get-tuple-element.75), channel_id=1, source_target_pairs={{0,1},{1,2},{2,3},{3,4},{4,5},{5,6},{6,7},{7,8},{8,9},{9,10},{10,1... | collective-permute-start | bytes 393224 | tf_op jit(solution)/shard_map/ppermute | solution.py:422
  116.2 3.3 %shard_map.163.part_ref = f32[2048,256]{1,0:T(8,128)S(1)} custom-call(bf16[2048,256]{1,0:T(8,128)(2,1)} %get-tuple-element.76.dq_ref, bf16[2048,256]{1,0:T(8,128)(2,1)} %get-tuple-element.77.du_ref, bf16[2048,256]{1,0:T(8,128)(2,1)} %cot_ref.5, bf16[512,256]{1,0:T(8,128)(2,1)} %get-tuple-element.78.dcs_ref, s32[16,128]{1,0:T(8,128)} %bitcast.23, ...), custom_call_target="tpu_custom_call" | custom-call | flops 1500000000 | bytes 1048576 | tf_op jit(solution)/shard_map/pallas_call | solution.py:107
  119.5 5.9 %collective-permute-done.3.from_right_ref = bf16[256,256]{1,0:T(8,128)(2,1)S(1)} collective-permute-done((bf16[256,256]{1,0:T(8,128)(2,1)S(1)}, bf16[256,256]{1,0:T(8,128)(2,1)S(1)}, u32[]{:S(2)}, u32[]{:S(2)}) %collective-permute-start.3) | collective-permute-done | bytes 131104 | tf_op jit(solution)/shard_map/ppermute | solution.py:422
  125.4 0.0 collective-permute-done.4.from_left_ref
  125.4 3.7 %shard_map.164 = f32[2048,256]{1,0:T(8,128)} custom-call(bf16[2048,256]{1,0:T(8,128)(2,1)} %get-tuple-element.73.own_ref, bf16[256,256]{1,0:T(8,128)(2,1)S(1)} %collective-permute-done.3.from_right_ref, bf16[256,256]{1,0:T(8,128)(2,1)S(1)} %collective-permute-done.4.from_left_ref, s32[2,128]{1,0:T(2,128)} %bitcast.32, s32[2,128]{1,0:T(2,128)} %bitcast.34, ...), custom_call_target="tpu_custom_call" | custom-call | flops 2400000000 | bytes 1048576 | tf_op jit(solution)/shard_map/pallas_call | solution.py:107
  129.1 2.0 %collective-permute-done.5.ax_ref = bf16[1088,256]{1,0:T(8,128)(2,1)S(1)} collective-permute-done((bf16[1088,256]{1,0:T(8,128)(2,1)S(1)}, bf16[1088,256]{1,0:T(8,128)(2,1)S(1)}, u32[]{:S(2)}, u32[]{:S(2)}) %collective-permute-start.5) | collective-permute-done | bytes 557088 | tf_op jit(solution)/shard_map/ppermute | solution.py:426
  131.1 1.5 %shard_map.165 = (f32[1024,256]{1,0:T(8,128)}, f32[1024,256]{1,0:T(8,128)}, f32[2,256]{1,0:T(2,128)}) custom-call(s32[1]{0:T(128)} %bitcast.core_ref, bf16[1088,256]{1,0:T(8,128)(2,1)S(1)} %bitcast.16, bf16[1088,256]{1,0:T(8,128)(2,1)S(1)} %collective-permute-done.5.ax_ref), custom_call_target="tpu_custom_call" | custom-call | flops 1500000000 | bytes 1048576 | tf_op jit(solution)/shard_map/pallas_call | solution.py:107
  (12 shorter events, 0.0 us)
Async XLA Ops:
  0.6 7.7 %copy-start.4 = (s32[16,32]{1,0:T(8,128)S(1)}, s32[16,32]{1,0:T(8,128)}, u32[]{:S(2)}) copy-start(s32[16,32]{1,0:T(8,128)} %param.25) | copy-start | bytes 6148
  0.6 12.9 %copy-start.1 = (s32[8192]{0:T(1024)S(1)}, s32[8192]{0:T(1024)}, u32[]{:S(2)}) copy-start(s32[8192]{0:T(1024)} %src_ref.3) | copy-start | bytes 98308
  2.7 6.3 %collective-permute-start = (bf16[256,256]{1,0:T(8,128)(2,1)S(1)}, bf16[256,256]{1,0:T(8,128)(2,1)S(1)}, u32[]{:S(2)}, u32[]{:S(2)}) collective-permute-start(bf16[256,256]{1,0:T(8,128)(2,1)S(1)} %get-tuple-element.44), channel_id=1, source_target_pairs={{0,1},{1,2},{2,3},{3,4},{4,5},{5,6},{6,7},{7,8},{8,9},{9,10},{10,1... | collective-permute-start | bytes 393224 | tf_op jit(solution)/shard_map/ppermute | solution.py:422
  6.4 7.2 %collective-permute-start.1 = (bf16[256,256]{1,0:T(8,128)(2,1)S(1)}, bf16[256,256]{1,0:T(8,128)(2,1)S(1)}, u32[]{:S(2)}, u32[]{:S(2)}) collective-permute-start(bf16[256,256]{1,0:T(8,128)(2,1)S(1)} %get-tuple-element.45), channel_id=1, source_target_pairs={{1,0},{2,1},{3,2},{4,3},{5,4},{6,5},{7,6},{8,7},{9,8},{10,9},{11,1... | collective-permute-start | bytes 393224 | tf_op jit(solution)/shard_map/ppermute | solution.py:422
  33.3 12.9 %all-to-all-start = ((bf16[16,32,256]{2,1,0:T(8,128)(2,1)}), bf16[16,32,256]{2,1,0:T(8,128)(2,1)S(1)}, u32[]{:S(2)}, u32[]{:S(2)}) async-start(bf16[16,32,256]{2,1,0:T(8,128)(2,1)} %bitcast.7), calls=%async_computation | async-start | bytes 524288 | tf_op jit(solution)/shard_map/all_to_all | solution.py:431
  53.9 13.8 %copy-start = (bf16[2048,256]{1,0:T(8,128)(2,1)S(1)}, bf16[2048,256]{1,0:T(8,128)(2,1)}, u32[]{:S(2)}) copy-start(bf16[2048,256]{1,0:T(8,128)(2,1)} %cot_ref.5) | copy-start | bytes 3145732
  53.9 13.8 %copy-start.3 = (bf16[2048,256]{1,0:T(8,128)(2,1)S(1)}, bf16[2048,256]{1,0:T(8,128)(2,1)}, u32[]{:S(2)}) copy-start(bf16[2048,256]{1,0:T(8,128)(2,1)} %get-tuple-element.58.dsu_ref) | copy-start | bytes 3145732
  53.9 13.8 %all-to-all-start.1 = ((bf16[16,32,256]{2,1,0:T(8,128)(2,1)}), bf16[16,32,256]{2,1,0:T(8,128)(2,1)S(1)}, u32[]{:S(2)}, u32[]{:S(2)}) async-start(bf16[16,32,256]{2,1,0:T(8,128)(2,1)} %bitcast.9), calls=%async_computation.1 | async-start | bytes 524288 | tf_op jit(solution)/shard_map/all_to_all | solution.py:431
  63.3 0.6 copy-start.2
  81.5 2.0 %collective-permute-start.2 = (bf16[1088,256]{1,0:T(8,128)(2,1)S(1)}, bf16[1088,256]{1,0:T(8,128)(2,1)S(1)}, u32[]{:S(2)}, u32[]{:S(2)}) collective-permute-start(bf16[1088,256]{1,0:T(8,128)(2,1)S(1)} %get-tuple-element.65), channel_id=1, source_target_pairs={{0,1},{1,0},{2,3},{3,2},{4,5},{5,4},{6,7},{7,6},{8,9},{9,8},{10,11... | collective-permute-start | bytes 1671176 | tf_op jit(solution)/shard_map/ppermute | solution.py:426
  84.5 18.6 %all-to-all-start.2 = ((bf16[8,136,256]{2,1,0:T(8,128)(2,1)}), bf16[8,136,256]{2,1,0:T(8,128)(2,1)S(1)}, u32[]{:S(2)}, u32[]{:S(2)}) async-start(bf16[8,136,256]{2,1,0:T(8,128)(2,1)} %bitcast.11), calls=%async_computation.2 | async-start | bytes 1114112 | tf_op jit(solution)/shard_map/all_to_all | solution.py:442
  104.0 25.1 %all-to-all-start.3 = ((bf16[8,136,256]{2,1,0:T(8,128)(2,1)}), bf16[8,136,256]{2,1,0:T(8,128)(2,1)S(1)}, u32[]{:S(2)}, u32[]{:S(2)}) async-start(bf16[8,136,256]{2,1,0:T(8,128)(2,1)} %broadcast_in_dim.2), calls=%async_computation.3 | async-start | bytes 1114112 | tf_op jit(solution)/shard_map/all_to_all | solution.py:442
  109.8 15.7 %collective-permute-start.3 = (bf16[256,256]{1,0:T(8,128)(2,1)S(1)}, bf16[256,256]{1,0:T(8,128)(2,1)S(1)}, u32[]{:S(2)}, u32[]{:S(2)}) collective-permute-start(bf16[256,256]{1,0:T(8,128)(2,1)S(1)} %get-tuple-element.74), channel_id=1, source_target_pairs={{1,0},{2,1},{3,2},{4,3},{5,4},{6,5},{7,6},{8,7},{9,8},{10,9},{11,1... | collective-permute-start | bytes 393224 | tf_op jit(solution)/shard_map/ppermute | solution.py:422
  112.7 12.7 %collective-permute-start.4 = (bf16[256,256]{1,0:T(8,128)(2,1)S(1)}, bf16[256,256]{1,0:T(8,128)(2,1)S(1)}, u32[]{:S(2)}, u32[]{:S(2)}) collective-permute-start(bf16[256,256]{1,0:T(8,128)(2,1)S(1)} %get-tuple-element.75), channel_id=1, source_target_pairs={{0,1},{1,2},{2,3},{3,4},{4,5},{5,6},{6,7},{7,8},{8,9},{9,10},{10,1... | collective-permute-start | bytes 393224 | tf_op jit(solution)/shard_map/ppermute | solution.py:422
  129.1 2.0 %collective-permute-start.5 = (bf16[1088,256]{1,0:T(8,128)(2,1)S(1)}, bf16[1088,256]{1,0:T(8,128)(2,1)S(1)}, u32[]{:S(2)}, u32[]{:S(2)}) collective-permute-start(bf16[1088,256]{1,0:T(8,128)(2,1)S(1)} %bitcast.15), channel_id=1, source_target_pairs={{0,1},{1,0},{2,3},{3,2},{4,5},{5,4},{6,7},{7,6},{8,9},{9,8},{10,11... | collective-permute-start | bytes 1671176 | tf_op jit(solution)/shard_map/ppermute | solution.py:426
